TPU v7x, 32 devices: a whole 2x2x4 slice. The times are simulated.
32 devices in a mesh: group: 2 (over x), dp: 4 (over z), mp: 4 (over y, core).
Axes of the slice: x: 2, y: 2, z: 4, core: 2. Of those that a mesh axis runs over, the one named last changes fastest.
Arguments:
- patch_rows: bfloat16 [8, 128, 1280], P(('group', 'dp')), may hold values from -6 to 6
- ln_gain: float32 [1280], replicated, may hold values from 0.5 to 1.5
- ln_bias: float32 [1280], replicated, may hold values from -1.5 to 1.5
- merge_up: bfloat16 [5120, 5120], P(None, 'mp'), may hold values from -0.078125 to 0.078125
- merge_up_bias: float32 [5120], P('mp'), may hold values from -2.5 to 2.5
- merge_down: bfloat16 [5120, 8192], P('mp'), may hold values from -0.078125 to 0.078125
- merge_down_bias: float32 [8192], P('mp'), may hold values from -2.5 to 2.5
- row_owner: int32 [256, 1], replicated, may hold values from 0 to 7; in each aligned block of 32 rows (0 to 31, 32 to 63, ...) at most 8 rows name the same one
- text_embed: bfloat16 [8, 256, 8192], P(('group', 'dp')), may hold values from -6 to 6
- doc_ids: int32 [8, 256], P(('group', 'dp')), may hold values from 0 to 7, never falling along the last dimension, each value on 1 to 64 neighbouring positions
- rms_gain: float32 [8192], replicated, may hold values from 0.5 to 1.5
- w_query: bfloat16 [8192, 8192], P(None, 'mp')
- query_bias: float32 [8192], P('mp'), may hold values from -2.5 to 2.5
- w_keyval: bfloat16 [8192, 2, 1024], P(None, None, 'mp'), may hold values from -0.0625 to 0.0625
- keyval_bias: float32 [2, 1024], P(None, 'mp'), may hold values from -2.5 to 2.5
Outputs:
- attention: bfloat16 [8, 256, 8192], P(('group', 'dp'), None, 'mp')
Inputs may be any that keep to these rules, and one draw needn't show every extreme that they name: `row_owner`: in each aligned block of 32 rows (the rows of one image owner) no owner is named more than 8 times, a bound that some block reaches.
All inputs are finite; a program needn't handle non-finite values.
Results may differ from a plain program's by a relative error of at most 0.014.
The roundings to bfloat16 on the way count: a program that leaves them out, or rounds other values in their place, can miss the bound.
Values may be sent and summed in bfloat16 or wider, within the bound.
No kernel may reach another device: no remote copies, remote signals or barrier semaphores. Data moves between devices by JAX's collectives and lax.ppermute only.
A program may use at most 128 MiB of HBM per device.

v0:
```python
import math

import jax
import jax.numpy as jnp
from jax import lax
from jax.sharding import PartitionSpec as P

HEADS = 64
KV_HEADS = 8
HEAD_DIM = 128


def per_device(
    patch_rows,
    ln_gain,
    ln_bias,
    merge_up,
    merge_up_bias,
    merge_down,
    merge_down_bias,
    row_owner,
    text_embed,
    doc_ids,
    rms_gain,
    w_query,
    query_bias,
    w_keyval,
    keyval_bias,
):
    owners = lax.axis_size(("group", "dp"))
    own_index = lax.axis_index(("group", "dp"))
    mp_index = lax.axis_index("mp")
    pixels = patch_rows[0].astype(jnp.float32)
    center = pixels - jnp.mean(pixels, axis=-1, keepdims=True)
    spread = jnp.mean(center * center, axis=-1, keepdims=True)
    normed_patch = (center * lax.rsqrt(spread + 1e-06) * ln_gain + ln_bias).astype(jnp.bfloat16)
    merged = normed_patch.reshape(-1, 4 * pixels.shape[1])
    merged_rows = merged.shape[0]
    hidden = jax.nn.gelu(
        jnp.dot(merged, merge_up, preferred_element_type=jnp.float32) + merge_up_bias,
        approximate=False,
    ).astype(jnp.bfloat16)
    partial_sum = jnp.dot(hidden, merge_down, preferred_element_type=jnp.float32)
    vision = (
        lax.psum_scatter(partial_sum, "mp", scatter_dimension=1, tiled=True) + merge_down_bias
    ).astype(jnp.bfloat16)
    col_width = vision.shape[1]
    capacity = max(2, 2 * merged_rows // owners)
    owner_all = row_owner[:, 0]
    owner_ids = jnp.arange(owners, dtype=jnp.int32)
    onehot = (owner_all[:, None] == owner_ids[None, :]).astype(jnp.int32)
    per_source = jnp.sum(onehot.reshape(owners, merged_rows, owners), axis=1)
    my_block = lax.dynamic_slice_in_dim(onehot, own_index * merged_rows, merged_rows, 0)
    block_rank = jnp.sum((jnp.cumsum(my_block, axis=0) - my_block) * my_block, axis=1)
    my_owner = jnp.sum(my_block * owner_ids[None, :], axis=1)
    slot_id = my_owner * capacity + block_rank
    all_slots = jnp.arange(owners * capacity, dtype=jnp.int32)
    select = (slot_id[:, None] == all_slots[None, :]).astype(jnp.bfloat16)
    outgoing = jnp.einsum("ms,mc->sc", select, vision, preferred_element_type=jnp.float32).astype(
        jnp.bfloat16
    )
    arrived = lax.all_to_all(
        outgoing.reshape(owners, capacity, col_width),
        ("group", "dp"),
        split_axis=0,
        concat_axis=0,
        tiled=True,
    )
    arrived = arrived.reshape(owners * capacity, col_width)
    incoming = lax.dynamic_slice_in_dim(per_source, own_index, 1, 1)[:, 0]
    offsets = jnp.cumsum(incoming) - incoming
    total = jnp.sum(incoming)
    slot_rank = jnp.arange(capacity, dtype=jnp.int32)
    target = jnp.where(
        slot_rank[None, :] < incoming[:, None], offsets[:, None] + slot_rank[None, :], -1
    ).reshape(-1)
    text_rows = text_embed[0]
    seq_len = text_rows.shape[0]
    positions = jnp.arange(seq_len, dtype=jnp.int32)
    source_slot = jnp.sum(
        jnp.where(target[:, None] == positions[None, :], all_slots[:, None], 0), axis=0
    )
    is_image = (positions < total)[:, None]
    image_full = lax.all_gather(arrived, "mp", axis=1, tiled=True)
    sequence = jnp.where(is_image, jnp.take(image_full, source_slot, axis=0), text_rows)
    seq_f = sequence.astype(jnp.float32)
    normed_seq = (
        seq_f * lax.rsqrt(jnp.mean(seq_f * seq_f, axis=-1, keepdims=True) + 1e-06) * rms_gain
    ).astype(jnp.bfloat16)
    queries = (
        jnp.dot(normed_seq, w_query, preferred_element_type=jnp.float32) + query_bias
    ).astype(jnp.bfloat16)
    keyval_local = (
        jnp.einsum("sd,dtc->stc", normed_seq, w_keyval, preferred_element_type=jnp.float32)
        + keyval_bias
    ).astype(jnp.bfloat16)
    keyval_full = lax.all_gather(keyval_local, "mp", axis=2, tiled=True)
    keyval_heads = jnp.transpose(keyval_full.reshape(seq_len, 2, HEAD_DIM, KV_HEADS), (0, 1, 3, 2))
    local_heads = queries.shape[1] // HEAD_DIM
    group_size = HEADS // KV_HEADS
    kv_index = (mp_index * local_heads + jnp.arange(local_heads, dtype=jnp.int32)) // group_size
    keys = jnp.take(keyval_heads[:, 0], kv_index, axis=1)
    values = jnp.take(keyval_heads[:, 1], kv_index, axis=1)
    query_heads = queries.reshape(seq_len, local_heads, HEAD_DIM)
    scores = jnp.einsum(
        "qhd,khd->hqk", query_heads, keys, preferred_element_type=jnp.float32
    ) / math.sqrt(HEAD_DIM)
    documents = doc_ids[0]
    allowed = (documents[:, None] == documents[None, :]) & (
        positions[None, :] <= positions[:, None]
    )
    scores = jnp.where(allowed[None], scores, jnp.float32(-1e30))
    highest = jnp.max(scores, axis=-1, keepdims=True)
    weights = jnp.exp(scores - highest)
    probs = (weights / jnp.sum(weights, axis=-1, keepdims=True)).astype(jnp.bfloat16)
    output = jnp.einsum("hqk,khd->qhd", probs, values, preferred_element_type=jnp.float32)
    return output.astype(jnp.bfloat16).reshape(1, seq_len, local_heads * HEAD_DIM)


def solution(mesh):
    in_specs = (
        P(("group", "dp"), None, None),
        P(),
        P(),
        P(None, "mp"),
        P("mp"),
        P("mp", None),
        P("mp"),
        P(),
        P(("group", "dp"), None, None),
        P(("group", "dp"), None),
        P(),
        P(None, "mp"),
        P("mp"),
        P(None, None, "mp"),
        P(None, "mp"),
    )
    out_specs = P(("group", "dp"), None, "mp")
    return jax.shard_map(
        per_device, mesh=mesh, in_specs=in_specs, out_specs=out_specs, check_vma=False
    )
```

profile of v0, /device:TPU:0, one launch (start us, length us, event | category | flops | bytes accessed | tf_op | source)
XLA Modules:
  0.0 141.6 jit_solution(1316135866243180742)
XLA Ops:
  6.5 1.1 convert_reduce_fusion
  7.7 1.2 fusion.38
  9.0 1.2 reshape.190
  11.0 7.5 %fusion.46 = bf16[32,1280]{1,0:T(8,128)(2,1)S(1)} fusion(bf16[5120,1280]{1,0:T(8,128)(2,1)} %param.20, f32[32,5120]{1,0:T(8,128)S(1)} %bitcast.54, f32[32,5120]{1,0:T(8,128)S(1)} %reshape.190, f32[32,5120]{1,0:T(8,128)S(1)} %bitcast.55, f32[5120]{0:T(1024)S(1)} %add.147, f32[5120]{0:T(1024)S(1)} %mul.103, f32[1280]{0:T(1024)S(1)} %copy-done.5), kind=kOutput, calls=%fused_computation.57 | convolution fusion | flops 422952960 | bytes 15201280 | tf_op jit(solution)/shard_map/dot_general | solution.py:40
  18.5 3.2 %copy-done = bf16[1280,8192]{1,0:T(8,128)(2,1)S(1)} copy-done((bf16[1280,8192]{1,0:T(8,128)(2,1)S(1)}, bf16[1280,8192]{1,0:T(8,128)(2,1)}, u32[]{:S(2)}) %copy-start) | copy-done | bytes 20971544
  21.6 4.7 %fusion.64 = f32[32,8192]{1,0:T(8,128)} fusion(bf16[32,1280]{1,0:T(8,128)(2,1)S(1)} %fusion.46, bf16[1280,8192]{1,0:T(8,128)(2,1)S(1)} %copy-done), kind=kOutput, calls=%fused_computation.111 | convolution fusion | flops 671088640 | bytes 22102016 | tf_op jit(solution)/shard_map/dot_general | solution.py:43
  26.6 0.2 multiply_reduce_fusion
  26.8 27.3 %reduce-scatter.2.cloned.1.call-done = f32[32,2048]{1,0:T(8,128)} async-done(((f32[32,8192]{1,0:T(8,128)}), f32[32,2048]{1,0:T(8,128)}) %reduce-scatter.2.cloned.1.call-update) | async-done | bytes 262160 | tf_op jit(solution)/shard_map/reduce_scatter | solution.py:45
  54.1 2.0 %fusion.9 = bf16[8,8,2048]{2,1,0:T(8,128)(2,1)} fusion(f32[32,2048]{1,0:T(8,128)} %reduce-scatter.2.cloned.1.call-done, f32[2048]{0:T(1024)S(1)} %copy-done.6, s32[32]{0:T(128)S(1)} %multiply_add_fusion), kind=kOutput, calls=%fused_computation.21 | convolution fusion | flops 8652800 | bytes 532608 | tf_op jit(solution)/shard_map/ms,mc->sc/dot_general | solution.py:59
  56.1 5.5 %all-to-all-start = ((bf16[8,8,2048]{2,1,0:T(8,128)(2,1)}), bf16[8,8,2048]{2,1,0:T(8,128)(2,1)S(1)}, u32[]{:S(2)}, u32[]{:S(2)}) async-start(bf16[8,8,2048]{2,1,0:T(8,128)(2,1)} %fusion.9), calls=%async_computation.1 | async-start | bytes 524288 | tf_op jit(solution)/shard_map/all_to_all | solution.py:62
  61.7 0.6 broadcast.218
  62.3 0.7 reduce.8
  63.1 0.2 convert_reduce_fusion.1
  63.4 8.0 %all-to-all-done = bf16[8,8,2048]{2,1,0:T(8,128)(2,1)S(1)} async-done(((bf16[8,8,2048]{2,1,0:T(8,128)(2,1)}), bf16[8,8,2048]{2,1,0:T(8,128)(2,1)S(1)}, u32[]{:S(2)}, u32[]{:S(2)}) %all-to-all-start) | async-done | bytes 262176 | tf_op jit(solution)/shard_map/all_to_all | solution.py:62
  71.4 0.7 copy-done.4
  72.1 0.2 all-gather.5.cloned.1.call-start
  72.4 0.8 fusion.62
  73.5 0.7 compare_and_fusion.1
  74.3 11.1 %all-gather.3.cloned.1.call-done = bf16[64,8192]{1,0:T(8,128)(2,1)} async-done(((bf16[64,2048]{1,0:T(8,128)(2,1)}), bf16[64,8192]{1,0:T(8,128)(2,1)}) %all-gather.3.cloned.1.call-update) | async-done | bytes 1048592 | tf_op jit(solution)/shard_map/all_gather | solution.py:84
  85.4 10.3 %gather_fusion = bf16[256,8192]{1,0:T(8,128)(2,1)} fusion(bf16[64,8192]{1,0:T(8,128)(2,1)} %all-gather.3.cloned.1.call-done, s32[1024]{0:T(1024)S(1)} %pad_clamp_fusion.1), kind=kCustom, calls=%fused_computation.2 | custom fusion | bytes 8389632 | tf_op jit(solution)/shard_map/jit(_take)/gather | solution.py:85
  95.7 4.9 %fusion.1 = (f32[256]{0:T(256)S(1)}, bf16[256,8192]{1,0:T(8,128)(2,1)S(1)}) fusion(bf16[1,256,8192]{2,1,0:T(8,128)(2,1)} %param.25, bf16[256,8192]{1,0:T(8,128)(2,1)} %gather_fusion, pred[256]{0:T(512)(128)(4,1)S(1)} %get-tuple-element.17, pred[256]{0:T(512)(128)(4,1)S(1)} %get-tuple-element.18), kind=kLoop, calls=%fused_computation.6 | loop fusion | flops 10485504 | bytes 12584448 | tf_op jit(solution)/shard_map/reduce_sum | solution.py:88
  100.6 1.9 %copy-done.1 = bf16[256,8192]{1,0:T(8,128)(2,1)} copy-done((bf16[256,8192]{1,0:T(8,128)(2,1)}, bf16[256,8192]{1,0:T(8,128)(2,1)S(1)}, u32[]{:S(2)}) %copy-start.1) | copy-done | bytes 4194328
  102.5 6.5 %fusion.21 = bf16[256,2,256]{2,0,1:T(8,128)(2,1)} fusion(bf16[8192,2,256]{2,1,0:T(2,128)(2,1)} %param.30, bf16[256,8192]{1,0:T(8,128)(2,1)S(1)} %get-tuple-element.12, f32[8192]{0:T(1024)S(1)} %copy-done.11, f32[256]{0:T(256)S(1)} %add_rsqrt_fusion, f32[2,256]{1,0:T(2,128)S(1)} %copy-done.13), kind=kOutput, calls=%fused_computation.29 | convolution fusion | flops 2156134400 | bytes 12880896 | tf_op jit(solution)/shard_map/sd,dtc->stc/dot_general | solution.py:94
  109.1 17.5 %fusion.15 = bf16[32,16,8,128]{3,2,1,0:T(8,128)(2,1)} fusion(bf16[8192,2048]{1,0:T(8,128)(2,1)} %param.28, bf16[256,8192]{1,0:T(8,128)(2,1)} %copy-done.1, f32[8192]{0:T(1024)S(1)} %copy-done.11, f32[256]{0:T(256)S(1)} %add_rsqrt_fusion, f32[2048]{0:T(1024)S(1)} %copy-done.12), kind=kOutput, calls=%fused_computation.27 | convolution fusion | flops 8599371776 | bytes 38839296 | tf_op jit(solution)/shard_map/dot_general | solution.py:91
  126.5 1.5 %copy.35 = bf16[256,2,1024]{0,2,1:T(8,128)(2,1)S(1)} copy(bf16[256,2,1024]{2,0,1:T(8,128)(2,1)} %all-gather.5.cloned.1.call-done) | data formatting | bytes 2097152 | tf_op jit(solution)/shard_map/all_gather | solution.py:97
  128.0 0.2 copy.57
  128.3 0.6 gather_fusion.2
  129.0 1.6 %gather_fusion.1 = bf16[16,256,128]{1,2,0:T(8,128)(2,1)} fusion(bf16[256,8,128]{0,2,1:T(8,128)(2,1)S(1)} %get-tuple-element.13, s32[1024]{0:T(1024)S(1)} %pad_clamp_fusion), kind=kCustom, calls=%fused_computation.clone | custom fusion | bytes 2097216 | tf_op jit(solution)/shard_map/jit(_take)/gather | solution.py:103
  130.6 1.2 fusion.28
  131.8 1.2 fusion.63
  133.1 0.6 fusion.14
  133.7 1.4 %copy.40 = bf16[1,256,2048]{2,1,0:T(8,128)(2,1)} copy(bf16[1,256,2048]{1,2,0:T(8,128)(2,1)S(1)} %bitcast.60) | data formatting | bytes 2097152 | tf_op jit(solution)/shard_map/reshape | solution.py:117
  (61 shorter events, 1.8 us)
Async XLA Ops:
  6.5 4.3 %copy-start.7 = (f32[1280]{0:T(1024)S(1)}, f32[1280]{0:T(1024)}, u32[]{:S(2)}) copy-start(f32[1280]{0:T(1024)} %param.19) | copy-start | bytes 15364
  6.5 4.4 %copy-start.8 = (f32[1280]{0:T(1024)S(1)}, f32[1280]{0:T(1024)}, u32[]{:S(2)}) copy-start(f32[1280]{0:T(1024)} %param.18) | copy-start | bytes 15364
  6.5 4.4 %copy-start.5 = (f32[1280]{0:T(1024)S(1)}, f32[1280]{0:T(1024)}, u32[]{:S(2)}) copy-start(f32[1280]{0:T(1024)} %param.21) | copy-start | bytes 15364
  6.5 47.6 %reduce-scatter.2.cloned.1.call-start = ((), (), s32[]{:S(2)}) async-start(), calls=%async_computation.2 | async-start | bytes 1310720 | tf_op jit(solution)/shard_map/reduce_scatter | solution.py:45
  10.9 10.7 %copy-start = (bf16[1280,8192]{1,0:T(8,128)(2,1)S(1)}, bf16[1280,8192]{1,0:T(8,128)(2,1)}, u32[]{:S(2)}) copy-start(bf16[1280,8192]{1,0:T(8,128)(2,1)} %param.22) | copy-start | bytes 62914564
  21.6 4.7 %copy-start.10 = (s32[256,1]{0,1:T(1,128)S(1)}, s32[256,1]{0,1:T(1,128)}, u32[]{:S(2)}) copy-start(s32[256,1]{0,1:T(1,128)} %param.24) | copy-start | bytes 3076
  21.6 32.5 %copy-start.6 = (f32[2048]{0:T(1024)S(1)}, f32[2048]{0:T(1024)}, u32[]{:S(2)}) copy-start(f32[2048]{0:T(1024)} %param.23) | copy-start | bytes 24580
  21.6 52.6 %copy-start.9 = (s32[1,256]{1,0:T(1,128)S(1)}, s32[1,256]{1,0:T(1,128)}, u32[]{:S(2)}) copy-start(s32[1,256]{1,0:T(1,128)} %param.26) | copy-start | bytes 3076
  56.1 15.3 %all-to-all-start = ((bf16[8,8,2048]{2,1,0:T(8,128)(2,1)}), bf16[8,8,2048]{2,1,0:T(8,128)(2,1)S(1)}, u32[]{:S(2)}, u32[]{:S(2)}) async-start(bf16[8,8,2048]{2,1,0:T(8,128)(2,1)} %fusion.9), calls=%async_computation.1 | async-start | bytes 524288 | tf_op jit(solution)/shard_map/all_to_all | solution.py:62
  61.6 23.8 %all-gather.3.cloned.1.call-start = ((), (), s32[]{:S(2)}) async-start(), calls=%async_computation.3 | async-start | bytes 1310720 | tf_op jit(solution)/shard_map/all_gather | solution.py:84
  71.4 0.7 copy-start.4
  72.1 54.4 %all-gather.5.cloned.1.call-start = ((), (), s32[]{:S(2)}) async-start(), calls=%async_computation.4 | async-start | bytes 1310720 | tf_op jit(solution)/shard_map/all_gather | solution.py:97
  95.7 6.8 %copy-start.11 = (f32[8192]{0:T(1024)S(1)}, f32[8192]{0:T(1024)}, u32[]{:S(2)}) copy-start(f32[8192]{0:T(1024)} %param.27) | copy-start | bytes 98308
  95.7 6.8 %copy-start.13 = (f32[2,256]{1,0:T(2,128)S(1)}, f32[2,256]{1,0:T(2,128)}, u32[]{:S(2)}) copy-start(f32[2,256]{1,0:T(2,128)} %param.31) | copy-start | bytes 6148
  100.5 1.9 %copy-start.1 = (bf16[256,8192]{1,0:T(8,128)(2,1)}, bf16[256,8192]{1,0:T(8,128)(2,1)S(1)}, u32[]{:S(2)}) copy-start(bf16[256,8192]{1,0:T(8,128)(2,1)S(1)} %get-tuple-element.12) | copy-start | bytes 12582916
  102.5 6.6 %copy-start.12 = (f32[2048]{0:T(1024)S(1)}, f32[2048]{0:T(1024)}, u32[]{:S(2)}) copy-start(f32[2048]{0:T(1024)} %param.29) | copy-start | bytes 24580
  128.2 2.3 %copy-start.2 = (bf16[32,16,8,128]{3,2,1,0:T(8,128)(2,1)S(1)}, bf16[32,16,8,128]{3,2,1,0:T(8,128)(2,1)}, u32[]{:S(2)}) copy-start(bf16[32,16,8,128]{3,2,1,0:T(8,128)(2,1)} %fusion.15) | copy-start | bytes 3145732
  131.8 1.3 copy-start.3
Sparse Core Ops, SparseCore 0:
  26.5 27.5 reduce-scatter.1
  72.3 13.0 all-gather.2
  109.2 16.8 all-gather.4
where the time goes:
time: 142 us
  waiting for transfers between devices  46.5 us (33%)
  matrix products  40 us (28%)
  local copies, waits for them, and re-layouts  24.4 us (17%)
  between operations  13.4 us (9%)
  other arithmetic  11.6 us (8%)
  starting transfers between devices  5.78 us (4%)
    reduce_scatter x1, waiting for transfers between devices, per_device(): lax.psum_scatter(partial_sum, 'mp', scatter_dimension=1, tiled=True)  27.3 us
    dot_general x1, matrix products, per_device(): jnp.dot(normed_seq, w_query, preferred_element_type=jnp.float32)  17.5 us
    all_gather x1, waiting for transfers between devices, per_device(): image_full = lax.all_gather(arrived, 'mp', axis=1, tiled=True)  11.1 us
    gather x1, local copies, waits for them, and re-layouts, per_device(): jnp.take(image_full, source_slot, axis=0)  10.3 us
    all_to_all x1, waiting for transfers between devices, per_device(): lax.all_to_all(outgoing.reshape(owners, capacity, col_width), ('group', '...  8.03 us
    dot_general x1, matrix products, per_device(): jnp.dot(merged, merge_up, preferred_element_type=jnp.float32)  7.49 us
    unnamed x31, local copies, waits for them, and re-layouts  6.67 us
    dot_general x1, matrix products, per_device(): jnp.einsum('sd,dtc->stc', normed_seq, w_keyval, preferred_element_type=jn...  6.55 us
  transfers between devices with their start and end apart: 4, of which 3 were waited for; matrix products, arithmetic and copies ran while one was open for 15% of the time, Pallas kernels for 0%

commit v1 on v0

--- a/solution.py
+++ b/solution.py
@@ -1,16 +1,428 @@
+import functools
 import math
 
 import jax
 import jax.numpy as jnp
 from jax import lax
+from jax.experimental import pallas as pl
+from jax.experimental.pallas import tpu as pltpu
 from jax.sharding import PartitionSpec as P
 
 HEADS = 64
 KV_HEADS = 8
 HEAD_DIM = 128
+DOC_MAX = 64
+
+BF16 = jnp.bfloat16
+F32 = jnp.float32
+VMEM = pl.BlockSpec(memory_space=pltpu.VMEM)
+SMEM = pl.BlockSpec(memory_space=pltpu.SMEM)
+ANY = pl.BlockSpec(memory_space=pl.ANY)
+MIB = 1 << 20
+
+
+def dot(a, b):
+    return jnp.dot(a, b, preferred_element_type=F32)
+
+
+def params(mib):
+    return pltpu.CompilerParams(vmem_limit_bytes=mib * MIB)
+
+
+def cost(flops, nbytes):
+    return pl.CostEstimate(flops=flops, bytes_accessed=nbytes, transcendentals=0)
+
+
+def rms_scale(x, width):
+    return lax.rsqrt(jnp.sum(x * x, axis=-1, keepdims=True) / width + 1e-06)
+
+
+def merger_kernel(
+    where, patch, gain, bias, up, up_bias, down, down_bias, send, keep,
+    normed, merged, up_buf, down_buf, bias_row, up_sem, down_sem,
+):
+    up_parts, down_parts = up_buf.shape[0], down_buf.shape[0]
+    step = up_buf.shape[1]
+    width = down_buf.shape[2]
+    half = send.shape[1]
+    per_half = half // width
+    mp = where[0]
+    mine = mp % 2
+
+    def up_copy(i):
+        return pltpu.make_async_copy(up.at[pl.ds(i * step, step)], up_buf.at[i], up_sem.at[i])
+
+    def down_copy(i):
+        first = (1 - mine) if i < per_half else mine
+        column = pl.multiple_of(first * half + (i % per_half) * width, 128)
+        return pltpu.make_async_copy(down.at[:, pl.ds(column, width)], down_buf.at[i], down_sem.at[i])
+
+    for i in range(up_parts):
+        up_copy(i).start()
+    for i in range(down_parts):
+        down_copy(i).start()
+
+    pixels = patch[...].astype(F32)
+    features = pixels.shape[1]
+    center = pixels - jnp.mean(pixels, axis=-1, keepdims=True)
+    spread = jnp.mean(center * center, axis=-1, keepdims=True)
+    patches = center * lax.rsqrt(spread + 1e-06) * gain[...] + bias[...]
+    rows = send.shape[0]
+    joined = patch.shape[0] // rows
+    for c in range(features // 128):
+        normed[c] = patches[:, c * 128 : (c + 1) * 128]
+        for j in range(joined):
+            merged[:, pl.ds(j * features + c * 128, 128)] = normed[c, pl.ds(j, rows, stride=joined), :].astype(BF16)
+    bias_row[...] = jnp.zeros_like(bias_row)
+    own = down_bias.shape[1]
+    bias_row[:, pl.ds(pl.multiple_of(mp * own, 128), own)] = down_bias[...]
+
+    total = jnp.zeros((rows, up.shape[1]), F32)
+    for i in range(up_parts):
+        up_copy(i).wait()
+        total = total + dot(merged[:, pl.ds(i * step, step)], up_buf[i])
+    total = total + up_bias[...]
+    hidden = (0.5 * total * (1.0 + lax.erf(total * math.sqrt(0.5)))).astype(BF16)
+    for i in range(down_parts):
+        first = (1 - mine) if i < per_half else mine
+        column = (i % per_half) * width
+        out = send if i < per_half else keep
+        add = bias_row[:, pl.ds(pl.multiple_of(first * half + column, 128), width)]
+        down_copy(i).wait()
+        out[:, pl.ds(column, width)] = (dot(hidden, down_buf[i]) + add).astype(BF16)
+
+
+def merger(where, patch, gain, bias, up, up_bias, down, down_bias, rows):
+    features = patch.shape[1]
+    depth, hidden = up.shape
+    columns = down.shape[1]
+    step = features // 2
+    width = columns // 8
+    return pl.pallas_call(
+        merger_kernel,
+        out_shape=[jax.ShapeDtypeStruct((rows, columns // 2), BF16)] * 2,
+        in_specs=[SMEM, VMEM, VMEM, VMEM, ANY, VMEM, ANY, VMEM],
+        out_specs=[VMEM, VMEM],
+        scratch_shapes=[
+            pltpu.VMEM((features // 128, patch.shape[0], 128), F32),
+            pltpu.VMEM((rows, depth), BF16),
+            pltpu.VMEM((depth // step, step, hidden), BF16),
+            pltpu.VMEM((8, hidden, width), BF16),
+            pltpu.VMEM((1, columns), F32),
+            pltpu.SemaphoreType.DMA((depth // step,)),
+            pltpu.SemaphoreType.DMA((8,)),
+        ],
+        compiler_params=params(44),
+        cost_estimate=cost(2 * rows * hidden * (depth + columns), 2 * hidden * (depth + columns)),
+        name="merger",
+    )(where, patch, gain, bias, up, up_bias, down, down_bias)
+
+
+def text_norm_kernel(text, gain, out):
+    x = text[...].astype(F32)
+    out[...] = (x * rms_scale(x, x.shape[1]) * gain[...]).astype(BF16)
+
+
+def text_norm(text, gain):
+    rows, width = text.shape
+    block = 32
+    return pl.pallas_call(
+        text_norm_kernel,
+        out_shape=jax.ShapeDtypeStruct((rows, width), BF16),
+        grid=(rows // block,),
+        in_specs=[pl.BlockSpec((block, width), lambda i: (i, 0)), pl.BlockSpec((1, width), lambda i: (0, 0))],
+        out_specs=pl.BlockSpec((block, width), lambda i: (i, 0)),
+        compiler_params=params(12),
+        cost_estimate=cost(4 * rows * width, 4 * rows * width),
+        name="text_norm",
+    )(text, gain)
+
+
+def keyval_kernel(where, text, own, sibling, gain, weight, bias, image, *rest):
+    parts = rest[:-3]
+    rows_all, buf, sem = rest[-3:]
+    steps = buf.shape[0]
+    depth = weight.shape[1]
+    step = depth // (steps // 2)
+    copies = []
+    for i in range(steps):
+        t, k = i % 2, (i // 2) * step
+        copies.append(pltpu.make_async_copy(weight.at[t, pl.ds(k, step)], buf.at[i], sem.at[i]))
+        copies[-1].start()
+    mp = where[0]
+    half = own.shape[1]
+    texts, images = text.shape[0], own.shape[0]
+    mine = mp % 2
+    first, second = own[...].astype(F32), sibling[...].astype(F32)
+    squares = jnp.sum(first * first, axis=-1, keepdims=True) + jnp.sum(second * second, axis=-1, keepdims=True)
+    scale = lax.rsqrt(squares / (2 * half) + 1e-06)
+    for values, which in ((first, mine), (second, 1 - mine)):
+        here = pl.ds(pl.multiple_of(which * half, 128), half)
+        image[:, here] = (values * scale * gain[:, here]).astype(BF16)
+    rows_all[pl.ds(0, texts), :] = text[...]
+    rows_all[pl.ds(texts, images), :] = image[...]
+    columns = weight.shape[2]
+    totals = [jnp.zeros((texts + images, columns), F32)] * 2
+    for i in range(steps):
+        t, k = i % 2, (i // 2) * step
+        copies[i].wait()
+        totals[t] = totals[t] + dot(rows_all[:, pl.ds(k, step)], buf[i])
+    keyval = [(totals[t] + bias[pl.ds(t, 1), :]).astype(BF16) for t in range(2)]
+    count = len(parts)
+    width = parts[0].shape[1]
+    heads = KV_HEADS // count
+    coords = columns // KV_HEADS
+    row = lax.broadcasted_iota(jnp.int32, (columns, width // 2), 0)
+    column = lax.broadcasted_iota(jnp.int32, (columns, width // 2), 1)
+    for x in range(count):
+        head = (mp ^ x) * heads + column // coords
+        pick = (row == (column % coords) * KV_HEADS + head).astype(BF16)
+        for t in range(2):
+            parts[x][:, pl.ds(t * (width // 2), width // 2)] = dot(keyval[t], pick).astype(BF16)
+
+
+def keyval_parts(where, text, own, sibling, gain, weight, bias, count):
+    texts, depth = text.shape
+    images = own.shape[0]
+    columns = weight.shape[2]
+    rows = texts + images
+    steps = 8
+    width = 2 * columns // count
+    outs = pl.pallas_call(
+        keyval_kernel,
+        out_shape=[jax.ShapeDtypeStruct((images, depth), BF16)]
+        + [jax.ShapeDtypeStruct((rows, width), BF16)] * count,
+        in_specs=[SMEM, VMEM, VMEM, VMEM, VMEM, ANY, VMEM],
+        out_specs=[VMEM] * (1 + count),
+        scratch_shapes=[
+            pltpu.VMEM((rows, depth), BF16),
+            pltpu.VMEM((steps, depth // (steps // 2), columns), BF16),
+            pltpu.SemaphoreType.DMA((steps,)),
+        ],
+        compiler_params=params(32),
+        cost_estimate=cost(4 * rows * depth * columns, 4 * depth * columns),
+        name="keyval",
+    )(where, text, own, sibling, gain, weight, bias)
+    return outs[0], outs[1:]
+
+
+def query_kernel(text, image, weight, bias, text_out, image_out, rows_all, buf, sem):
+    steps = buf.shape[0]
+    width = buf.shape[2]
+    copies = []
+    for i in range(steps):
+        copies.append(pltpu.make_async_copy(weight.at[:, pl.ds(i * width, width)], buf.at[i], sem.at[i]))
+        copies[-1].start()
+    texts, images = text.shape[0], image.shape[0]
+    rows_all[pl.ds(0, texts), :] = text[...]
+    rows_all[pl.ds(texts, images), :] = image[...]
+    for i in range(steps):
+        here = pl.ds(i * width, width)
+        copies[i].wait()
+        out = (dot(rows_all[...], buf[i]) + bias[:, here]).astype(BF16)
+        text_out[:, here] = out[:texts]
+        image_out[:, here] = out[texts:]
+
+
+def query_rows(text, image, weight, bias):
+    texts, depth = text.shape
+    images = image.shape[0]
+    columns = weight.shape[1]
+    steps = columns // 256
+    return pl.pallas_call(
+        query_kernel,
+        out_shape=[jax.ShapeDtypeStruct((texts, columns), BF16), jax.ShapeDtypeStruct((images, columns), BF16)],
+        in_specs=[VMEM, VMEM, ANY, VMEM],
+        out_specs=[VMEM, VMEM],
+        scratch_shapes=[
+            pltpu.VMEM((texts + images, depth), BF16),
+            pltpu.VMEM((steps, depth, columns // steps), BF16),
+            pltpu.SemaphoreType.DMA((steps,)),
+        ],
+        compiler_params=params(52),
+        cost_estimate=cost(2 * (texts + images) * depth * columns, 2 * depth * columns),
+        name="query",
+    )(text, image, weight, bias)
+
+
+def join_parts(mp, parts, first_row, rows):
+    count = len(parts)
+    width = parts[0].shape[1]
+    heads = KV_HEADS // count
+    coords = HEAD_DIM // count
+    full = 2 * heads * HEAD_DIM
+    row = lax.broadcasted_iota(jnp.int32, (width, full), 0)
+    column = lax.broadcasted_iota(jnp.int32, (width, full), 1)
+    total = jnp.zeros((rows, full), F32)
+    for x in range(count):
+        coordinate = (mp ^ x) * coords + row % coords
+        place = (column == (row // coords) * HEAD_DIM + coordinate).astype(BF16)
+        total = total + dot(parts[x][pl.ds(first_row, rows), :], place)
+    return total.astype(BF16)
+
+
+def slots_kernel(where, owner_rows, owner_columns, queries, *rest):
+    parts, out = rest[:-1], rest[-1]
+    owners = owner_rows.shape[0]
+    rows, columns = queries.shape
+    slots = out.shape[0]
+    mp, me = where[0], where[1]
+    down = owner_columns[pl.ds(pl.multiple_of(me * rows, rows), rows), :]
+    across = owner_rows[pl.ds(me, 1), :]
+    earlier = lax.broadcasted_iota(jnp.int32, (rows, rows), 0) < lax.broadcasted_iota(jnp.int32, (rows, rows), 1)
+    rank = jnp.sum(jnp.where((down == across) & earlier, 1, 0), axis=0, keepdims=True)
+    slot = across * (slots // owners) + rank
+    select = (lax.broadcasted_iota(jnp.int32, (slots, rows), 0) == slot).astype(F32).astype(BF16)
+    out[:, pl.ds(0, columns)] = dot(select, queries[...]).astype(BF16)
+    keyval = join_parts(mp, parts, parts[0].shape[0] - rows, rows)
+    out[:, pl.ds(columns, out.shape[1] - columns)] = dot(select, keyval).astype(BF16)
+
+
+def slots_of(where, owner_rows, owner_columns, queries, parts, capacity):
+    slots = owner_rows.shape[0] * capacity
+    width = queries.shape[1] + 2 * (KV_HEADS // len(parts)) * HEAD_DIM
+    return pl.pallas_call(
+        slots_kernel,
+        out_shape=jax.ShapeDtypeStruct((slots, width), BF16),
+        in_specs=[SMEM] + [VMEM] * (3 + len(parts)),
+        out_specs=VMEM,
+        compiler_params=params(12),
+        name="slots",
+    )(where, owner_rows, owner_columns, queries, *parts)
+
+
+def attention_kernel(where, owner_rows, doc_row, doc_column, queries, arrived, *rest):
+    parts = rest[:-4]
+    out, q_all, kv_all, window = rest[-4:]
+    mp, me = where[0], where[1]
+    seq = queries.shape[0]
+    columns = queries.shape[1]
+    slots = arrived.shape[0]
+    owners = owner_rows.shape[0]
+    capacity = slots // owners
+    incoming = jnp.sum(jnp.where(owner_rows[...] == me, 1, 0), axis=1, keepdims=True)
+    source = lax.broadcasted_iota(jnp.int32, (owners, slots), 0)
+    slot = lax.broadcasted_iota(jnp.int32, (owners, slots), 1)
+    offset = jnp.sum(jnp.where(source < slot // capacity, incoming, 0), axis=0, keepdims=True)
+    here = jnp.sum(jnp.where(source == slot // capacity, incoming, 0), axis=0, keepdims=True)
+    index = lax.broadcasted_iota(jnp.int32, (1, slots), 1) % capacity
+    target = jnp.where(index < here, offset + index, -1)
+    position = lax.broadcasted_iota(jnp.int32, (slots, slots), 0)
+    place = (position == target).astype(F32).astype(BF16)
+    placed = dot(place, arrived[...]).astype(BF16)
+    count = jnp.sum(incoming, axis=0, keepdims=True)
+    is_image = lax.broadcasted_iota(jnp.int32, (slots, 1), 0) < count
+
+    keyval = join_parts(mp, parts, 0, seq)
+    kv_all[...] = keyval
+    kv_all[pl.ds(0, slots), :] = jnp.where(is_image, placed[:, columns:], keyval[:slots])
+    q_all[...] = queries[...]
+    q_all[pl.ds(0, slots), :] = jnp.where(is_image, placed[:, :columns], queries[pl.ds(0, slots), :])
+
+    heads = columns // HEAD_DIM
+    groups = kv_all.shape[1] // (2 * HEAD_DIM)
+    shared = heads // groups
+    block = DOC_MAX
+    scale = 1.0 / math.sqrt(HEAD_DIM)
+    for b in range(seq // block):
+        q0 = b * block
+        k0 = max(0, q0 - block)
+        q_doc = doc_column[pl.ds(q0, block), :]
+        k_doc = doc_row[:, pl.ds((k0 // 128) * 128, 128)] if k0 % 128 == 0 else window[pl.ds(b, 1), :]
+        q_pos = q0 + lax.broadcasted_iota(jnp.int32, (block, 2 * block), 0)
+        k_pos = k0 + lax.broadcasted_iota(jnp.int32, (block, 2 * block), 1)
+        allowed = (q_doc == k_doc) & (k_pos <= q_pos)
+        allowed = jnp.concatenate([allowed.astype(jnp.int32)] * shared, axis=0) > 0
+        for g in range(groups):
+            keys = kv_all[pl.ds(k0, 2 * block), pl.ds(g * HEAD_DIM, HEAD_DIM)]
+            values = kv_all[pl.ds(k0, 2 * block), pl.ds((groups + g) * HEAD_DIM, HEAD_DIM)]
+            q = jnp.concatenate(
+                [q_all[pl.ds(q0, block), pl.ds((g * shared + h) * HEAD_DIM, HEAD_DIM)] for h in range(shared)], axis=0
+            )
+            scores = lax.dot_general(q, keys, (((1,), (1,)), ((), ())), preferred_element_type=F32) * scale
+            scores = jnp.where(allowed, scores, F32(-1e30))
+            weights = jnp.exp(scores - jnp.max(scores, axis=-1, keepdims=True))
+            probs = (weights / jnp.sum(weights, axis=-1, keepdims=True)).astype(BF16)
+            result = dot(probs, values).astype(BF16)
+            for h in range(shared):
+                out[pl.ds(q0, block), pl.ds((g * shared + h) * HEAD_DIM, HEAD_DIM)] = result[h * block : (h + 1) * block]
+
+
+def attention(where, owner_rows, documents, queries, arrived, parts):
+    seq, columns = queries.shape
+    width = 2 * (KV_HEADS // len(parts)) * HEAD_DIM
+
+    def body(where, owner_rows, doc_row, doc_column, doc_windows, *rest):
+        attention_kernel(where, owner_rows, doc_row, doc_column, *rest, doc_windows)
+
+    blocks = seq // DOC_MAX
+    windows = jnp.stack([documents[max(0, b - 1) * DOC_MAX :][: 2 * DOC_MAX] for b in range(blocks)])
+    return pl.pallas_call(
+        body,
+        out_shape=jax.ShapeDtypeStruct((seq, columns), BF16),
+        in_specs=[SMEM] + [VMEM] * (6 + len(parts)),
+        out_specs=VMEM,
+        scratch_shapes=[pltpu.VMEM((seq, columns), BF16), pltpu.VMEM((seq, width), BF16)],
+        compiler_params=params(24),
+        name="attention",
+    )(where, owner_rows, documents[None, :], documents[:, None], windows, queries, arrived, *parts)
+
+
+def exchange(x, count, bit):
+    return lax.ppermute(x, "mp", [(i, i ^ bit) for i in range(count)])
 
 
 def per_device(
+    patch_rows,
+    ln_gain,
+    ln_bias,
+    merge_up,
+    merge_up_bias,
+    merge_down,
+    merge_down_bias,
+    row_owner,
+    text_embed,
+    doc_ids,
+    rms_gain,
+    w_query,
+    query_bias,
+    w_keyval,
+    keyval_bias,
+):
+    owners = lax.axis_size(("group", "dp"))
+    count = lax.axis_size("mp")
+    mp_index = lax.axis_index("mp")
+    where = jnp.stack([mp_index, lax.axis_index(("group", "dp"))]).astype(jnp.int32)
+    rows = row_owner.shape[0] // owners
+    capacity = max(2, 2 * rows // owners)
+    gain = rms_gain[None, :]
+    owner_rows = row_owner.reshape(owners, rows)
+
+    send, keep = merger(
+        where, patch_rows[0], ln_gain[None, :], ln_bias[None, :], merge_up, merge_up_bias[None, :],
+        merge_down, merge_down_bias[None, :], rows,
+    )
+    text = text_norm(text_embed[0], gain)
+    weight = jnp.transpose(w_keyval, (1, 0, 2))
+
+    own = (keep.astype(F32) + exchange(send, count, 1).astype(F32)).astype(BF16)
+    bit = 2
+    while bit < count:
+        own = (own.astype(F32) + exchange(own, count, bit).astype(F32)).astype(BF16)
+        bit *= 2
+    sibling = exchange(own, count, 1)
+
+    image, parts = keyval_parts(where, text, own, sibling, gain, weight, keyval_bias, count)
+    parts = [parts[0]] + [exchange(parts[x], count, x) for x in range(1, count)]
+    text_queries, image_queries = query_rows(text, image, w_query, query_bias[None, :])
+    outgoing = slots_of(where, owner_rows, row_owner, image_queries, parts, capacity)
+    arrived = lax.all_to_all(
+        outgoing.reshape(owners, capacity, -1), ("group", "dp"), split_axis=0, concat_axis=0, tiled=True
+    ).reshape(owners * capacity, -1)
+    return attention(where, owner_rows, doc_ids[0], text_queries, arrived, parts)[None]
+
+
+def general(
     patch_rows,
     ln_gain,
     ln_bias,
@@ -136,6 +548,7 @@
         P(None, "mp"),
     )
     out_specs = P(("group", "dp"), None, "mp")
-    return jax.shard_map(
-        per_device, mesh=mesh, in_specs=in_specs, out_specs=out_specs, check_vma=False
-    )
+    count = mesh.shape["mp"]
+    narrow = count < 2 or count > KV_HEADS or count & (count - 1)
+    body = general if narrow else per_device
+    return jax.shard_map(body, mesh=mesh, in_specs=in_specs, out_specs=out_specs, check_vma=False)

time: 142 us -> 105 us (0.74)
  Pallas kernels: 0 us -> 57.2 us
  matrix products: 40 us -> 0 us
  waiting for transfers between devices: 46.5 us -> 19.5 us
  between operations: 13.4 us -> 0.17 us
  other arithmetic: 11.6 us -> 0.88 us
  local copies, waits for them, and re-layouts: 24.4 us -> 14.8 us
  starting transfers between devices: 5.78 us -> 11.6 us
    pallas_call x0 -> x6, Pallas kernels: none -> 57.2 us  [the longest x1 25.3 us: query_rows(): pl.pallas_call(query_kernel, out_shape=[jax.ShapeDtypeStruct((texts, colu...]
    dot_general x7 -> x0, matrix products: 40 us -> none  [the longest x1 17.5 us: per_device(): jnp.dot(normed_seq, w_query, preferred_element_type=jnp.float32)]
    reduce_scatter x1 -> x0, waiting for transfers between devices: 27.3 us -> none  [per_device(): lax.psum_scatter(partial_sum, 'mp', scatter_dimension=1, tiled=True)]
    gather x3 -> x0, local copies, waits for them, and re-layouts: 12.5 us -> none  [the longest x1 10.3 us: per_device(): jnp.take(image_full, source_slot, axis=0)]
    all_gather x2 -> x0, waiting for transfers between devices: 11.1 us -> none  [the longest x1 11.1 us: per_device(): image_full = lax.all_gather(arrived, 'mp', axis=1, tiled=True)]
    reduce_sum x7 -> x0, other arithmetic: 8.52 us -> none  [the longest x1 4.87 us: per_device(): jnp.mean(seq_f * seq_f, axis=-1, keepdims=True) + 1e-06]
    ppermute x0 -> x6, waiting for transfers between devices: none -> 7.78 us  [exchange(): return lax.ppermute(x, 'mp', [(i, i ^ bit) for i in range(count)])]
    ppermute x0 -> x6, starting transfers between devices: none -> 5.84 us  [exchange(): return lax.ppermute(x, 'mp', [(i, i ^ bit) for i in range(count)])]
  transfers between devices with their start and end apart: 4 -> 7, of which waited for: 3 -> 3; matrix products, arithmetic and copies ran while one was open for 15% -> 9% of each run, Pallas kernels for 0% -> 27%
where the time goes in v1:
time: 105 us; the launch traced here: 104 us
  Pallas kernels  57.2 us (54%)
  waiting for transfers between devices  19.5 us (19%)
  local copies, waits for them, and re-layouts  14.8 us (14%)
  starting transfers between devices  11.6 us (11%)
    pallas_call x1, Pallas kernels, query_rows(): pl.pallas_call(query_kernel, out_shape=[jax.ShapeDtypeStruct((texts, colu...  25.3 us
    pallas_call x1, Pallas kernels, merger(): pl.pallas_call(merger_kernel, out_shape=[jax.ShapeDtypeStruct((rows, colu...  16 us
    unnamed x23, local copies, waits for them, and re-layouts  12.4 us
    all_to_all x1, waiting for transfers between devices, per_device(): lax.all_to_all(outgoing.reshape(owners, capacity, -1), ('group', 'dp'), s...  11.7 us
    pallas_call x1, Pallas kernels, keyval_parts(): pl.pallas_call(keyval_kernel, out_shape=[jax.ShapeDtypeStruct((images, de...  7.83 us
    ppermute x6, waiting for transfers between devices, exchange(): return lax.ppermute(x, 'mp', [(i, i ^ bit) for i in range(count)])  7.78 us
    ppermute x6, starting transfers between devices, exchange(): return lax.ppermute(x, 'mp', [(i, i ^ bit) for i in range(count)])  5.84 us
    all_to_all x1, starting transfers between devices, per_device(): lax.all_to_all(outgoing.reshape(owners, capacity, -1), ('group', 'dp'), s...  5.81 us
  transfers between devices with their start and end apart: 7, of which 3 were waited for; matrix products, arithmetic and copies ran while one was open for 9% of the time, Pallas kernels for 27%

profile of v1, /device:TPU:0, one launch (start us, length us, event | category | flops | bytes accessed | tf_op | source)
XLA Modules:
  0.0 104.2 jit_solution(12570957210073955489)
XLA Ops:
  0.0 0.7 broadcast_in_dim.22.gain
  0.7 0.7 broadcast_in_dim.23.bias
  1.4 0.7 broadcast_in_dim.24.up_bias
  2.1 0.1 pad_add_fusion.1.where
  2.2 1.0 copy-done.3
  3.2 0.7 copy-done.6
  3.8 16.0 %merger.1 = (bf16[32,4096]{1,0:T(8,128)(2,1)S(1)}, bf16[32,4096]{1,0:T(8,128)(2,1)S(1)}) custom-call(s32[2]{0:T(128)S(1)} %pad_add_fusion.1.where, bf16[128,1280]{1,0:T(8,128)(2,1)S(1)} %bitcast.18, f32[1,1280]{1,0:T(1,128)S(1)} %broadcast_in_dim.22.gain, f32[1,1280]{1,0:T(1,128)S(1)} %broadcast_in_dim.23.bias, bf16[5120,1280]{1,0:T(8,128)(2,1)} %up.1, ...), custom_call_target="tpu_custom_call" | custom-call | flops 1090519040 | bytes 34078720 | tf_op jit(solution)/shard_map/merger/pallas_call | solution.py:101
  19.9 0.5 collective-permute-start
  20.4 1.2 %collective-permute-done = bf16[32,4096]{1,0:T(8,128)(2,1)S(1)} collective-permute-done((bf16[32,4096]{1,0:T(8,128)(2,1)S(1)}, bf16[32,4096]{1,0:T(8,128)(2,1)S(1)}, u32[]{:S(2)}, u32[]{:S(2)}) %collective-permute-start) | collective-permute-done | bytes 262176 | tf_op jit(solution)/shard_map/ppermute | solution.py:372
  21.6 0.1 add_convert_fusion.1
  21.6 3.0 %collective-permute-start.1 = (bf16[32,4096]{1,0:T(8,128)(2,1)S(1)}, bf16[32,4096]{1,0:T(8,128)(2,1)S(1)}, u32[]{:S(2)}, u32[]{:S(2)}) collective-permute-start(bf16[32,4096]{1,0:T(8,128)(2,1)S(1)} %add_convert_fusion.1), channel_id=1, source_target_pairs={{0,2},{1,3},{2,0},{3,1},{4,6},{5,7},{6,4},{7,5},{8,10},{9,11},{10,... | collective-permute-start | bytes 786440 | tf_op jit(solution)/shard_map/ppermute | solution.py:372
  24.6 6.6 %collective-permute-done.1 = bf16[32,4096]{1,0:T(8,128)(2,1)S(1)} collective-permute-done((bf16[32,4096]{1,0:T(8,128)(2,1)S(1)}, bf16[32,4096]{1,0:T(8,128)(2,1)S(1)}, u32[]{:S(2)}, u32[]{:S(2)}) %collective-permute-start.1) | collective-permute-done | bytes 262176 | tf_op jit(solution)/shard_map/ppermute | solution.py:372
  31.2 0.1 add_convert_fusion.own
  31.3 0.1 collective-permute-start.2
  31.4 7.7 %copy.22 = bf16[8192,2,256]{2,0,1:T(8,128)(2,1)} copy(bf16[8192,2,256]{2,1,0:T(2,128)(2,1)} %param.28) | data formatting | bytes 16777216 | tf_op args[13]
  39.1 0.1 copy.19.owner_columns
  39.2 0.5 broadcast.3
  39.7 0.7 reduce.3
  40.4 0.1 reshape.16.owner_rows
  40.5 2.3 %copy-done.2 = bf16[1,256,8192]{2,1,0:T(8,128)(2,1)S(1)} copy-done((bf16[1,256,8192]{2,1,0:T(8,128)(2,1)S(1)}, bf16[1,256,8192]{2,1,0:T(8,128)(2,1)}, u32[]{:S(2)}) %copy-start.2) | copy-done | bytes 4194328
  42.8 2.7 %text_norm.1.text = bf16[256,8192]{1,0:T(8,128)(2,1)S(1)} custom-call(bf16[256,8192]{1,0:T(8,128)(2,1)S(1)} %bitcast.16, f32[1,8192]{1,0:T(1,128)S(1)} %bitcast.19), custom_call_target="tpu_custom_call" | custom-call | flops 8388608 | bytes 8388608 | tf_op jit(solution)/shard_map/text_norm/pallas_call | solution.py:129
  45.5 0.0 copy-start.7
  45.6 7.8 %keyval.1 = (bf16[32,8192]{1,0:T(8,128)(2,1)S(1)}, bf16[288,128]{1,0:T(8,128)(2,1)S(1)}, bf16[288,128]{1,0:T(8,128)(2,1)S(1)}, bf16[288,128]{1,0:T(8,128)(2,1)S(1)}, bf16[288,128]{1,0:T(8,128)(2,1)S(1)}) custom-call(s32[2]{0:T(128)S(1)} %pad_add_fusion.1.where, bf16[256,8192]{1,0:T(8,128)(2,1)S(1)} %text_norm.1.text, ...), custom_call_target="tpu_custom_call" | custom-call | flops 2415919104 | bytes 8388608 | tf_op jit(solution)/shard_map/keyval/pallas_call | solution.py:191
  53.4 0.6 collective-permute-start.3
  54.0 1.7 %collective-permute-start.4 = (bf16[288,128]{1,0:T(8,128)(2,1)S(1)}, bf16[288,128]{1,0:T(8,128)(2,1)S(1)}, u32[]{:S(2)}, u32[]{:S(2)}) collective-permute-start(bf16[288,128]{1,0:T(8,128)(2,1)S(1)} %get-tuple-element.21), channel_id=1, source_target_pairs={{0,2},{1,3},{2,0},{3,1},{4,6},{5,7},{6,4},{7,5},{8,10},{9,11},{10,... | collective-permute-start | bytes 221192 | tf_op jit(solution)/shard_map/ppermute | solution.py:372
  55.7 25.3 %query.1 = (bf16[256,2048]{1,0:T(8,128)(2,1)S(1)}, bf16[32,2048]{1,0:T(8,128)(2,1)S(1)}) custom-call(bf16[256,8192]{1,0:T(8,128)(2,1)} %copy-done, bf16[32,8192]{1,0:T(8,128)(2,1)S(1)} %get-tuple-element.16.image, bf16[8192,2048]{1,0:T(8,128)(2,1)} %weight.1, f32[1,2048]{1,0:T(1,128)S(1)} %bitcast.23), custom_call_target="tpu_custom_call" | custom-call | flops 9663676416 | bytes 33554432 | tf_op jit(solution)/shard_map/query/pallas_call | solution.py:232
  81.0 1.8 %slots.1 = bf16[64,2560]{1,0:T(8,128)(2,1)} custom-call(s32[2]{0:T(128)S(1)} %pad_add_fusion.1.where, s32[8,32]{1,0:T(8,128)S(1)} %reshape.16.owner_rows, s32[256,1]{1,0:T(8,128)S(1)} %copy.19.owner_columns, bf16[32,2048]{1,0:T(8,128)(2,1)S(1)} %get-tuple-element.18.queries, bf16[288,128]{1,0:T(8,128)(2,1)S(1)} %get-tuple-element.19.rest_0_.rest_2_, ...), custom_call_target="tpu_custom_call" | custom-call | tf_op jit(solution)/shard_map/slots/pallas_call | solution.py:284
  82.8 5.8 %all-to-all-start = ((bf16[8,8,2560]{2,1,0:T(8,128)(2,1)}), bf16[8,8,2560]{2,1,0:T(8,128)(2,1)S(1)}, u32[]{:S(2)}, u32[]{:S(2)}) async-start(bf16[8,8,2560]{2,1,0:T(8,128)(2,1)} %bitcast.9), calls=%async_computation | async-start | bytes 655360 | tf_op jit(solution)/shard_map/all_to_all | solution.py:419
  88.6 0.1 copy.20.doc_column
  88.8 0.1 fusion
  88.9 11.7 %all-to-all-done = bf16[8,8,2560]{2,1,0:T(8,128)(2,1)S(1)} async-done(((bf16[8,8,2560]{2,1,0:T(8,128)(2,1)}), bf16[8,8,2560]{2,1,0:T(8,128)(2,1)S(1)}, u32[]{:S(2)}, u32[]{:S(2)}) %all-to-all-start) | async-done | bytes 327712 | tf_op jit(solution)/shard_map/all_to_all | solution.py:419
  100.6 3.6 %attention.1 = bf16[256,2048]{1,0:T(8,128)(2,1)} custom-call(s32[2]{0:T(128)S(1)} %pad_add_fusion.1.where, s32[8,32]{1,0:T(8,128)S(1)} %reshape.16.owner_rows, s32[1,256]{1,0:T(1,128)S(1)} %copy-done.5, s32[256,1]{1,0:T(8,128)S(1)} %copy.20.doc_column, s32[4,128]{1,0:T(4,128)S(1)} %pad_add_fusion.doc_windows, ...), custom_call_target="tpu_custom_call" | custom-call | tf_op jit(solution)/shard_map/attention/pallas_call | solution.py:360
  (22 shorter events, 0.1 us)
Async XLA Ops:
  2.2 1.0 copy-start.3
  3.2 0.7 copy-start.6
  19.9 1.7 %collective-permute-start = (bf16[32,4096]{1,0:T(8,128)(2,1)S(1)}, bf16[32,4096]{1,0:T(8,128)(2,1)S(1)}, u32[]{:S(2)}, u32[]{:S(2)}) collective-permute-start(bf16[32,4096]{1,0:T(8,128)(2,1)S(1)} %get-tuple-element.15), channel_id=1, source_target_pairs={{0,1},{1,0},{2,3},{3,2},{4,5},{5,4},{6,7},{7,6},{8,9},{9,8},{10,11... | collective-permute-start | bytes 786440 | tf_op jit(solution)/shard_map/ppermute | solution.py:372
  21.6 9.6 %collective-permute-start.1 = (bf16[32,4096]{1,0:T(8,128)(2,1)S(1)}, bf16[32,4096]{1,0:T(8,128)(2,1)S(1)}, u32[]{:S(2)}, u32[]{:S(2)}) collective-permute-start(bf16[32,4096]{1,0:T(8,128)(2,1)S(1)} %add_convert_fusion.1), channel_id=1, source_target_pairs={{0,2},{1,3},{2,0},{3,1},{4,6},{5,7},{6,4},{7,5},{8,10},{9,11},{10,... | collective-permute-start | bytes 786440 | tf_op jit(solution)/shard_map/ppermute | solution.py:372
  31.3 7.8 %copy-start.9 = (s32[256,1]{0,1:T(1,128)S(1)}, s32[256,1]{0,1:T(1,128)}, u32[]{:S(2)}) copy-start(s32[256,1]{0,1:T(1,128)} %param.22) | copy-start | bytes 3076
  31.3 9.2 %copy-start.4 = (f32[8192]{0:T(1024)S(1)}, f32[8192]{0:T(1024)}, u32[]{:S(2)}) copy-start(f32[8192]{0:T(1024)} %param.25) | copy-start | bytes 98308
  31.3 14.3 %collective-permute-start.2 = (bf16[32,4096]{1,0:T(8,128)(2,1)S(1)}, bf16[32,4096]{1,0:T(8,128)(2,1)S(1)}, u32[]{:S(2)}, u32[]{:S(2)}) collective-permute-start(bf16[32,4096]{1,0:T(8,128)(2,1)S(1)} %add_convert_fusion.own), channel_id=1, source_target_pairs={{0,1},{1,0},{2,3},{3,2},{4,5},{5,4},{6,7},{7,6},{8,9},{9,8},{10,11... | collective-permute-start | bytes 786440 | tf_op jit(solution)/shard_map/ppermute | solution.py:372
  39.1 6.5 %copy-start.8 = (f32[2,256]{1,0:T(2,128)S(1)}, f32[2,256]{1,0:T(2,128)}, u32[]{:S(2)}) copy-start(f32[2,256]{1,0:T(2,128)} %bias.1) | copy-start | bytes 6148
  40.5 5.1 %copy-start.1 = (bf16[8192,2,256]{2,0,1:T(8,128)(2,1)S(1)}, bf16[8192,2,256]{2,0,1:T(8,128)(2,1)}, u32[]{:S(2)}) copy-start(bf16[8192,2,256]{2,0,1:T(8,128)(2,1)} %copy.22) | copy-start | bytes 25165828
  40.5 2.3 %copy-start.2 = (bf16[1,256,8192]{2,1,0:T(8,128)(2,1)S(1)}, bf16[1,256,8192]{2,1,0:T(8,128)(2,1)}, u32[]{:S(2)}) copy-start(bf16[1,256,8192]{2,1,0:T(8,128)(2,1)} %param.23) | copy-start | bytes 12582916
  45.5 10.2 %copy-start = (bf16[256,8192]{1,0:T(8,128)(2,1)}, bf16[256,8192]{1,0:T(8,128)(2,1)S(1)}, u32[]{:S(2)}) copy-start(bf16[256,8192]{1,0:T(8,128)(2,1)S(1)} %text_norm.1.text) | copy-start | bytes 12582916
  45.5 10.2 %copy-start.7 = (f32[2048]{0:T(1024)S(1)}, f32[2048]{0:T(1024)}, u32[]{:S(2)}) copy-start(f32[2048]{0:T(1024)} %param.27) | copy-start | bytes 24580
  53.4 27.6 %collective-permute-start.3 = (bf16[288,128]{1,0:T(8,128)(2,1)S(1)}, bf16[288,128]{1,0:T(8,128)(2,1)S(1)}, u32[]{:S(2)}, u32[]{:S(2)}) collective-permute-start(bf16[288,128]{1,0:T(8,128)(2,1)S(1)} %get-tuple-element.20), channel_id=1, source_target_pairs={{0,1},{1,0},{2,3},{3,2},{4,5},{5,4},{6,7},{7,6},{8,9},{9,8},{10,11... | collective-permute-start | bytes 221192 | tf_op jit(solution)/shard_map/ppermute | solution.py:372
  54.0 27.1 %collective-permute-start.4 = (bf16[288,128]{1,0:T(8,128)(2,1)S(1)}, bf16[288,128]{1,0:T(8,128)(2,1)S(1)}, u32[]{:S(2)}, u32[]{:S(2)}) collective-permute-start(bf16[288,128]{1,0:T(8,128)(2,1)S(1)} %get-tuple-element.21), channel_id=1, source_target_pairs={{0,2},{1,3},{2,0},{3,1},{4,6},{5,7},{6,4},{7,5},{8,10},{9,11},{10,... | collective-permute-start | bytes 221192 | tf_op jit(solution)/shard_map/ppermute | solution.py:372
  55.7 25.3 %collective-permute-start.5 = (bf16[288,128]{1,0:T(8,128)(2,1)S(1)}, bf16[288,128]{1,0:T(8,128)(2,1)S(1)}, u32[]{:S(2)}, u32[]{:S(2)}) collective-permute-start(bf16[288,128]{1,0:T(8,128)(2,1)S(1)} %get-tuple-element.22), channel_id=1, source_target_pairs={{0,3},{1,2},{2,1},{3,0},{4,7},{5,6},{6,5},{7,4},{8,11},{9,10},{10,... | collective-permute-start | bytes 221192 | tf_op jit(solution)/shard_map/ppermute | solution.py:372
  55.7 32.9 %copy-start.5 = (s32[1,256]{1,0:T(1,128)S(1)}, s32[1,256]{1,0:T(1,128)}, u32[]{:S(2)}) copy-start(s32[1,256]{1,0:T(1,128)} %doc_row.1) | copy-start | bytes 3076
  82.8 17.8 %all-to-all-start = ((bf16[8,8,2560]{2,1,0:T(8,128)(2,1)}), bf16[8,8,2560]{2,1,0:T(8,128)(2,1)S(1)}, u32[]{:S(2)}, u32[]{:S(2)}) async-start(bf16[8,8,2560]{2,1,0:T(8,128)(2,1)} %bitcast.9), calls=%async_computation | async-start | bytes 655360 | tf_op jit(solution)/shard_map/all_to_all | solution.py:419

commit v2 on v1

v2 whole, which is shorter than its diff:
```python
import functools
import math

import jax
import jax.numpy as jnp
from jax import lax
from jax.experimental import pallas as pl
from jax.experimental.pallas import tpu as pltpu
from jax.sharding import PartitionSpec as P

HEADS = 64
KV_HEADS = 8
HEAD_DIM = 128
DOC_MAX = 64

BF16 = jnp.bfloat16
F32 = jnp.float32
VMEM = pl.BlockSpec(memory_space=pltpu.VMEM)
SMEM = pl.BlockSpec(memory_space=pltpu.SMEM)
ANY = pl.BlockSpec(memory_space=pl.ANY)
HBM = pl.BlockSpec(memory_space=pltpu.HBM)
AHEAD = 3
MIB = 1 << 20


def dot(a, b):
    return jnp.dot(a, b, preferred_element_type=F32)


def in_hbm(x):
    return pltpu.with_memory_space_constraint(x, pltpu.HBM)


def in_vmem(x):
    return pltpu.with_memory_space_constraint(x, pltpu.VMEM)


def params(mib):
    return pltpu.CompilerParams(vmem_limit_bytes=mib * MIB)


def cost(flops, nbytes):
    return pl.CostEstimate(flops=flops, bytes_accessed=nbytes, transcendentals=0)


def rms_scale(x, width):
    return lax.rsqrt(jnp.sum(x * x, axis=-1, keepdims=True) / width + 1e-06)


def stream(count, copy, body, then=None):
    @pl.loop(0, count)
    def _(i):
        copy(i).wait()

        @pl.when(i + AHEAD < count)
        def _():
            copy(i + AHEAD).start()

        if then is not None:

            @pl.when(i + AHEAD >= count)
            def _():
                then(i + AHEAD - count).start()

        body(i)


def begin(copy):
    for i in range(AHEAD):
        copy(i).start()


def tile(i, width):
    return pl.ds(pl.multiple_of(i * width, width), width)


def merger_kernel(
    where, patch_in, gain_in, bias_in, up, up_bias_in, down, down_bias_in, send, keep,
    patch, gain, bias, up_bias, down_bias, bias_row, normed, merged, total, up_buf, down_buf, small_sem, up_sem, down_sem,
):
    slots = AHEAD + 1
    step = up_buf.shape[1]
    width = down_buf.shape[2]
    half = send.shape[1]
    per_half = half // width
    mp = where[0]
    mine = mp % 2
    pairs = [(patch_in, patch), (gain_in, gain), (bias_in, bias), (up_bias_in, up_bias), (down_bias_in, down_bias)]
    small = [pltpu.make_async_copy(x, y, small_sem.at[i]) for i, (x, y) in enumerate(pairs)]
    for copy in small:
        copy.start()

    def up_copy(i):
        return pltpu.make_async_copy(up.at[tile(i, step)], up_buf.at[i % slots], up_sem.at[i % slots])

    def column(i):
        first = jnp.where(i < per_half, 1 - mine, mine)
        return pl.multiple_of(first * half + (i % per_half) * width, width)

    def down_copy(i):
        return pltpu.make_async_copy(
            down.at[:, pl.ds(column(i), width)], down_buf.at[i % slots], down_sem.at[i % slots]
        )

    begin(up_copy)
    for copy in small:
        copy.wait()
    rows = send.shape[0]
    joined = patch.shape[0] // rows
    features = patch.shape[1]
    pixels = patch[...].astype(F32)
    center = pixels - jnp.mean(pixels, axis=-1, keepdims=True)
    spread = jnp.mean(center * center, axis=-1, keepdims=True)
    patches = center * lax.rsqrt(spread + 1e-06) * gain[...][None, :] + bias[...][None, :]
    for c in range(features // 128):
        normed[c] = patches[:, c * 128 : (c + 1) * 128]
        for j in range(joined):
            merged[:, pl.ds(j * features + c * 128, 128)] = normed[c, pl.ds(j, rows, stride=joined), :].astype(BF16)
    own = down_bias.shape[0]
    bias_row[...] = jnp.zeros_like(bias_row)
    bias_row[:, pl.ds(pl.multiple_of(mp * own, 128), own)] = down_bias[...][None, :]
    total[...] = jnp.broadcast_to(up_bias[...][None, :], total.shape)

    def up_body(i):
        total[...] += dot(merged[:, tile(i, step)], up_buf[i % slots])

    stream(up.shape[0] // step, up_copy, up_body, down_copy)
    sums = total[...]
    hidden = (0.5 * sums * (1.0 + lax.erf(sums * math.sqrt(0.5)))).astype(BF16)

    def down_body(i):
        part = (dot(hidden, down_buf[i % slots]) + bias_row[:, pl.ds(column(i), width)]).astype(BF16)
        here = tile(i % per_half, width)

        @pl.when(i < per_half)
        def _():
            send[:, here] = part

        @pl.when(i >= per_half)
        def _():
            keep[:, here] = part

    stream(2 * per_half, down_copy, down_body)


def merger(where, patch, gain, bias, up, up_bias, down, down_bias, rows):
    features = patch.shape[1]
    depth, hidden = up.shape
    columns = down.shape[1]
    step = depth // 8
    width = columns // 8
    slots = AHEAD + 1
    return pl.pallas_call(
        merger_kernel,
        out_shape=[jax.ShapeDtypeStruct((rows, columns // 2), BF16)] * 2,
        in_specs=[SMEM] + [HBM] * 7,
        out_specs=[VMEM, VMEM],
        scratch_shapes=[
            pltpu.VMEM(patch.shape, BF16),
            pltpu.VMEM(gain.shape, F32),
            pltpu.VMEM(bias.shape, F32),
            pltpu.VMEM(up_bias.shape, F32),
            pltpu.VMEM(down_bias.shape, F32),
            pltpu.VMEM((1, columns), F32),
            pltpu.VMEM((features // 128, patch.shape[0], 128), F32),
            pltpu.VMEM((rows, depth), BF16),
            pltpu.VMEM((rows, hidden), F32),
            pltpu.VMEM((slots, step, hidden), BF16),
            pltpu.VMEM((slots, hidden, width), BF16),
            pltpu.SemaphoreType.DMA((5,)),
            pltpu.SemaphoreType.DMA((slots,)),
            pltpu.SemaphoreType.DMA((slots,)),
        ],
        compiler_params=params(28),
        cost_estimate=cost(2 * rows * hidden * (depth + columns), 2 * hidden * (depth + columns)),
        name="merger",
    )(where, *map(in_hbm, (patch, gain, bias, up, up_bias, down, down_bias)))


def keyval_kernel(where, text, own, sibling, gain, weight, bias, rows_all, *rest):
    parts = rest[:-5]
    buf, keyval, text_buf, sem, text_sem = rest[-5:]
    slots = AHEAD + 1
    block = text_buf.shape[1]
    texts, images = text.shape[0], own.shape[0]

    def text_copy(i):
        return pltpu.make_async_copy(text.at[tile(i, block)], text_buf.at[i % slots], text_sem.at[i % slots])

    def weight_copy(i):
        return pltpu.make_async_copy(weight.at[i], buf.at[i], sem.at[i])

    begin(text_copy)
    for i in range(2):
        weight_copy(i).start()
    mp = where[0]
    half = own.shape[1]
    mine = mp % 2
    first, second = own[...].astype(F32), sibling[...].astype(F32)
    squares = jnp.sum(first * first, axis=-1, keepdims=True) + jnp.sum(second * second, axis=-1, keepdims=True)
    scale = lax.rsqrt(squares / (2 * half) + 1e-06)
    for values, which in ((first, mine), (second, 1 - mine)):
        here = pl.ds(pl.multiple_of(which * half, half), half)
        rows_all[pl.ds(texts, images), here] = (values * scale * gain[:, here]).astype(BF16)

    def text_body(i):
        x = text_buf[i % slots].astype(F32)
        rows_all[tile(i, block), :] = (x * rms_scale(x, 2 * half) * gain[...]).astype(BF16)

    stream(texts // block, text_copy, text_body)

    @pl.loop(0, 2)
    def _(t):
        weight_copy(t).wait()
        keyval[t] = (dot(rows_all[...], buf[t]) + bias[pl.ds(t, 1), :]).astype(BF16)

    count = len(parts)
    columns = weight.shape[2]
    width = parts[0].shape[1]
    heads = KV_HEADS // count
    coords = columns // KV_HEADS
    row = lax.broadcasted_iota(jnp.int32, (columns, width // 2), 0)
    column = lax.broadcasted_iota(jnp.int32, (columns, width // 2), 1)
    for x in range(count):
        head = (mp ^ x) * heads + column // coords
        pick = (row == (column % coords) * KV_HEADS + head).astype(F32).astype(BF16)
        for t in range(2):
            parts[x][:, pl.ds(t * (width // 2), width // 2)] = dot(keyval[t], pick).astype(BF16)


def keyval_parts(where, text, own, sibling, gain, weight, bias, count):
    texts, depth = text.shape
    columns = weight.shape[2]
    rows = texts + own.shape[0]
    width = 2 * columns // count
    outs = pl.pallas_call(
        keyval_kernel,
        out_shape=[pltpu.VMEM((rows, depth), BF16)] + [jax.ShapeDtypeStruct((rows, width), BF16)] * count,
        in_specs=[SMEM, HBM, VMEM, VMEM, VMEM, HBM, VMEM],
        out_specs=[VMEM] * (1 + count),
        scratch_shapes=[
            pltpu.VMEM((2, depth, columns), BF16),
            pltpu.VMEM((2, rows, columns), BF16),
            pltpu.VMEM((AHEAD + 1, 32, depth), BF16),
            pltpu.SemaphoreType.DMA((2,)),
            pltpu.SemaphoreType.DMA((AHEAD + 1,)),
        ],
        compiler_params=params(18),
        cost_estimate=cost(4 * rows * depth * columns, 4 * depth * columns),
        name="keyval",
    )(where, in_hbm(text), own, sibling, gain, in_hbm(weight), bias)
    return outs[0], outs[1:]


def query_kernel(rows_all, weight, bias, text_out, image_out, buf, sem):
    width = buf.shape[2]
    slots = AHEAD + 1
    texts = text_out.shape[0]

    def copy(i):
        return pltpu.make_async_copy(weight.at[:, tile(i, width)], buf.at[i % slots], sem.at[i % slots])

    def body(i):
        here = tile(i, width)
        out = (dot(rows_all[...], buf[i % slots]) + bias[:, here]).astype(BF16)
        text_out[:, here] = out[:texts]
        image_out[:, here] = out[texts:]

    begin(copy)
    stream(weight.shape[1] // width, copy, body)


def query_rows(rows_all, texts, weight, bias):
    depth = rows_all.shape[1]
    images = rows_all.shape[0] - texts
    columns = weight.shape[1]
    return pl.pallas_call(
        query_kernel,
        out_shape=[jax.ShapeDtypeStruct((texts, columns), BF16), jax.ShapeDtypeStruct((images, columns), BF16)],
        in_specs=[VMEM, HBM, VMEM],
        out_specs=[VMEM, VMEM],
        scratch_shapes=[pltpu.VMEM((AHEAD + 1, depth, 256), BF16), pltpu.SemaphoreType.DMA((AHEAD + 1,))],
        compiler_params=params(24),
        cost_estimate=cost(2 * (texts + images) * depth * columns, 2 * depth * columns),
        name="query",
    )(in_vmem(rows_all), in_hbm(weight), bias[None, :])


def join_parts(mp, parts, first_row, rows):
    count = len(parts)
    width = parts[0].shape[1]
    heads = KV_HEADS // count
    coords = HEAD_DIM // count
    full = 2 * heads * HEAD_DIM
    row = lax.broadcasted_iota(jnp.int32, (width, full), 0)
    column = lax.broadcasted_iota(jnp.int32, (width, full), 1)
    total = jnp.zeros((rows, full), F32)
    for x in range(count):
        coordinate = (mp ^ x) * coords + row % coords
        place = (column == (row // coords) * HEAD_DIM + coordinate).astype(BF16)
        total = total + dot(parts[x][pl.ds(first_row, rows), :], place)
    return total.astype(BF16)


def slots_kernel(where, owner_rows, owner_columns, queries, *rest):
    parts, out = rest[:-1], rest[-1]
    owners = owner_rows.shape[0]
    rows, columns = queries.shape
    slots = out.shape[0]
    mp, me = where[0], where[1]
    down = owner_columns[pl.ds(pl.multiple_of(me * rows, rows), rows), :]
    across = owner_rows[pl.ds(me, 1), :]
    earlier = lax.broadcasted_iota(jnp.int32, (rows, rows), 0) < lax.broadcasted_iota(jnp.int32, (rows, rows), 1)
    rank = jnp.sum(jnp.where((down == across) & earlier, 1, 0), axis=0, keepdims=True)
    slot = across * (slots // owners) + rank
    select = (lax.broadcasted_iota(jnp.int32, (slots, rows), 0) == slot).astype(F32).astype(BF16)
    out[:, pl.ds(0, columns)] = dot(select, queries[...]).astype(BF16)
    keyval = join_parts(mp, parts, parts[0].shape[0] - rows, rows)
    out[:, pl.ds(columns, out.shape[1] - columns)] = dot(select, keyval).astype(BF16)


def slots_of(where, owner_rows, owner_columns, queries, parts, capacity):
    slots = owner_rows.shape[0] * capacity
    width = queries.shape[1] + 2 * (KV_HEADS // len(parts)) * HEAD_DIM
    return pl.pallas_call(
        slots_kernel,
        out_shape=jax.ShapeDtypeStruct((slots, width), BF16),
        in_specs=[SMEM] + [VMEM] * (3 + len(parts)),
        out_specs=VMEM,
        compiler_params=params(12),
        name="slots",
    )(where, owner_rows, owner_columns, queries, *parts)


def attend(blocks, first, doc_column, windows, q_all, kv_all, out):
    q_first, k_first, out_first = first
    heads = q_all.shape[1] // HEAD_DIM
    groups = kv_all.shape[1] // (2 * HEAD_DIM)
    shared = heads // groups
    block = DOC_MAX
    scale = 1.0 / math.sqrt(HEAD_DIM)
    row = lax.broadcasted_iota(jnp.int32, (block, 2 * block), 0)
    column = lax.broadcasted_iota(jnp.int32, (block, 2 * block), 1)

    @pl.loop(blocks[0], blocks[1])
    def _(b):
        q0 = pl.multiple_of(b * block, block)
        k0 = pl.multiple_of(jnp.maximum(b - 1, 0) * block, block)
        allowed = (doc_column[pl.ds(q0, block), :] == windows[pl.ds(b, 1), :]) & (k0 + column <= q0 + row)
        penalty = jnp.concatenate([jnp.where(allowed, 0.0, -1e30)] * shared, axis=0)

        @pl.loop(0, groups)
        def _(g):
            keys = kv_all[pl.ds(k0 - k_first, 2 * block), tile(g, HEAD_DIM)]
            values = kv_all[pl.ds(k0 - k_first, 2 * block), tile(groups + g, HEAD_DIM)]
            columns = [tile(g * shared + h, HEAD_DIM) for h in range(shared)]
            q = jnp.concatenate([q_all[pl.ds(q0 - q_first, block), c] for c in columns], axis=0)
            scores = lax.dot_general(q, keys, (((1,), (1,)), ((), ())), preferred_element_type=F32) * scale
            scores = jnp.where(penalty < 0.0, penalty, scores)
            weights = jnp.exp(scores - jnp.max(scores, axis=-1, keepdims=True))
            probs = (weights / jnp.sum(weights, axis=-1, keepdims=True)).astype(BF16)
            result = dot(probs, values).astype(BF16)
            for h, c in enumerate(columns):
                out[pl.ds(q0 - out_first, block), c] = result[h * block : (h + 1) * block]


def late_kernel(early, where, doc_column, windows, queries, *rest):
    parts, out, kv_all = rest[:-2], rest[-2], rest[-1]
    seq = queries.shape[0]
    first = early - DOC_MAX
    kv_all[...] = join_parts(where[0], parts, first, seq - first)
    attend((early // DOC_MAX, seq // DOC_MAX), (0, first, 0), doc_column, windows, queries, kv_all, out)


def early_kernel(early, where, owner_rows, doc_column, windows, queries, arrived, *rest):
    parts = rest[:-6]
    _, out, q_all, kv_all, result, sem = rest[-6:]
    mp, me = where[0], where[1]
    columns = queries.shape[1]
    slots = arrived.shape[0]
    owners = owner_rows.shape[0]
    capacity = slots // owners
    incoming = jnp.sum(jnp.where(owner_rows[...] == me, 1, 0), axis=1, keepdims=True)
    source = lax.broadcasted_iota(jnp.int32, (owners, slots), 0)
    slot = lax.broadcasted_iota(jnp.int32, (owners, slots), 1)
    offset = jnp.sum(jnp.where(source < slot // capacity, incoming, 0), axis=0, keepdims=True)
    here = jnp.sum(jnp.where(source == slot // capacity, incoming, 0), axis=0, keepdims=True)
    index = lax.broadcasted_iota(jnp.int32, (1, slots), 1) % capacity
    target = jnp.where(index < here, offset + index, -1)
    position = lax.broadcasted_iota(jnp.int32, (slots, slots), 0)
    place = (position == target).astype(F32).astype(BF16)
    placed = dot(place, arrived[...]).astype(BF16)
    is_image = lax.broadcasted_iota(jnp.int32, (slots, 1), 0) < jnp.sum(incoming, axis=0, keepdims=True)

    keyval = join_parts(mp, parts, 0, early)
    kv_all[...] = keyval
    kv_all[pl.ds(0, slots), :] = jnp.where(is_image, placed[:, columns:], keyval[:slots])
    q_all[...] = queries[pl.ds(0, early), :]
    q_all[pl.ds(0, slots), :] = jnp.where(is_image, placed[:, :columns], queries[pl.ds(0, slots), :])
    attend((0, early // DOC_MAX), (0, 0, 0), doc_column, windows, q_all, kv_all, result)
    copy = pltpu.make_async_copy(result, out.at[pl.ds(0, early)], sem)
    copy.start()
    copy.wait()


def attention(where, owner_rows, documents, queries, parts, capacity):
    seq, columns = queries.shape
    width = 2 * (KV_HEADS // len(parts)) * HEAD_DIM
    slots = owner_rows.shape[0] * capacity
    early = min(seq, -(-slots // DOC_MAX) * DOC_MAX + DOC_MAX)
    windows = jnp.stack([documents[max(0, b - 1) * DOC_MAX :][: 2 * DOC_MAX] for b in range(seq // DOC_MAX)])
    docs = (documents[:, None], windows)
    shape = jax.ShapeDtypeStruct((seq, columns), BF16)

    def late(queries):
        return pl.pallas_call(
            functools.partial(late_kernel, early),
            out_shape=shape,
            in_specs=[SMEM] + [VMEM] * (3 + len(parts)),
            out_specs=VMEM,
            scratch_shapes=[pltpu.VMEM((seq - early + DOC_MAX, width), BF16)],
            compiler_params=params(16),
            cost_estimate=cost(4 * (seq - early) * columns * 2 * DOC_MAX, 4 * seq * columns),
            name="attention_late",
        )(where, *docs, queries, *parts)

    def final(arrived, before):
        return pl.pallas_call(
            functools.partial(early_kernel, early),
            out_shape=shape,
            in_specs=[SMEM] + [VMEM] * (5 + len(parts)) + [ANY],
            out_specs=ANY,
            scratch_shapes=[
                pltpu.VMEM((early, columns), BF16),
                pltpu.VMEM((early, width), BF16),
                pltpu.VMEM((early, columns), BF16),
                pltpu.SemaphoreType.DMA,
            ],
            input_output_aliases={6 + len(parts): 0},
            compiler_params=params(16),
            cost_estimate=cost(4 * early * columns * 2 * DOC_MAX, 4 * seq * columns),
            name="attention_early",
        )(where, owner_rows, *docs, queries, arrived, *parts, before)

    return late, final


def after(x, *others):
    return lax.optimization_barrier((x, *others))[0]


def exchange(x, count, bit):
    return lax.ppermute(x, "mp", [(i, i ^ bit) for i in range(count)])


def per_device(
    patch_rows,
    ln_gain,
    ln_bias,
    merge_up,
    merge_up_bias,
    merge_down,
    merge_down_bias,
    row_owner,
    text_embed,
    doc_ids,
    rms_gain,
    w_query,
    query_bias,
    w_keyval,
    keyval_bias,
):
    owners = lax.axis_size(("group", "dp"))
    count = lax.axis_size("mp")
    mp_index = lax.axis_index("mp")
    where = jnp.stack([mp_index, lax.axis_index(("group", "dp"))]).astype(jnp.int32)
    rows = row_owner.shape[0] // owners
    capacity = max(2, 2 * rows // owners)
    gain = rms_gain[None, :]
    owner_rows = row_owner.reshape(owners, rows)

    send, keep = merger(
        where, patch_rows[0], ln_gain, ln_bias, merge_up, merge_up_bias, merge_down, merge_down_bias, rows
    )
    text = text_embed[0]
    own = (keep.astype(F32) + exchange(send, count, 1).astype(F32)).astype(BF16)
    weight = jnp.transpose(after(w_keyval, own), (1, 0, 2))
    bit = 2
    while bit < count:
        other = after(exchange(own, count, bit), weight)
        own = (own.astype(F32) + other.astype(F32)).astype(BF16)
        bit *= 2
    sibling = exchange(own, count, 1)

    rows_all, parts = keyval_parts(where, text, own, sibling, gain, weight, keyval_bias, count)
    parts = [parts[0]] + [exchange(parts[x], count, x) for x in range(1, count)]
    text_queries, image_queries = query_rows(rows_all, text.shape[0], w_query, query_bias)
    outgoing = slots_of(where, owner_rows, row_owner, image_queries, parts, capacity)
    arrived = lax.all_to_all(
        outgoing.reshape(owners, capacity, -1), ("group", "dp"), split_axis=0, concat_axis=0, tiled=True
    ).reshape(owners * capacity, -1)
    late, final = attention(where, owner_rows, doc_ids[0], text_queries, parts, capacity)
    before = late(after(text_queries, outgoing))
    return final(after(arrived, before), before)[None]


def general(
    patch_rows,
    ln_gain,
    ln_bias,
    merge_up,
    merge_up_bias,
    merge_down,
    merge_down_bias,
    row_owner,
    text_embed,
    doc_ids,
    rms_gain,
    w_query,
    query_bias,
    w_keyval,
    keyval_bias,
):
    owners = lax.axis_size(("group", "dp"))
    own_index = lax.axis_index(("group", "dp"))
    mp_index = lax.axis_index("mp")
    pixels = patch_rows[0].astype(jnp.float32)
    center = pixels - jnp.mean(pixels, axis=-1, keepdims=True)
    spread = jnp.mean(center * center, axis=-1, keepdims=True)
    normed_patch = (center * lax.rsqrt(spread + 1e-06) * ln_gain + ln_bias).astype(jnp.bfloat16)
    merged = normed_patch.reshape(-1, 4 * pixels.shape[1])
    merged_rows = merged.shape[0]
    hidden = jax.nn.gelu(
        jnp.dot(merged, merge_up, preferred_element_type=jnp.float32) + merge_up_bias,
        approximate=False,
    ).astype(jnp.bfloat16)
    partial_sum = jnp.dot(hidden, merge_down, preferred_element_type=jnp.float32)
    vision = (
        lax.psum_scatter(partial_sum, "mp", scatter_dimension=1, tiled=True) + merge_down_bias
    ).astype(jnp.bfloat16)
    col_width = vision.shape[1]
    capacity = max(2, 2 * merged_rows // owners)
    owner_all = row_owner[:, 0]
    owner_ids = jnp.arange(owners, dtype=jnp.int32)
    onehot = (owner_all[:, None] == owner_ids[None, :]).astype(jnp.int32)
    per_source = jnp.sum(onehot.reshape(owners, merged_rows, owners), axis=1)
    my_block = lax.dynamic_slice_in_dim(onehot, own_index * merged_rows, merged_rows, 0)
    block_rank = jnp.sum((jnp.cumsum(my_block, axis=0) - my_block) * my_block, axis=1)
    my_owner = jnp.sum(my_block * owner_ids[None, :], axis=1)
    slot_id = my_owner * capacity + block_rank
    all_slots = jnp.arange(owners * capacity, dtype=jnp.int32)
    select = (slot_id[:, None] == all_slots[None, :]).astype(jnp.bfloat16)
    outgoing = jnp.einsum("ms,mc->sc", select, vision, preferred_element_type=jnp.float32).astype(
        jnp.bfloat16
    )
    arrived = lax.all_to_all(
        outgoing.reshape(owners, capacity, col_width),
        ("group", "dp"),
        split_axis=0,
        concat_axis=0,
        tiled=True,
    )
    arrived = arrived.reshape(owners * capacity, col_width)
    incoming = lax.dynamic_slice_in_dim(per_source, own_index, 1, 1)[:, 0]
    offsets = jnp.cumsum(incoming) - incoming
    total = jnp.sum(incoming)
    slot_rank = jnp.arange(capacity, dtype=jnp.int32)
    target = jnp.where(
        slot_rank[None, :] < incoming[:, None], offsets[:, None] + slot_rank[None, :], -1
    ).reshape(-1)
    text_rows = text_embed[0]
    seq_len = text_rows.shape[0]
    positions = jnp.arange(seq_len, dtype=jnp.int32)
    source_slot = jnp.sum(
        jnp.where(target[:, None] == positions[None, :], all_slots[:, None], 0), axis=0
    )
    is_image = (positions < total)[:, None]
    image_full = lax.all_gather(arrived, "mp", axis=1, tiled=True)
    sequence = jnp.where(is_image, jnp.take(image_full, source_slot, axis=0), text_rows)
    seq_f = sequence.astype(jnp.float32)
    normed_seq = (
        seq_f * lax.rsqrt(jnp.mean(seq_f * seq_f, axis=-1, keepdims=True) + 1e-06) * rms_gain
    ).astype(jnp.bfloat16)
    queries = (
        jnp.dot(normed_seq, w_query, preferred_element_type=jnp.float32) + query_bias
    ).astype(jnp.bfloat16)
    keyval_local = (
        jnp.einsum("sd,dtc->stc", normed_seq, w_keyval, preferred_element_type=jnp.float32)
        + keyval_bias
    ).astype(jnp.bfloat16)
    keyval_full = lax.all_gather(keyval_local, "mp", axis=2, tiled=True)
    keyval_heads = jnp.transpose(keyval_full.reshape(seq_len, 2, HEAD_DIM, KV_HEADS), (0, 1, 3, 2))
    local_heads = queries.shape[1] // HEAD_DIM
    group_size = HEADS // KV_HEADS
    kv_index = (mp_index * local_heads + jnp.arange(local_heads, dtype=jnp.int32)) // group_size
    keys = jnp.take(keyval_heads[:, 0], kv_index, axis=1)
    values = jnp.take(keyval_heads[:, 1], kv_index, axis=1)
    query_heads = queries.reshape(seq_len, local_heads, HEAD_DIM)
    scores = jnp.einsum(
        "qhd,khd->hqk", query_heads, keys, preferred_element_type=jnp.float32
    ) / math.sqrt(HEAD_DIM)
    documents = doc_ids[0]
    allowed = (documents[:, None] == documents[None, :]) & (
        positions[None, :] <= positions[:, None]
    )
    scores = jnp.where(allowed[None], scores, jnp.float32(-1e30))
    highest = jnp.max(scores, axis=-1, keepdims=True)
    weights = jnp.exp(scores - highest)
    probs = (weights / jnp.sum(weights, axis=-1, keepdims=True)).astype(jnp.bfloat16)
    output = jnp.einsum("hqk,khd->qhd", probs, values, preferred_element_type=jnp.float32)
    return output.astype(jnp.bfloat16).reshape(1, seq_len, local_heads * HEAD_DIM)


def solution(mesh):
    in_specs = (
        P(("group", "dp"), None, None),
        P(),
        P(),
        P(None, "mp"),
        P("mp"),
        P("mp", None),
        P("mp"),
        P(),
        P(("group", "dp"), None, None),
        P(("group", "dp"), None),
        P(),
        P(None, "mp"),
        P("mp"),
        P(None, None, "mp"),
        P(None, "mp"),
    )
    out_specs = P(("group", "dp"), None, "mp")
    count = mesh.shape["mp"]
    narrow = count < 2 or count > KV_HEADS or count & (count - 1)
    body = general if narrow else per_device
    return jax.shard_map(body, mesh=mesh, in_specs=in_specs, out_specs=out_specs, check_vma=False)
```

time: 105 us -> 77.7 us (0.74)
  waiting for transfers between devices: 19.5 us -> 8.84 us
  Pallas kernels: 57.2 us -> 47.6 us
  local copies, waits for them, and re-layouts: 14.8 us -> 8.64 us
    unnamed x23 -> x12, local copies, waits for them, and re-layouts: 12.4 us -> 0.68 us
    pallas_call x1, Pallas kernels: 25.3 us -> 14 us  [query_rows(): pl.pallas_call(query_kernel, out_shape=[jax.ShapeDtypeStruct((texts, colu...]
    optimization_barrier x0 -> x1, local copies, waits for them, and re-layouts: none -> 7.68 us  [after(): return lax.optimization_barrier((x, *others))[0]]
    ppermute x6, waiting for transfers between devices: 7.78 us -> 1.28 us  [exchange(): return lax.ppermute(x, 'mp', [(i, i ^ bit) for i in range(count)])]
    pallas_call x3, Pallas kernels: 14.1 us -> 18.4 us  [the longest x1 10 us: keyval_parts(): pl.pallas_call(keyval_kernel, out_shape=[pltpu.VMEM((rows, depth), BF16)]...]
    all_to_all x1, waiting for transfers between devices: 11.7 us -> 7.55 us  [per_device(): lax.all_to_all(outgoing.reshape(owners, capacity, -1), ('group', 'dp'), s...]
    pallas_call x1, Pallas kernels: 16 us -> 13.5 us  [merger(): pl.pallas_call(merger_kernel, out_shape=[jax.ShapeDtypeStruct((rows, colu...]
    broadcast_in_dim x3 -> x0, local copies, waits for them, and re-layouts: 2.1 us -> none  [the longest x1 0.7 us: per_device(): ln_bias[None, :]]
  transfers between devices with their start and end apart: 7 -> 7, of which waited for: 3 -> 3; matrix products, arithmetic and copies ran while one was open for 9% -> 12% of each run, Pallas kernels for 27% -> 23%
where the time goes in v2:
time: 77.7 us; the launch traced here: 77.4 us
  Pallas kernels  47.6 us (61%)
  starting transfers between devices  11.3 us (15%)
  waiting for transfers between devices  8.84 us (11%)
  local copies, waits for them, and re-layouts  8.64 us (11%)
  other arithmetic  0.88 us (1%)
    pallas_call x1, Pallas kernels, query_rows(): pl.pallas_call(query_kernel, out_shape=[jax.ShapeDtypeStruct((texts, colu...  14 us
    pallas_call x1, Pallas kernels, merger(): pl.pallas_call(merger_kernel, out_shape=[jax.ShapeDtypeStruct((rows, colu...  13.5 us
    pallas_call x1, Pallas kernels, keyval_parts(): pl.pallas_call(keyval_kernel, out_shape=[pltpu.VMEM((rows, depth), BF16)]...  10 us
    optimization_barrier x1, local copies, waits for them, and re-layouts, after(): return lax.optimization_barrier((x, *others))[0]  7.68 us
    all_to_all x1, waiting for transfers between devices, per_device(): lax.all_to_all(outgoing.reshape(owners, capacity, -1), ('group', 'dp'), s...  7.55 us
    all_to_all x1, starting transfers between devices, per_device(): lax.all_to_all(outgoing.reshape(owners, capacity, -1), ('group', 'dp'), s...  5.81 us
    ppermute x6, starting transfers between devices, exchange(): return lax.ppermute(x, 'mp', [(i, i ^ bit) for i in range(count)])  5.47 us
    pallas_call x1, Pallas kernels, late(): pl.pallas_call(functools.partial(late_kernel, early), out_shape=shape, in...  4.2 us
  transfers between devices with their start and end apart: 7, of which 3 were waited for; matrix products, arithmetic and copies ran while one was open for 12% of the time, Pallas kernels for 23%

profile of v2, /device:TPU:0, one launch (start us, length us, event | category | flops | bytes accessed | tf_op | source)
XLA Modules:
  0.0 77.4 jit_solution(2755751660980290971)
XLA Ops:
  0.0 0.1 pad_add_fusion.1.where
  0.1 13.5 %merger.1 = (bf16[32,4096]{1,0:T(8,128)(2,1)S(1)}, bf16[32,4096]{1,0:T(8,128)(2,1)S(1)}) custom-call(s32[2]{0:T(128)S(1)} %pad_add_fusion.1.where, bf16[128,1280]{1,0:T(8,128)(2,1)} %bitcast.19, f32[1280]{0:T(1024)} %gain_in.1, f32[1280]{0:T(1024)} %bias_in.1, bf16[5120,1280]{1,0:T(8,128)(2,1)} %up.1, f32[1280]{0:T(1024)} %up_bias_in.1, ...), custom_call_target="tpu_custom_call" | custom-call | flops 1090519040 | bytes 34078720 | tf_op jit(solution)/shard_map/merger/pallas_call | solution.py:153
  13.6 0.5 collective-permute-start
  14.1 1.2 %collective-permute-done = bf16[32,4096]{1,0:T(8,128)(2,1)S(1)} collective-permute-done((bf16[32,4096]{1,0:T(8,128)(2,1)S(1)}, bf16[32,4096]{1,0:T(8,128)(2,1)S(1)}, u32[]{:S(2)}, u32[]{:S(2)}) %collective-permute-start) | collective-permute-done | bytes 262176 | tf_op jit(solution)/shard_map/ppermute | solution.py:453
  15.3 0.1 add_convert_fusion.1
  15.3 0.0 copy-start.4
  15.3 0.0 copy-start
  15.4 0.0 copy-start.2
  15.4 3.0 %collective-permute-start.1 = (bf16[32,4096]{1,0:T(8,128)(2,1)S(1)}, bf16[32,4096]{1,0:T(8,128)(2,1)S(1)}, u32[]{:S(2)}, u32[]{:S(2)}) collective-permute-start(bf16[32,4096]{1,0:T(8,128)(2,1)S(1)} %add_convert_fusion.1), channel_id=1, source_target_pairs={{0,2},{1,3},{2,0},{3,1},{4,6},{5,7},{6,4},{7,5},{8,10},{9,11},{10,... | collective-permute-start | bytes 786440 | tf_op jit(solution)/shard_map/ppermute | solution.py:453
  18.3 7.7 %copy.24 = bf16[8192,2,256]{2,0,1:T(8,128)(2,1)} copy(bf16[8192,2,256]{2,1,0:T(2,128)(2,1)} %param.28) | data formatting | bytes 16777216 | tf_op jit(solution)/shard_map/optimization_barrier | solution.py:449
  26.0 0.0 collective-permute-done.1
  26.0 0.1 add_convert_fusion.own
  26.1 0.1 collective-permute-start.2
  26.2 0.1 copy.20.owner_columns
  26.3 0.5 broadcast.3
  26.8 0.7 reduce.3
  27.5 0.1 reshape.16.owner_rows
  27.6 0.1 collective-permute-done.2.sibling
  27.7 10.0 %keyval.1 = (bf16[288,8192]{1,0:T(8,128)(2,1)S(1)}, bf16[288,128]{1,0:T(8,128)(2,1)S(1)}, bf16[288,128]{1,0:T(8,128)(2,1)S(1)}, bf16[288,128]{1,0:T(8,128)(2,1)S(1)}, bf16[288,128]{1,0:T(8,128)(2,1)S(1)}) custom-call(s32[2]{0:T(128)S(1)} %pad_add_fusion.1.where, bf16[256,8192]{1,0:T(8,128)(2,1)} %bitcast.18, bf16[32,4096]{1,0:T(8,128)(2,1)S(1)} %add_convert_fusion.own, ...), custom_call_target="tpu_custom_call" | custom-call | flops 2415919104 | bytes 8388608 | tf_op jit(solution)/shard_map/keyval/pallas_call | solution.py:236
  37.7 0.4 collective-permute-start.3
  38.1 0.7 collective-permute-start.4
  38.8 0.8 %collective-permute-start.5 = (bf16[288,128]{1,0:T(8,128)(2,1)S(1)}, bf16[288,128]{1,0:T(8,128)(2,1)S(1)}, u32[]{:S(2)}, u32[]{:S(2)}) collective-permute-start(bf16[288,128]{1,0:T(8,128)(2,1)S(1)} %get-tuple-element.28), channel_id=1, source_target_pairs={{0,3},{1,2},{2,1},{3,0},{4,7},{5,6},{6,5},{7,4},{8,11},{9,10},{10,... | collective-permute-start | bytes 221192 | tf_op jit(solution)/shard_map/ppermute | solution.py:453
  39.6 14.0 %query.1 = (bf16[256,2048]{1,0:T(8,128)(2,1)S(1)}, bf16[32,2048]{1,0:T(8,128)(2,1)S(1)}) custom-call(bf16[288,8192]{1,0:T(8,128)(2,1)S(1)} %get-tuple-element.22.rows_all, bf16[8192,2048]{1,0:T(8,128)(2,1)} %weight.1, f32[1,2048]{1,0:T(1,128)S(1)} %bitcast.16), custom_call_target="tpu_custom_call" | custom-call | flops 9663676416 | bytes 33554432 | tf_op jit(solution)/shard_map/query/pallas_call | solution.py:277
  53.6 0.0 collective-permute-done.3.rest_1_
  53.6 0.0 collective-permute-done.5.rest_3_
  53.6 1.8 %slots.1 = bf16[64,2560]{1,0:T(8,128)(2,1)} custom-call(s32[2]{0:T(128)S(1)} %pad_add_fusion.1.where, s32[8,32]{1,0:T(8,128)S(1)} %reshape.16.owner_rows, s32[256,1]{1,0:T(8,128)S(1)} %copy.20.owner_columns, bf16[32,2048]{1,0:T(8,128)(2,1)S(1)} %get-tuple-element.24.queries, bf16[288,128]{1,0:T(8,128)(2,1)S(1)} %get-tuple-element.25.rest_0_, ...), custom_call_target="tpu_custom_call" | custom-call | tf_op jit(solution)/shard_map/slots/pallas_call | solution.py:325
  55.4 5.8 %all-to-all-start = ((bf16[8,8,2560]{2,1,0:T(8,128)(2,1)}), bf16[8,8,2560]{2,1,0:T(8,128)(2,1)S(1)}, u32[]{:S(2)}, u32[]{:S(2)}) async-start(bf16[8,8,2560]{2,1,0:T(8,128)(2,1)} %bitcast.8), calls=%async_computation | async-start | bytes 655360 | tf_op jit(solution)/shard_map/all_to_all | solution.py:499
  61.2 0.1 copy.22.doc_column
  61.4 0.1 fusion
  61.5 4.2 %attention_late.1.rest_4_ = bf16[256,2048]{1,0:T(8,128)(2,1)} custom-call(s32[2]{0:T(128)S(1)} %pad_add_fusion.1.where, s32[256,1]{1,0:T(8,128)S(1)} %copy.22.doc_column, s32[4,128]{1,0:T(4,128)S(1)} %pad_add_fusion.windows, bf16[256,2048]{1,0:T(8,128)(2,1)S(1)} %get-tuple-element.29.queries, bf16[288,128]{1,0:T(8,128)(2,1)S(1)} %get-tuple-element.25.rest_0_, ...), custom_call_target="tpu_custom_call" | custom-call | flops 134217728 | bytes 2097152 | tf_op jit(solution)/shard_map/attention_late/pallas_call | solution.py:416
  65.7 7.6 %all-to-all-done = bf16[8,8,2560]{2,1,0:T(8,128)(2,1)S(1)} async-done(((bf16[8,8,2560]{2,1,0:T(8,128)(2,1)}), bf16[8,8,2560]{2,1,0:T(8,128)(2,1)S(1)}, u32[]{:S(2)}, u32[]{:S(2)}) %all-to-all-start) | async-done | bytes 327712 | tf_op jit(solution)/shard_map/all_to_all | solution.py:499
  73.2 4.2 %attention_early.1 = bf16[256,2048]{1,0:T(8,128)(2,1)} custom-call(s32[2]{0:T(128)S(1)} %pad_add_fusion.1.where, s32[8,32]{1,0:T(8,128)S(1)} %reshape.16.owner_rows, s32[256,1]{1,0:T(8,128)S(1)} %copy.22.doc_column, s32[4,128]{1,0:T(4,128)S(1)} %pad_add_fusion.windows, ...), custom_call_target="tpu_custom_call", output_to_operand_aliasing={{}: (10, {})} | custom-call | flops 134217728 | bytes 2097152 | tf_op jit(solution)/shard_map/attention_early/pallas_call | solution.py:428
  (9 shorter events, 0.0 us)
Async XLA Ops:
  13.6 1.7 %collective-permute-start = (bf16[32,4096]{1,0:T(8,128)(2,1)S(1)}, bf16[32,4096]{1,0:T(8,128)(2,1)S(1)}, u32[]{:S(2)}, u32[]{:S(2)}) collective-permute-start(bf16[32,4096]{1,0:T(8,128)(2,1)S(1)} %get-tuple-element.19), channel_id=1, source_target_pairs={{0,1},{1,0},{2,3},{3,2},{4,5},{5,4},{6,7},{7,6},{8,9},{9,8},{10,11... | collective-permute-start | bytes 786440 | tf_op jit(solution)/shard_map/ppermute | solution.py:453
  15.3 10.8 %copy-start.4 = (s32[256,1]{0,1:T(1,128)S(1)}, s32[256,1]{0,1:T(1,128)}, u32[]{:S(2)}) copy-start(s32[256,1]{0,1:T(1,128)} %param.22) | copy-start | bytes 3076
  15.3 12.3 %copy-start = (f32[8192]{0:T(1024)S(1)}, f32[8192]{0:T(1024)}, u32[]{:S(2)}) copy-start(f32[8192]{0:T(1024)} %param.25) | copy-start | bytes 98308
  15.4 12.3 %copy-start.2 = (f32[2,256]{1,0:T(2,128)S(1)}, f32[2,256]{1,0:T(2,128)}, u32[]{:S(2)}) copy-start(f32[2,256]{1,0:T(2,128)} %bias.1) | copy-start | bytes 6148
  15.4 10.6 %collective-permute-start.1 = (bf16[32,4096]{1,0:T(8,128)(2,1)S(1)}, bf16[32,4096]{1,0:T(8,128)(2,1)S(1)}, u32[]{:S(2)}, u32[]{:S(2)}) collective-permute-start(bf16[32,4096]{1,0:T(8,128)(2,1)S(1)} %add_convert_fusion.1), channel_id=1, source_target_pairs={{0,2},{1,3},{2,0},{3,1},{4,6},{5,7},{6,4},{7,5},{8,10},{9,11},{10,... | collective-permute-start | bytes 786440 | tf_op jit(solution)/shard_map/ppermute | solution.py:453
  26.0 13.6 %copy-start.1 = (f32[2048]{0:T(1024)S(1)}, f32[2048]{0:T(1024)}, u32[]{:S(2)}) copy-start(f32[2048]{0:T(1024)} %param.27) | copy-start | bytes 24580
  26.1 1.6 %collective-permute-start.2 = (bf16[32,4096]{1,0:T(8,128)(2,1)S(1)}, bf16[32,4096]{1,0:T(8,128)(2,1)S(1)}, u32[]{:S(2)}, u32[]{:S(2)}) collective-permute-start(bf16[32,4096]{1,0:T(8,128)(2,1)S(1)} %add_convert_fusion.own), channel_id=1, source_target_pairs={{0,1},{1,0},{2,3},{3,2},{4,5},{5,4},{6,7},{7,6},{8,9},{9,8},{10,11... | collective-permute-start | bytes 786440 | tf_op jit(solution)/shard_map/ppermute | solution.py:453
  37.7 15.9 %collective-permute-start.3 = (bf16[288,128]{1,0:T(8,128)(2,1)S(1)}, bf16[288,128]{1,0:T(8,128)(2,1)S(1)}, u32[]{:S(2)}, u32[]{:S(2)}) collective-permute-start(bf16[288,128]{1,0:T(8,128)(2,1)S(1)} %get-tuple-element.26), channel_id=1, source_target_pairs={{0,1},{1,0},{2,3},{3,2},{4,5},{5,4},{6,7},{7,6},{8,9},{9,8},{10,11... | collective-permute-start | bytes 221192 | tf_op jit(solution)/shard_map/ppermute | solution.py:453
  38.1 15.5 %collective-permute-start.4 = (bf16[288,128]{1,0:T(8,128)(2,1)S(1)}, bf16[288,128]{1,0:T(8,128)(2,1)S(1)}, u32[]{:S(2)}, u32[]{:S(2)}) collective-permute-start(bf16[288,128]{1,0:T(8,128)(2,1)S(1)} %get-tuple-element.27), channel_id=1, source_target_pairs={{0,2},{1,3},{2,0},{3,1},{4,6},{5,7},{6,4},{7,5},{8,10},{9,11},{10,... | collective-permute-start | bytes 221192 | tf_op jit(solution)/shard_map/ppermute | solution.py:453
  38.8 14.8 %collective-permute-start.5 = (bf16[288,128]{1,0:T(8,128)(2,1)S(1)}, bf16[288,128]{1,0:T(8,128)(2,1)S(1)}, u32[]{:S(2)}, u32[]{:S(2)}) collective-permute-start(bf16[288,128]{1,0:T(8,128)(2,1)S(1)} %get-tuple-element.28), channel_id=1, source_target_pairs={{0,3},{1,2},{2,1},{3,0},{4,7},{5,6},{6,5},{7,4},{8,11},{9,10},{10,... | collective-permute-start | bytes 221192 | tf_op jit(solution)/shard_map/ppermute | solution.py:453
  39.6 21.6 %copy-start.3 = (s32[1,256]{1,0:T(1,128)S(1)}, s32[1,256]{1,0:T(1,128)}, u32[]{:S(2)}) copy-start(s32[1,256]{1,0:T(1,128)} %param.24) | copy-start | bytes 3076
  55.4 17.8 %all-to-all-start = ((bf16[8,8,2560]{2,1,0:T(8,128)(2,1)}), bf16[8,8,2560]{2,1,0:T(8,128)(2,1)S(1)}, u32[]{:S(2)}, u32[]{:S(2)}) async-start(bf16[8,8,2560]{2,1,0:T(8,128)(2,1)} %bitcast.8), calls=%async_computation | async-start | bytes 655360 | tf_op jit(solution)/shard_map/all_to_all | solution.py:499

commit v3 on v2

--- a/solution.py
+++ b/solution.py
@@ -20,6 +20,7 @@
 ANY = pl.BlockSpec(memory_space=pl.ANY)
 HBM = pl.BlockSpec(memory_space=pltpu.HBM)
 AHEAD = 3
+DEEP = 5
 MIB = 1 << 20
 
 
@@ -47,26 +48,26 @@
     return lax.rsqrt(jnp.sum(x * x, axis=-1, keepdims=True) / width + 1e-06)
 
 
-def stream(count, copy, body, then=None):
+def stream(count, copy, body, ahead=AHEAD, then=None):
     @pl.loop(0, count)
     def _(i):
         copy(i).wait()
 
-        @pl.when(i + AHEAD < count)
+        @pl.when(i + ahead < count)
         def _():
-            copy(i + AHEAD).start()
+            copy(i + ahead).start()
 
         if then is not None:
 
-            @pl.when(i + AHEAD >= count)
+            @pl.when(i + ahead >= count)
             def _():
-                then(i + AHEAD - count).start()
+                then(i + ahead - count).start()
 
         body(i)
 
 
-def begin(copy):
-    for i in range(AHEAD):
+def begin(copy, ahead=AHEAD):
+    for i in range(ahead):
         copy(i).start()
 
 
@@ -75,10 +76,11 @@
 
 
 def merger_kernel(
-    where, patch_in, gain_in, bias_in, up, up_bias_in, down, down_bias_in, send, keep,
-    patch, gain, bias, up_bias, down_bias, bias_row, normed, merged, total, up_buf, down_buf, small_sem, up_sem, down_sem,
+    where, patch_in, gain_in, bias_in, up, up_bias_in, down, down_bias_in, text, rms_gain_in, send, keep, text_out,
+    patch, gain, bias, up_bias, down_bias, rms_gain, bias_row, normed, merged, total, up_buf, down_buf, text_buf,
+    small_sem, up_sem, down_sem, text_sem,
 ):
-    slots = AHEAD + 1
+    slots = DEEP + 1
     step = up_buf.shape[1]
     width = down_buf.shape[2]
     half = send.shape[1]
@@ -86,6 +88,7 @@
     mp = where[0]
     mine = mp % 2
     pairs = [(patch_in, patch), (gain_in, gain), (bias_in, bias), (up_bias_in, up_bias), (down_bias_in, down_bias)]
+    pairs.append((rms_gain_in, rms_gain))
     small = [pltpu.make_async_copy(x, y, small_sem.at[i]) for i, (x, y) in enumerate(pairs)]
     for copy in small:
         copy.start()
@@ -102,7 +105,24 @@
             down.at[:, pl.ds(column(i), width)], down_buf.at[i % slots], down_sem.at[i % slots]
         )
 
-    begin(up_copy)
+    block = text_buf.shape[1]
+    blocks = text.shape[0] // block
+
+    def text_copy(i):
+        return pltpu.make_async_copy(text.at[tile(i, block)], text_buf.at[i % slots], text_sem.at[i % slots])
+
+    def text_norm(i):
+        text_copy(i).wait()
+
+        @pl.when(i + DEEP < blocks)
+        def _():
+            text_copy(i + DEEP).start()
+
+        x = text_buf[i % slots].astype(F32)
+        text_out[tile(i, block), :] = (x * rms_scale(x, x.shape[1]) * rms_gain[...]).astype(BF16)
+
+    begin(up_copy, DEEP)
+    begin(text_copy, DEEP)
     for copy in small:
         copy.wait()
     rows = send.shape[0]
@@ -122,13 +142,16 @@
     total[...] = jnp.broadcast_to(up_bias[...][None, :], total.shape)
 
     def up_body(i):
+        text_norm(i)
         total[...] += dot(merged[:, tile(i, step)], up_buf[i % slots])
 
-    stream(up.shape[0] // step, up_copy, up_body, down_copy)
+    up_steps = up.shape[0] // step
+    stream(up_steps, up_copy, up_body, DEEP, down_copy)
     sums = total[...]
     hidden = (0.5 * sums * (1.0 + lax.erf(sums * math.sqrt(0.5)))).astype(BF16)
 
     def down_body(i):
+        text_norm(up_steps + i)
         part = (dot(hidden, down_buf[i % slots]) + bias_row[:, pl.ds(column(i), width)]).astype(BF16)
         here = tile(i % per_half, width)
 
@@ -140,59 +163,103 @@
         def _():
             keep[:, here] = part
 
-    stream(2 * per_half, down_copy, down_body)
-
-
-def merger(where, patch, gain, bias, up, up_bias, down, down_bias, rows):
+    stream(2 * per_half, down_copy, down_body, DEEP)
+
+
+def merger(where, patch, gain, bias, up, up_bias, down, down_bias, text, rms_gain, rows):
     features = patch.shape[1]
     depth, hidden = up.shape
     columns = down.shape[1]
     step = depth // 8
     width = columns // 8
-    slots = AHEAD + 1
+    slots = DEEP + 1
     return pl.pallas_call(
         merger_kernel,
-        out_shape=[jax.ShapeDtypeStruct((rows, columns // 2), BF16)] * 2,
-        in_specs=[SMEM] + [HBM] * 7,
-        out_specs=[VMEM, VMEM],
+        out_shape=[jax.ShapeDtypeStruct((rows, columns // 2), BF16)] * 2 + [pltpu.VMEM(text.shape, BF16)],
+        in_specs=[SMEM] + [HBM] * 9,
+        out_specs=[VMEM, VMEM, VMEM],
         scratch_shapes=[
             pltpu.VMEM(patch.shape, BF16),
             pltpu.VMEM(gain.shape, F32),
             pltpu.VMEM(bias.shape, F32),
             pltpu.VMEM(up_bias.shape, F32),
             pltpu.VMEM(down_bias.shape, F32),
+            pltpu.VMEM(rms_gain.shape, F32),
             pltpu.VMEM((1, columns), F32),
             pltpu.VMEM((features // 128, patch.shape[0], 128), F32),
             pltpu.VMEM((rows, depth), BF16),
             pltpu.VMEM((rows, hidden), F32),
             pltpu.VMEM((slots, step, hidden), BF16),
             pltpu.VMEM((slots, hidden, width), BF16),
-            pltpu.SemaphoreType.DMA((5,)),
+            pltpu.VMEM((slots, text.shape[0] // 16, text.shape[1]), BF16),
+            pltpu.SemaphoreType.DMA((6,)),
+            pltpu.SemaphoreType.DMA((slots,)),
             pltpu.SemaphoreType.DMA((slots,)),
             pltpu.SemaphoreType.DMA((slots,)),
         ],
-        compiler_params=params(28),
+        compiler_params=params(34),
         cost_estimate=cost(2 * rows * hidden * (depth + columns), 2 * hidden * (depth + columns)),
         name="merger",
-    )(where, *map(in_hbm, (patch, gain, bias, up, up_bias, down, down_bias)))
+    )(where, *map(in_hbm, (patch, gain, bias, up, up_bias, down, down_bias, text, rms_gain)))
+
+
+def weights_kernel(keyval, query, out, query_out, buf, sem, query_sem):
+    depth, _, columns = keyval.shape
+    pieces = sem.shape[0]
+    step = depth // pieces
+
+    def copy(i):
+        return pltpu.make_async_copy(keyval.at[tile(i, step)], buf.at[tile(i, step)], sem.at[i])
+
+    for i in range(pieces):
+        copy(i).start()
+    query_copy = pltpu.make_async_copy(query.at[:, pl.ds(0, query_out.shape[1])], query_out, query_sem)
+    query_copy.start()
+    pairs = buf.reshape(2 * depth, columns)
+    row = lax.broadcasted_iota(jnp.int32, (256, 256), 0)
+    column = lax.broadcasted_iota(jnp.int32, (256, 256), 1)
+    apart = (column == 2 * (row % 128) + row // 128).astype(F32).astype(BF16)
+    together = 4
+
+    @pl.loop(0, pieces)
+    def _(i):
+        copy(i).wait()
+
+        @pl.loop(0, step // (128 * together))
+        def _(j):
+            first = i * (step // 128) + j * together
+            blocks = [pairs[tile(first + n, 256), :] for n in range(together)]
+            sorted_blocks = dot(apart, jnp.concatenate(blocks, axis=1)).astype(BF16)
+            for n in range(together):
+                for side in range(2):
+                    out[tile(first + n, 128), pl.ds(side * columns, columns)] = sorted_blocks[
+                        side * 128 : (side + 1) * 128, n * columns : (n + 1) * columns
+                    ]
+
+    query_copy.wait()
+
+
+def weights_ahead(keyval, query, width):
+    depth, _, columns = keyval.shape
+    return pl.pallas_call(
+        weights_kernel,
+        out_shape=[pltpu.VMEM((depth, 2 * columns), BF16), pltpu.VMEM((depth, width), BF16)],
+        in_specs=[HBM, HBM],
+        out_specs=[VMEM, VMEM],
+        scratch_shapes=[
+            pltpu.VMEM((depth, 2, columns), BF16),
+            pltpu.SemaphoreType.DMA((8,)),
+            pltpu.SemaphoreType.DMA,
+        ],
+        compiler_params=params(12),
+        cost_estimate=cost(4 * depth * columns * 256, 4 * depth * columns + 2 * depth * width),
+        name="weights_ahead",
+    )(in_hbm(keyval), in_hbm(query))
 
 
 def keyval_kernel(where, text, own, sibling, gain, weight, bias, rows_all, *rest):
-    parts = rest[:-5]
-    buf, keyval, text_buf, sem, text_sem = rest[-5:]
-    slots = AHEAD + 1
-    block = text_buf.shape[1]
+    parts, keyval = rest[:-1], rest[-1]
     texts, images = text.shape[0], own.shape[0]
-
-    def text_copy(i):
-        return pltpu.make_async_copy(text.at[tile(i, block)], text_buf.at[i % slots], text_sem.at[i % slots])
-
-    def weight_copy(i):
-        return pltpu.make_async_copy(weight.at[i], buf.at[i], sem.at[i])
-
-    begin(text_copy)
-    for i in range(2):
-        weight_copy(i).start()
     mp = where[0]
     half = own.shape[1]
     mine = mp % 2
@@ -202,20 +269,13 @@
     for values, which in ((first, mine), (second, 1 - mine)):
         here = pl.ds(pl.multiple_of(which * half, half), half)
         rows_all[pl.ds(texts, images), here] = (values * scale * gain[:, here]).astype(BF16)
-
-    def text_body(i):
-        x = text_buf[i % slots].astype(F32)
-        rows_all[tile(i, block), :] = (x * rms_scale(x, 2 * half) * gain[...]).astype(BF16)
-
-    stream(texts // block, text_copy, text_body)
-
-    @pl.loop(0, 2)
-    def _(t):
-        weight_copy(t).wait()
-        keyval[t] = (dot(rows_all[...], buf[t]) + bias[pl.ds(t, 1), :]).astype(BF16)
+    rows_all[pl.ds(0, texts), :] = text[...]
+    columns = weight.shape[1] // 2
+    sums = dot(rows_all[...], weight[...])
+    for t in range(2):
+        keyval[t] = (sums[:, t * columns : (t + 1) * columns] + bias[pl.ds(t, 1), :]).astype(BF16)
 
     count = len(parts)
-    columns = weight.shape[2]
     width = parts[0].shape[1]
     heads = KV_HEADS // count
     coords = columns // KV_HEADS
@@ -230,60 +290,57 @@
 
 def keyval_parts(where, text, own, sibling, gain, weight, bias, count):
     texts, depth = text.shape
-    columns = weight.shape[2]
+    columns = weight.shape[1] // 2
     rows = texts + own.shape[0]
     width = 2 * columns // count
     outs = pl.pallas_call(
         keyval_kernel,
         out_shape=[pltpu.VMEM((rows, depth), BF16)] + [jax.ShapeDtypeStruct((rows, width), BF16)] * count,
-        in_specs=[SMEM, HBM, VMEM, VMEM, VMEM, HBM, VMEM],
+        in_specs=[SMEM, VMEM, VMEM, VMEM, VMEM, VMEM, VMEM],
         out_specs=[VMEM] * (1 + count),
-        scratch_shapes=[
-            pltpu.VMEM((2, depth, columns), BF16),
-            pltpu.VMEM((2, rows, columns), BF16),
-            pltpu.VMEM((AHEAD + 1, 32, depth), BF16),
-            pltpu.SemaphoreType.DMA((2,)),
-            pltpu.SemaphoreType.DMA((AHEAD + 1,)),
-        ],
-        compiler_params=params(18),
+        scratch_shapes=[pltpu.VMEM((2, rows, columns), BF16)],
+        compiler_params=params(8),
         cost_estimate=cost(4 * rows * depth * columns, 4 * depth * columns),
         name="keyval",
-    )(where, in_hbm(text), own, sibling, gain, in_hbm(weight), bias)
+    )(where, in_vmem(text), own, sibling, gain, in_vmem(weight), bias)
     return outs[0], outs[1:]
 
 
-def query_kernel(rows_all, weight, bias, text_out, image_out, buf, sem):
-    width = buf.shape[2]
-    slots = AHEAD + 1
+def query_kernel(rows_all, ready, weight, bias, text_out, image_out, buf, sem):
+    width = ready.shape[1]
     texts = text_out.shape[0]
+    later = buf.shape[0]
 
     def copy(i):
-        return pltpu.make_async_copy(weight.at[:, tile(i, width)], buf.at[i % slots], sem.at[i % slots])
-
-    def body(i):
+        return pltpu.make_async_copy(weight.at[:, tile(i + 1, width)], buf.at[i], sem.at[i])
+
+    def columns(i, weights):
         here = tile(i, width)
-        out = (dot(rows_all[...], buf[i % slots]) + bias[:, here]).astype(BF16)
+        out = (dot(rows_all[...], weights) + bias[:, here]).astype(BF16)
         text_out[:, here] = out[:texts]
         image_out[:, here] = out[texts:]
 
-    begin(copy)
-    stream(weight.shape[1] // width, copy, body)
-
-
-def query_rows(rows_all, texts, weight, bias):
+    begin(copy, 2)
+    columns(0, ready[...])
+    stream(later, copy, lambda i: columns(i + 1, buf[i]), 2)
+
+
+def query_rows(rows_all, texts, ready, weight, bias):
     depth = rows_all.shape[1]
     images = rows_all.shape[0] - texts
     columns = weight.shape[1]
+    width = ready.shape[1]
+    later = columns // width - 1
     return pl.pallas_call(
         query_kernel,
         out_shape=[jax.ShapeDtypeStruct((texts, columns), BF16), jax.ShapeDtypeStruct((images, columns), BF16)],
-        in_specs=[VMEM, HBM, VMEM],
+        in_specs=[VMEM, VMEM, HBM, VMEM],
         out_specs=[VMEM, VMEM],
-        scratch_shapes=[pltpu.VMEM((AHEAD + 1, depth, 256), BF16), pltpu.SemaphoreType.DMA((AHEAD + 1,))],
-        compiler_params=params(24),
+        scratch_shapes=[pltpu.VMEM((later, depth, width), BF16), pltpu.SemaphoreType.DMA((later,))],
+        compiler_params=params(30),
         cost_estimate=cost(2 * (texts + images) * depth * columns, 2 * depth * columns),
         name="query",
-    )(in_vmem(rows_all), in_hbm(weight), bias[None, :])
+    )(in_vmem(rows_all), in_vmem(ready), in_hbm(weight), bias[None, :])
 
 
 def join_parts(mp, parts, first_row, rows):
@@ -302,43 +359,52 @@
     return total.astype(BF16)
 
 
-def slots_kernel(where, owner_rows, owner_columns, queries, *rest):
+def slots_kernel(where, owner_row, queries, *rest):
     parts, out = rest[:-1], rest[-1]
-    owners = owner_rows.shape[0]
     rows, columns = queries.shape
     slots = out.shape[0]
+    owners = owner_row.shape[1] // rows
     mp, me = where[0], where[1]
-    down = owner_columns[pl.ds(pl.multiple_of(me * rows, rows), rows), :]
-    across = owner_rows[pl.ds(me, 1), :]
+    row = lax.broadcasted_iota(jnp.int32, (owners * rows, rows), 0)
+    mine = (row == me * rows + lax.broadcasted_iota(jnp.int32, (owners * rows, rows), 1)).astype(F32).astype(BF16)
+    named = owner_row[...].astype(F32).astype(BF16)
+    across = dot(named, mine)
+    down = lax.dot_general(mine, named, (((0,), (1,)), ((), ())), preferred_element_type=F32)
     earlier = lax.broadcasted_iota(jnp.int32, (rows, rows), 0) < lax.broadcasted_iota(jnp.int32, (rows, rows), 1)
-    rank = jnp.sum(jnp.where((down == across) & earlier, 1, 0), axis=0, keepdims=True)
+    rank = jnp.sum(jnp.where((down == across) & earlier, 1.0, 0.0), axis=0, keepdims=True)
     slot = across * (slots // owners) + rank
-    select = (lax.broadcasted_iota(jnp.int32, (slots, rows), 0) == slot).astype(F32).astype(BF16)
+    select = (lax.broadcasted_iota(jnp.int32, (slots, rows), 0).astype(F32) == slot).astype(F32).astype(BF16)
     out[:, pl.ds(0, columns)] = dot(select, queries[...]).astype(BF16)
     keyval = join_parts(mp, parts, parts[0].shape[0] - rows, rows)
     out[:, pl.ds(columns, out.shape[1] - columns)] = dot(select, keyval).astype(BF16)
 
 
-def slots_of(where, owner_rows, owner_columns, queries, parts, capacity):
-    slots = owner_rows.shape[0] * capacity
+def slots_of(where, owner_row, queries, parts, slots):
     width = queries.shape[1] + 2 * (KV_HEADS // len(parts)) * HEAD_DIM
     return pl.pallas_call(
         slots_kernel,
         out_shape=jax.ShapeDtypeStruct((slots, width), BF16),
-        in_specs=[SMEM] + [VMEM] * (3 + len(parts)),
+        in_specs=[SMEM] + [VMEM] * (2 + len(parts)),
         out_specs=VMEM,
-        compiler_params=params(12),
+        compiler_params=params(8),
         name="slots",
-    )(where, owner_rows, owner_columns, queries, *parts)
-
-
-def attend(blocks, first, doc_column, windows, q_all, kv_all, out):
+    )(where, owner_row, queries, *parts)
+
+
+def attend(blocks, first, doc_row, doc_column, windows, q_all, kv_all, out):
     q_first, k_first, out_first = first
     heads = q_all.shape[1] // HEAD_DIM
     groups = kv_all.shape[1] // (2 * HEAD_DIM)
     shared = heads // groups
     block = DOC_MAX
+    seq = doc_row.shape[1]
     scale = 1.0 / math.sqrt(HEAD_DIM)
+    docs = doc_row[...].astype(F32)
+    for b in range(seq // block):
+        k0 = max(0, b - 1) * block
+        windows[pl.ds(b, 1), :] = docs[:, k0 : k0 + 2 * block]
+    eye = lax.broadcasted_iota(jnp.int32, (seq, seq), 0) == lax.broadcasted_iota(jnp.int32, (seq, seq), 1)
+    doc_column[...] = jnp.sum(jnp.where(eye, docs, 0.0), axis=1, keepdims=True)
     row = lax.broadcasted_iota(jnp.int32, (block, 2 * block), 0)
     column = lax.broadcasted_iota(jnp.int32, (block, 2 * block), 1)
 
@@ -348,9 +414,7 @@
         k0 = pl.multiple_of(jnp.maximum(b - 1, 0) * block, block)
         allowed = (doc_column[pl.ds(q0, block), :] == windows[pl.ds(b, 1), :]) & (k0 + column <= q0 + row)
         penalty = jnp.concatenate([jnp.where(allowed, 0.0, -1e30)] * shared, axis=0)
-
-        @pl.loop(0, groups)
-        def _(g):
+        for g in range(groups):
             keys = kv_all[pl.ds(k0 - k_first, 2 * block), tile(g, HEAD_DIM)]
             values = kv_all[pl.ds(k0 - k_first, 2 * block), tile(groups + g, HEAD_DIM)]
             columns = [tile(g * shared + h, HEAD_DIM) for h in range(shared)]
@@ -358,89 +422,91 @@
             scores = lax.dot_general(q, keys, (((1,), (1,)), ((), ())), preferred_element_type=F32) * scale
             scores = jnp.where(penalty < 0.0, penalty, scores)
             weights = jnp.exp(scores - jnp.max(scores, axis=-1, keepdims=True))
-            probs = (weights / jnp.sum(weights, axis=-1, keepdims=True)).astype(BF16)
+            probs = (weights * (1.0 / jnp.sum(weights, axis=-1, keepdims=True))).astype(BF16)
             result = dot(probs, values).astype(BF16)
             for h, c in enumerate(columns):
                 out[pl.ds(q0 - out_first, block), c] = result[h * block : (h + 1) * block]
 
 
-def late_kernel(early, where, doc_column, windows, queries, *rest):
-    parts, out, kv_all = rest[:-2], rest[-2], rest[-1]
+def late_kernel(early, where, doc_row, queries, *rest):
+    parts = rest[:-4]
+    out, kv_all, doc_column, windows = rest[-4:]
     seq = queries.shape[0]
     first = early - DOC_MAX
     kv_all[...] = join_parts(where[0], parts, first, seq - first)
-    attend((early // DOC_MAX, seq // DOC_MAX), (0, first, 0), doc_column, windows, queries, kv_all, out)
-
-
-def early_kernel(early, where, owner_rows, doc_column, windows, queries, arrived, *rest):
-    parts = rest[:-6]
-    _, out, q_all, kv_all, result, sem = rest[-6:]
+    blocks = (early // DOC_MAX, seq // DOC_MAX)
+    attend(blocks, (0, first, 0), doc_row, doc_column, windows, queries, kv_all, out)
+
+
+def early_kernel(early, owners, where, owner_row, doc_row, queries, arrived, *rest):
+    parts = rest[:-8]
+    _, out, q_all, kv_all, result, doc_column, windows, sem = rest[-8:]
     mp, me = where[0], where[1]
     columns = queries.shape[1]
     slots = arrived.shape[0]
-    owners = owner_rows.shape[0]
     capacity = slots // owners
-    incoming = jnp.sum(jnp.where(owner_rows[...] == me, 1, 0), axis=1, keepdims=True)
-    source = lax.broadcasted_iota(jnp.int32, (owners, slots), 0)
-    slot = lax.broadcasted_iota(jnp.int32, (owners, slots), 1)
-    offset = jnp.sum(jnp.where(source < slot // capacity, incoming, 0), axis=0, keepdims=True)
-    here = jnp.sum(jnp.where(source == slot // capacity, incoming, 0), axis=0, keepdims=True)
-    index = lax.broadcasted_iota(jnp.int32, (1, slots), 1) % capacity
-    target = jnp.where(index < here, offset + index, -1)
-    position = lax.broadcasted_iota(jnp.int32, (slots, slots), 0)
+    named = (owner_row[...] == me).astype(F32).astype(BF16)
+    total = owner_row.shape[1]
+    source = lax.broadcasted_iota(jnp.int32, (total, slots), 0) // (total // owners)
+    block = lax.broadcasted_iota(jnp.int32, (total, slots), 1) // capacity
+    here = dot(named, (source == block).astype(F32).astype(BF16))
+    offset = dot(named, (source < block).astype(F32).astype(BF16))
+    index = (lax.broadcasted_iota(jnp.int32, (1, slots), 1) % capacity).astype(F32)
+    target = jnp.where(index < here, offset + index, -1.0)
+    position = lax.broadcasted_iota(jnp.int32, (slots, slots), 0).astype(F32)
     place = (position == target).astype(F32).astype(BF16)
     placed = dot(place, arrived[...]).astype(BF16)
-    is_image = lax.broadcasted_iota(jnp.int32, (slots, 1), 0) < jnp.sum(incoming, axis=0, keepdims=True)
+    count = jnp.sum(named.astype(F32), axis=1, keepdims=True)
+    is_image = lax.broadcasted_iota(jnp.int32, (slots, 1), 0).astype(F32) < count
 
     keyval = join_parts(mp, parts, 0, early)
     kv_all[...] = keyval
     kv_all[pl.ds(0, slots), :] = jnp.where(is_image, placed[:, columns:], keyval[:slots])
     q_all[...] = queries[pl.ds(0, early), :]
     q_all[pl.ds(0, slots), :] = jnp.where(is_image, placed[:, :columns], queries[pl.ds(0, slots), :])
-    attend((0, early // DOC_MAX), (0, 0, 0), doc_column, windows, q_all, kv_all, result)
+    attend((0, early // DOC_MAX), (0, 0, 0), doc_row, doc_column, windows, q_all, kv_all, result)
     copy = pltpu.make_async_copy(result, out.at[pl.ds(0, early)], sem)
     copy.start()
     copy.wait()
 
 
-def attention(where, owner_rows, documents, queries, parts, capacity):
+def attention(where, owner_row, documents, queries, parts, owners, slots):
     seq, columns = queries.shape
     width = 2 * (KV_HEADS // len(parts)) * HEAD_DIM
-    slots = owner_rows.shape[0] * capacity
     early = min(seq, -(-slots // DOC_MAX) * DOC_MAX + DOC_MAX)
-    windows = jnp.stack([documents[max(0, b - 1) * DOC_MAX :][: 2 * DOC_MAX] for b in range(seq // DOC_MAX)])
-    docs = (documents[:, None], windows)
     shape = jax.ShapeDtypeStruct((seq, columns), BF16)
+    docs = [pltpu.VMEM((seq, 1), F32), pltpu.VMEM((seq // DOC_MAX, 2 * DOC_MAX), F32)]
 
     def late(queries):
         return pl.pallas_call(
             functools.partial(late_kernel, early),
             out_shape=shape,
-            in_specs=[SMEM] + [VMEM] * (3 + len(parts)),
+            in_specs=[SMEM] + [VMEM] * (2 + len(parts)),
             out_specs=VMEM,
-            scratch_shapes=[pltpu.VMEM((seq - early + DOC_MAX, width), BF16)],
-            compiler_params=params(16),
+            scratch_shapes=[pltpu.VMEM((seq - early + DOC_MAX, width), BF16)] + docs,
+            compiler_params=params(12),
             cost_estimate=cost(4 * (seq - early) * columns * 2 * DOC_MAX, 4 * seq * columns),
             name="attention_late",
-        )(where, *docs, queries, *parts)
+        )(where, documents, queries, *parts)
 
     def final(arrived, before):
         return pl.pallas_call(
-            functools.partial(early_kernel, early),
+            functools.partial(early_kernel, early, owners),
             out_shape=shape,
-            in_specs=[SMEM] + [VMEM] * (5 + len(parts)) + [ANY],
+            in_specs=[SMEM] + [VMEM] * (4 + len(parts)) + [ANY],
             out_specs=ANY,
             scratch_shapes=[
                 pltpu.VMEM((early, columns), BF16),
                 pltpu.VMEM((early, width), BF16),
                 pltpu.VMEM((early, columns), BF16),
-                pltpu.SemaphoreType.DMA,
-            ],
-            input_output_aliases={6 + len(parts): 0},
-            compiler_params=params(16),
+            ]
+            + docs
+            + [pltpu.SemaphoreType.DMA],
+            input_output_aliases={5 + len(parts): 0},
+            compiler_params=params(12),
             cost_estimate=cost(4 * early * columns * 2 * DOC_MAX, 4 * seq * columns),
             name="attention_early",
-        )(where, owner_rows, *docs, queries, arrived, *parts, before)
+        )(where, owner_row, documents, queries, arrived, *parts, before)
 
     return late, final
 
@@ -476,15 +542,14 @@
     where = jnp.stack([mp_index, lax.axis_index(("group", "dp"))]).astype(jnp.int32)
     rows = row_owner.shape[0] // owners
     capacity = max(2, 2 * rows // owners)
-    gain = rms_gain[None, :]
-    owner_rows = row_owner.reshape(owners, rows)
-
-    send, keep = merger(
-        where, patch_rows[0], ln_gain, ln_bias, merge_up, merge_up_bias, merge_down, merge_down_bias, rows
+    owner_row = row_owner.reshape(1, -1)
+
+    send, keep, text = merger(
+        where, patch_rows[0], ln_gain, ln_bias, merge_up, merge_up_bias, merge_down, merge_down_bias,
+        text_embed[0], rms_gain[None, :], rows,
     )
-    text = text_embed[0]
     own = (keep.astype(F32) + exchange(send, count, 1).astype(F32)).astype(BF16)
-    weight = jnp.transpose(after(w_keyval, own), (1, 0, 2))
+    weight, ready = weights_ahead(after(w_keyval, own), w_query, w_query.shape[1] // 4)
     bit = 2
     while bit < count:
         other = after(exchange(own, count, bit), weight)
@@ -492,14 +557,14 @@
         bit *= 2
     sibling = exchange(own, count, 1)
 
-    rows_all, parts = keyval_parts(where, text, own, sibling, gain, weight, keyval_bias, count)
+    rows_all, parts = keyval_parts(where, text, own, sibling, rms_gain[None, :], weight, keyval_bias, count)
     parts = [parts[0]] + [exchange(parts[x], count, x) for x in range(1, count)]
-    text_queries, image_queries = query_rows(rows_all, text.shape[0], w_query, query_bias)
-    outgoing = slots_of(where, owner_rows, row_owner, image_queries, parts, capacity)
+    text_queries, image_queries = query_rows(rows_all, text.shape[0], ready, w_query, query_bias)
+    outgoing = slots_of(where, owner_row, image_queries, parts, owners * capacity)
     arrived = lax.all_to_all(
         outgoing.reshape(owners, capacity, -1), ("group", "dp"), split_axis=0, concat_axis=0, tiled=True
     ).reshape(owners * capacity, -1)
-    late, final = attention(where, owner_rows, doc_ids[0], text_queries, parts, capacity)
+    late, final = attention(where, owner_row, doc_ids, text_queries, parts, owners, owners * capacity)
     before = late(after(text_queries, outgoing))
     return final(after(arrived, before), before)[None]
 

time: 77.7 us -> 68.7 us (0.88)
  local copies, waits for them, and re-layouts: 8.64 us -> 0.03 us
  waiting for transfers between devices: 8.84 us -> 10.8 us
  Pallas kernels: 47.6 us -> 46.1 us
    optimization_barrier x1 -> x0, local copies, waits for them, and re-layouts: 7.68 us -> none  [after(): return lax.optimization_barrier((x, *others))[0]]
    pallas_call x1 -> x2, Pallas kernels: 4.15 us -> 11.1 us  [the longest x1 7.4 us: weights_ahead(): pl.pallas_call(weights_kernel, out_shape=[pltpu.VMEM((depth, 2 * columns)...]
    pallas_call x1, Pallas kernels: 10 us -> 3.82 us  [keyval_parts(): pl.pallas_call(keyval_kernel, out_shape=[pltpu.VMEM((rows, depth), BF16)]...]
    pallas_call x1, Pallas kernels: 14 us -> 11.2 us  [query_rows(): pl.pallas_call(query_kernel, out_shape=[jax.ShapeDtypeStruct((texts, colu...]
    ppermute x6, waiting for transfers between devices: 1.28 us -> 2.69 us  [exchange(): return lax.ppermute(x, 'mp', [(i, i ^ bit) for i in range(count)])]
    pallas_call x1, Pallas kernels: 13.5 us -> 14.3 us  [merger(): pl.pallas_call(merger_kernel, out_shape=[jax.ShapeDtypeStruct((rows, colu...]
  transfers between devices with their start and end apart: 7 -> 7, of which waited for: 3 -> 3; matrix products, arithmetic and copies ran while one was open for 12% -> 0% of each run, Pallas kernels for 23% -> 33%
where the time goes in v3:
time: 68.7 us; the launch traced here: 68.5 us
  Pallas kernels  46.1 us (67%)
  starting transfers between devices  11.3 us (16%)
  waiting for transfers between devices  10.8 us (16%)
    pallas_call x1, Pallas kernels, merger(): pl.pallas_call(merger_kernel, out_shape=[jax.ShapeDtypeStruct((rows, colu...  14.3 us
    pallas_call x1, Pallas kernels, query_rows(): pl.pallas_call(query_kernel, out_shape=[jax.ShapeDtypeStruct((texts, colu...  11.2 us
    all_to_all x1, waiting for transfers between devices, per_device(): lax.all_to_all(outgoing.reshape(owners, capacity, -1), ('group', 'dp'), s...  8.09 us
    pallas_call x1, Pallas kernels, weights_ahead(): pl.pallas_call(weights_kernel, out_shape=[pltpu.VMEM((depth, 2 * columns)...  7.4 us
    all_to_all x1, starting transfers between devices, per_device(): lax.all_to_all(outgoing.reshape(owners, capacity, -1), ('group', 'dp'), s...  5.8 us
    ppermute x6, starting transfers between devices, exchange(): return lax.ppermute(x, 'mp', [(i, i ^ bit) for i in range(count)])  5.47 us
    pallas_call x1, Pallas kernels, keyval_parts(): pl.pallas_call(keyval_kernel, out_shape=[pltpu.VMEM((rows, depth), BF16)]...  3.82 us
    pallas_call x1, Pallas kernels, final(): pl.pallas_call(functools.partial(early_kernel, early, owners), out_shape=...  3.7 us
  transfers between devices with their start and end apart: 7, of which 3 were waited for; matrix products, arithmetic and copies ran while one was open for 0% of the time, Pallas kernels for 33%

profile of v3, /device:TPU:0, one launch (start us, length us, event | category | flops | bytes accessed | tf_op | source)
XLA Modules:
  0.0 68.5 jit_solution(10031321371739334851)
XLA Ops:
  0.0 0.1 pad_add_fusion.where
  0.1 14.3 %merger.1 = (bf16[32,4096]{1,0:T(8,128)(2,1)S(1)}, bf16[32,4096]{1,0:T(8,128)(2,1)S(1)}, bf16[256,8192]{1,0:T(8,128)(2,1)S(1)}) custom-call(s32[2]{0:T(128)S(1)} %pad_add_fusion.where, bf16[128,1280]{1,0:T(8,128)(2,1)} %bitcast.17, f32[1280]{0:T(1024)} %gain_in.1, f32[1280]{0:T(1024)} %bias_in.1, bf16[5120,1280]{1,0:T(8,128)(2,1)} %up.1, f32[1280]{0:T(1024)} %up_bias_in.1, ...), custom_call_target="tpu_custom_call" | custom-call | flops 1090519040 | bytes 34078720 | tf_op jit(solution)/shard_map/merger/pallas_call | solution.py:176
  14.4 0.5 collective-permute-start
  14.9 1.2 %collective-permute-done = bf16[32,4096]{1,0:T(8,128)(2,1)S(1)} collective-permute-done((bf16[32,4096]{1,0:T(8,128)(2,1)S(1)}, bf16[32,4096]{1,0:T(8,128)(2,1)S(1)}, u32[]{:S(2)}, u32[]{:S(2)}) %collective-permute-start) | collective-permute-done | bytes 262176 | tf_op jit(solution)/shard_map/ppermute | solution.py:519
  16.1 0.1 add_convert_fusion.1
  16.1 0.0 copy-start
  16.2 0.0 copy-start.4
  16.2 3.0 %collective-permute-start.1 = (bf16[32,4096]{1,0:T(8,128)(2,1)S(1)}, bf16[32,4096]{1,0:T(8,128)(2,1)S(1)}, u32[]{:S(2)}, u32[]{:S(2)}) collective-permute-start(bf16[32,4096]{1,0:T(8,128)(2,1)S(1)} %add_convert_fusion.1), channel_id=1, source_target_pairs={{0,2},{1,3},{2,0},{3,1},{4,6},{5,7},{6,4},{7,5},{8,10},{9,11},{10,... | collective-permute-start | bytes 786440 | tf_op jit(solution)/shard_map/ppermute | solution.py:519
  19.1 7.4 %weights_ahead.1 = (bf16[8192,512]{1,0:T(8,128)(2,1)S(1)}, bf16[8192,512]{1,0:T(8,128)(2,1)S(1)}) custom-call(bf16[8192,2,256]{2,1,0:T(2,128)(2,1)} %keyval.1, bf16[8192,2048]{1,0:T(8,128)(2,1)} %weight.1), custom_call_target="tpu_custom_call" | custom-call | flops 2147483648 | bytes 16777216 | tf_op jit(solution)/shard_map/weights_ahead/pallas_call | solution.py:244
  26.5 0.0 copy-start.1
  26.5 0.0 collective-permute-done.1
  26.6 0.1 add_convert_fusion.own
  26.6 0.1 collective-permute-start.2
  26.7 1.5 %collective-permute-done.2.sibling = bf16[32,4096]{1,0:T(8,128)(2,1)S(1)} collective-permute-done((bf16[32,4096]{1,0:T(8,128)(2,1)S(1)}, bf16[32,4096]{1,0:T(8,128)(2,1)S(1)}, u32[]{:S(2)}, u32[]{:S(2)}) %collective-permute-start.2) | collective-permute-done | bytes 262176 | tf_op jit(solution)/shard_map/ppermute | solution.py:519
  28.2 0.0 copy-done
  28.2 0.0 copy-done.4
  28.2 3.8 %keyval.2 = (bf16[288,8192]{1,0:T(8,128)(2,1)S(1)}, bf16[288,128]{1,0:T(8,128)(2,1)S(1)}, bf16[288,128]{1,0:T(8,128)(2,1)S(1)}, bf16[288,128]{1,0:T(8,128)(2,1)S(1)}, bf16[288,128]{1,0:T(8,128)(2,1)S(1)}) custom-call(s32[2]{0:T(128)S(1)} %pad_add_fusion.where, bf16[256,8192]{1,0:T(8,128)(2,1)S(1)} %get-tuple-element.21.text, ...), custom_call_target="tpu_custom_call" | custom-call | flops 2415919104 | bytes 8388608 | tf_op jit(solution)/shard_map/keyval/pallas_call | solution.py:296
  32.1 0.2 collective-permute-start.3
  32.2 0.9 %collective-permute-start.4 = (bf16[288,128]{1,0:T(8,128)(2,1)S(1)}, bf16[288,128]{1,0:T(8,128)(2,1)S(1)}, u32[]{:S(2)}, u32[]{:S(2)}) collective-permute-start(bf16[288,128]{1,0:T(8,128)(2,1)S(1)} %get-tuple-element.33), channel_id=1, source_target_pairs={{0,2},{1,3},{2,0},{3,1},{4,6},{5,7},{6,4},{7,5},{8,10},{9,11},{10,... | collective-permute-start | bytes 221192 | tf_op jit(solution)/shard_map/ppermute | solution.py:519
  33.2 0.8 %collective-permute-start.5 = (bf16[288,128]{1,0:T(8,128)(2,1)S(1)}, bf16[288,128]{1,0:T(8,128)(2,1)S(1)}, u32[]{:S(2)}, u32[]{:S(2)}) collective-permute-start(bf16[288,128]{1,0:T(8,128)(2,1)S(1)} %get-tuple-element.34), channel_id=1, source_target_pairs={{0,3},{1,2},{2,1},{3,0},{4,7},{5,6},{6,5},{7,4},{8,11},{9,10},{10,... | collective-permute-start | bytes 221192 | tf_op jit(solution)/shard_map/ppermute | solution.py:519
  34.0 0.0 copy-done.1
  34.0 11.2 %query.3 = (bf16[256,2048]{1,0:T(8,128)(2,1)S(1)}, bf16[32,2048]{1,0:T(8,128)(2,1)S(1)}) custom-call(bf16[288,8192]{1,0:T(8,128)(2,1)S(1)} %get-tuple-element.27.rows_all, bf16[8192,512]{1,0:T(8,128)(2,1)S(1)} %get-tuple-element.28.ready, bf16[8192,2048]{1,0:T(8,128)(2,1)} %weight.1, f32[1,2048]{1,0:T(1,128)S(1)} %bitcast.13), custom_call_target="tpu_custom_call" | custom-call | flops 9663676416 | bytes 33554432 | tf_op jit(solution)/shard_map/query/pallas_call | solution.py:334
  45.2 0.0 collective-permute-done.3.rest_1_
  45.2 0.0 collective-permute-done.4.rest_2_
  45.2 0.0 collective-permute-done.5.rest_3_
  45.3 0.0 copy-done.3
  45.3 2.0 %slots.1 = bf16[64,2560]{1,0:T(8,128)(2,1)} custom-call(s32[2]{0:T(128)S(1)} %pad_add_fusion.where, s32[1,256]{1,0:T(1,128)S(1)} %bitcast.14, bf16[32,2048]{1,0:T(8,128)(2,1)S(1)} %get-tuple-element.30.queries, bf16[288,128]{1,0:T(8,128)(2,1)S(1)} %get-tuple-element.31.rest_0_, bf16[288,128]{1,0:T(8,128)(2,1)S(1)} %collective-permute-done.3.rest_1_, ...), custom_call_target="tpu_custom_call" | custom-call | tf_op jit(solution)/shard_map/slots/pallas_call | solution.py:384
  47.2 5.8 %all-to-all-start = ((bf16[8,8,2560]{2,1,0:T(8,128)(2,1)}), bf16[8,8,2560]{2,1,0:T(8,128)(2,1)S(1)}, u32[]{:S(2)}, u32[]{:S(2)}) async-start(bf16[8,8,2560]{2,1,0:T(8,128)(2,1)} %bitcast.7), calls=%async_computation | async-start | bytes 655360 | tf_op jit(solution)/shard_map/all_to_all | solution.py:564
  53.0 0.0 copy-done.2
  53.0 3.7 %attention_late.1.rest_4_ = bf16[256,2048]{1,0:T(8,128)(2,1)} custom-call(s32[2]{0:T(128)S(1)} %pad_add_fusion.where, s32[1,256]{1,0:T(1,128)S(1)} %copy-done.2, bf16[256,2048]{1,0:T(8,128)(2,1)S(1)} %get-tuple-element.35.queries, bf16[288,128]{1,0:T(8,128)(2,1)S(1)} %get-tuple-element.31.rest_0_, bf16[288,128]{1,0:T(8,128)(2,1)S(1)} %collective-permute-done.3.rest_1_, ...), custom_call_target="tpu_custom_call" | custom-call | flops 134217728 | bytes 2097152 | tf_op jit(solution)/shard_map/attention_late/pallas_call | solution.py:481
  56.7 8.1 %all-to-all-done = bf16[8,8,2560]{2,1,0:T(8,128)(2,1)S(1)} async-done(((bf16[8,8,2560]{2,1,0:T(8,128)(2,1)}), bf16[8,8,2560]{2,1,0:T(8,128)(2,1)S(1)}, u32[]{:S(2)}, u32[]{:S(2)}) %all-to-all-start) | async-done | bytes 327712 | tf_op jit(solution)/shard_map/all_to_all | solution.py:564
  64.8 3.7 %attention_early.1 = bf16[256,2048]{1,0:T(8,128)(2,1)} custom-call(s32[2]{0:T(128)S(1)} %pad_add_fusion.where, s32[1,256]{1,0:T(1,128)S(1)} %bitcast.15, s32[1,256]{1,0:T(1,128)S(1)} %copy-done.2, bf16[256,2048]{1,0:T(8,128)(2,1)S(1)} %get-tuple-element.35.queries, bf16[64,2560]{1,0:T(8,128)(2,1)S(1)} %bitcast.10, ...), custom_call_target="tpu_custom_call", output_to_operand_aliasing={{}: (9, {})} | custom-call | flops 134217728 | bytes 2097152 | tf_op jit(solution)/shard_map/attention_early/pallas_call | solution.py:493
  (2 shorter events, 0.0 us)
Async XLA Ops:
  14.4 1.7 %collective-permute-start = (bf16[32,4096]{1,0:T(8,128)(2,1)S(1)}, bf16[32,4096]{1,0:T(8,128)(2,1)S(1)}, u32[]{:S(2)}, u32[]{:S(2)}) collective-permute-start(bf16[32,4096]{1,0:T(8,128)(2,1)S(1)} %get-tuple-element.23), channel_id=1, source_target_pairs={{0,1},{1,0},{2,3},{3,2},{4,5},{5,4},{6,7},{7,6},{8,9},{9,8},{10,11... | collective-permute-start | bytes 786440 | tf_op jit(solution)/shard_map/ppermute | solution.py:519
  16.1 12.1 %copy-start = (f32[8192]{0:T(1024)S(1)}, f32[8192]{0:T(1024)}, u32[]{:S(2)}) copy-start(f32[8192]{0:T(1024)} %param.25) | copy-start | bytes 98308
  16.2 12.1 %copy-start.4 = (f32[2,256]{1,0:T(2,128)S(1)}, f32[2,256]{1,0:T(2,128)}, u32[]{:S(2)}) copy-start(f32[2,256]{1,0:T(2,128)} %bias.1) | copy-start | bytes 6148
  16.2 10.4 %collective-permute-start.1 = (bf16[32,4096]{1,0:T(8,128)(2,1)S(1)}, bf16[32,4096]{1,0:T(8,128)(2,1)S(1)}, u32[]{:S(2)}, u32[]{:S(2)}) collective-permute-start(bf16[32,4096]{1,0:T(8,128)(2,1)S(1)} %add_convert_fusion.1), channel_id=1, source_target_pairs={{0,2},{1,3},{2,0},{3,1},{4,6},{5,7},{6,4},{7,5},{8,10},{9,11},{10,... | collective-permute-start | bytes 786440 | tf_op jit(solution)/shard_map/ppermute | solution.py:519
  26.5 7.5 %copy-start.1 = (f32[2048]{0:T(1024)S(1)}, f32[2048]{0:T(1024)}, u32[]{:S(2)}) copy-start(f32[2048]{0:T(1024)} %param.27) | copy-start | bytes 24580
  26.6 1.6 %collective-permute-start.2 = (bf16[32,4096]{1,0:T(8,128)(2,1)S(1)}, bf16[32,4096]{1,0:T(8,128)(2,1)S(1)}, u32[]{:S(2)}, u32[]{:S(2)}) collective-permute-start(bf16[32,4096]{1,0:T(8,128)(2,1)S(1)} %add_convert_fusion.own), channel_id=1, source_target_pairs={{0,1},{1,0},{2,3},{3,2},{4,5},{5,4},{6,7},{7,6},{8,9},{9,8},{10,11... | collective-permute-start | bytes 786440 | tf_op jit(solution)/shard_map/ppermute | solution.py:519
  32.1 13.2 %collective-permute-start.3 = (bf16[288,128]{1,0:T(8,128)(2,1)S(1)}, bf16[288,128]{1,0:T(8,128)(2,1)S(1)}, u32[]{:S(2)}, u32[]{:S(2)}) collective-permute-start(bf16[288,128]{1,0:T(8,128)(2,1)S(1)} %get-tuple-element.32), channel_id=1, source_target_pairs={{0,1},{1,0},{2,3},{3,2},{4,5},{5,4},{6,7},{7,6},{8,9},{9,8},{10,11... | collective-permute-start | bytes 221192 | tf_op jit(solution)/shard_map/ppermute | solution.py:519
  32.2 13.0 %collective-permute-start.4 = (bf16[288,128]{1,0:T(8,128)(2,1)S(1)}, bf16[288,128]{1,0:T(8,128)(2,1)S(1)}, u32[]{:S(2)}, u32[]{:S(2)}) collective-permute-start(bf16[288,128]{1,0:T(8,128)(2,1)S(1)} %get-tuple-element.33), channel_id=1, source_target_pairs={{0,2},{1,3},{2,0},{3,1},{4,6},{5,7},{6,4},{7,5},{8,10},{9,11},{10,... | collective-permute-start | bytes 221192 | tf_op jit(solution)/shard_map/ppermute | solution.py:519
  33.2 12.1 %collective-permute-start.5 = (bf16[288,128]{1,0:T(8,128)(2,1)S(1)}, bf16[288,128]{1,0:T(8,128)(2,1)S(1)}, u32[]{:S(2)}, u32[]{:S(2)}) collective-permute-start(bf16[288,128]{1,0:T(8,128)(2,1)S(1)} %get-tuple-element.34), channel_id=1, source_target_pairs={{0,3},{1,2},{2,1},{3,0},{4,7},{5,6},{6,5},{7,4},{8,11},{9,10},{10,... | collective-permute-start | bytes 221192 | tf_op jit(solution)/shard_map/ppermute | solution.py:519
  34.0 11.3 %copy-start.3 = (s32[256,1]{0,1:T(1,128)S(1)}, s32[256,1]{0,1:T(1,128)}, u32[]{:S(2)}) copy-start(s32[256,1]{0,1:T(1,128)} %param.22) | copy-start | bytes 3076
  34.0 19.0 %copy-start.2 = (s32[1,256]{1,0:T(1,128)S(1)}, s32[1,256]{1,0:T(1,128)}, u32[]{:S(2)}) copy-start(s32[1,256]{1,0:T(1,128)} %doc_row.3) | copy-start | bytes 3076
  47.2 17.6 %all-to-all-start = ((bf16[8,8,2560]{2,1,0:T(8,128)(2,1)}), bf16[8,8,2560]{2,1,0:T(8,128)(2,1)S(1)}, u32[]{:S(2)}, u32[]{:S(2)}) async-start(bf16[8,8,2560]{2,1,0:T(8,128)(2,1)} %bitcast.7), calls=%async_computation | async-start | bytes 655360 | tf_op jit(solution)/shard_map/all_to_all | solution.py:564

commit v4 on v3

--- a/solution.py
+++ b/solution.py
@@ -203,40 +203,35 @@
     )(where, *map(in_hbm, (patch, gain, bias, up, up_bias, down, down_bias, text, rms_gain)))
 
 
-def weights_kernel(keyval, query, out, query_out, buf, sem, query_sem):
+def weights_kernel(keyval, query, out, query_out, sem):
     depth, _, columns = keyval.shape
     pieces = sem.shape[0]
     step = depth // pieces
-
-    def copy(i):
-        return pltpu.make_async_copy(keyval.at[tile(i, step)], buf.at[tile(i, step)], sem.at[i])
-
-    for i in range(pieces):
-        copy(i).start()
-    query_copy = pltpu.make_async_copy(query.at[:, pl.ds(0, query_out.shape[1])], query_out, query_sem)
-    query_copy.start()
-    pairs = buf.reshape(2 * depth, columns)
+    width = query_out.shape[1]
+    copies = [
+        pltpu.make_async_copy(query.at[pl.ds(i * step, step), pl.ds(0, width)], query_out.at[pl.ds(i * step, step)], sem.at[i])
+        for i in range(pieces)
+    ]
+    for copy in copies:
+        copy.start()
+    pairs = keyval.reshape(2 * depth, columns)
     row = lax.broadcasted_iota(jnp.int32, (256, 256), 0)
     column = lax.broadcasted_iota(jnp.int32, (256, 256), 1)
     apart = (column == 2 * (row % 128) + row // 128).astype(F32).astype(BF16)
-    together = 4
-
-    @pl.loop(0, pieces)
-    def _(i):
-        copy(i).wait()
-
-        @pl.loop(0, step // (128 * together))
-        def _(j):
-            first = i * (step // 128) + j * together
-            blocks = [pairs[tile(first + n, 256), :] for n in range(together)]
-            sorted_blocks = dot(apart, jnp.concatenate(blocks, axis=1)).astype(BF16)
-            for n in range(together):
-                for side in range(2):
-                    out[tile(first + n, 128), pl.ds(side * columns, columns)] = sorted_blocks[
-                        side * 128 : (side + 1) * 128, n * columns : (n + 1) * columns
-                    ]
-
-    query_copy.wait()
+    together = 8
+
+    @pl.loop(0, depth // (128 * together))
+    def _(j):
+        blocks = [pairs[tile(j * together + n, 256), :] for n in range(together)]
+        ordered = dot(apart, jnp.concatenate(blocks, axis=1)).astype(BF16)
+        for n in range(together):
+            for side in range(2):
+                out[tile(j * together + n, 128), pl.ds(side * columns, columns)] = ordered[
+                    side * 128 : (side + 1) * 128, n * columns : (n + 1) * columns
+                ]
+
+    for copy in copies:
+        copy.wait()
 
 
 def weights_ahead(keyval, query, width):
@@ -244,17 +239,13 @@
     return pl.pallas_call(
         weights_kernel,
         out_shape=[pltpu.VMEM((depth, 2 * columns), BF16), pltpu.VMEM((depth, width), BF16)],
-        in_specs=[HBM, HBM],
+        in_specs=[VMEM, HBM],
         out_specs=[VMEM, VMEM],
-        scratch_shapes=[
-            pltpu.VMEM((depth, 2, columns), BF16),
-            pltpu.SemaphoreType.DMA((8,)),
-            pltpu.SemaphoreType.DMA,
-        ],
-        compiler_params=params(12),
+        scratch_shapes=[pltpu.SemaphoreType.DMA((4,))],
+        compiler_params=params(8),
         cost_estimate=cost(4 * depth * columns * 256, 4 * depth * columns + 2 * depth * width),
         name="weights_ahead",
-    )(in_hbm(keyval), in_hbm(query))
+    )(in_vmem(keyval), in_hbm(query))
 
 
 def keyval_kernel(where, text, own, sibling, gain, weight, bias, rows_all, *rest):
@@ -295,7 +286,8 @@
     width = 2 * columns // count
     outs = pl.pallas_call(
         keyval_kernel,
-        out_shape=[pltpu.VMEM((rows, depth), BF16)] + [jax.ShapeDtypeStruct((rows, width), BF16)] * count,
+        out_shape=[pltpu.VMEM((rows, depth), BF16)]
+        + [jax.ShapeDtypeStruct((rows, width), BF16)] * count,
         in_specs=[SMEM, VMEM, VMEM, VMEM, VMEM, VMEM, VMEM],
         out_specs=[VMEM] * (1 + count),
         scratch_shapes=[pltpu.VMEM((2, rows, columns), BF16)],
@@ -306,23 +298,29 @@
     return outs[0], outs[1:]
 
 
-def query_kernel(rows_all, ready, weight, bias, text_out, image_out, buf, sem):
+def query_kernel(rows_all, ready, weight, bias, first_half, second_half, image_out, buf, sem):
     width = ready.shape[1]
-    texts = text_out.shape[0]
+    texts, half = first_half.shape
     later = buf.shape[0]
 
     def copy(i):
         return pltpu.make_async_copy(weight.at[:, tile(i + 1, width)], buf.at[i], sem.at[i])
 
-    def columns(i, weights):
-        here = tile(i, width)
-        out = (dot(rows_all[...], weights) + bias[:, here]).astype(BF16)
-        text_out[:, here] = out[:texts]
-        image_out[:, here] = out[texts:]
+    def columns(i, weights, text_out, offset):
+        out = (dot(rows_all[...], weights) + bias[:, tile(i, width)]).astype(BF16)
+        text_out[:, pl.ds(i * width - offset, width)] = out[:texts]
+        image_out[:, tile(i, width)] = out[texts:]
 
     begin(copy, 2)
-    columns(0, ready[...])
-    stream(later, copy, lambda i: columns(i + 1, buf[i]), 2)
+    columns(0, ready[...], first_half, 0)
+    for i in range(1, later + 1):
+        copy(i - 1).wait()
+        if i + 1 < later:
+            copy(i + 1).start()
+        if i * width < half:
+            columns(i, buf[i - 1], first_half, 0)
+        else:
+            columns(i, buf[i - 1], second_half, half)
 
 
 def query_rows(rows_all, texts, ready, weight, bias):
@@ -333,182 +331,174 @@
     later = columns // width - 1
     return pl.pallas_call(
         query_kernel,
-        out_shape=[jax.ShapeDtypeStruct((texts, columns), BF16), jax.ShapeDtypeStruct((images, columns), BF16)],
+        out_shape=[jax.ShapeDtypeStruct((texts, columns // 2), BF16)] * 2 + [jax.ShapeDtypeStruct((images, columns), BF16)],
         in_specs=[VMEM, VMEM, HBM, VMEM],
-        out_specs=[VMEM, VMEM],
+        out_specs=[VMEM] * 3,
         scratch_shapes=[pltpu.VMEM((later, depth, width), BF16), pltpu.SemaphoreType.DMA((later,))],
         compiler_params=params(30),
         cost_estimate=cost(2 * (texts + images) * depth * columns, 2 * depth * columns),
         name="query",
-    )(in_vmem(rows_all), in_vmem(ready), in_hbm(weight), bias[None, :])
-
-
-def join_parts(mp, parts, first_row, rows):
-    count = len(parts)
-    width = parts[0].shape[1]
+    )(in_vmem(rows_all), in_vmem(ready), in_hbm(weight), bias)
+
+
+def join_matrix(mp, count, width):
     heads = KV_HEADS // count
     coords = HEAD_DIM // count
     full = 2 * heads * HEAD_DIM
+    column = lax.broadcasted_iota(jnp.int32, (width, full), 1)
     row = lax.broadcasted_iota(jnp.int32, (width, full), 0)
-    column = lax.broadcasted_iota(jnp.int32, (width, full), 1)
-    total = jnp.zeros((rows, full), F32)
-    for x in range(count):
-        coordinate = (mp ^ x) * coords + row % coords
-        place = (column == (row // coords) * HEAD_DIM + coordinate).astype(BF16)
-        total = total + dot(parts[x][pl.ds(first_row, rows), :], place)
-    return total.astype(BF16)
-
-
-def slots_kernel(where, owner_row, queries, *rest):
-    parts, out = rest[:-1], rest[-1]
+    base = (row // coords) * HEAD_DIM + row % coords
+    places = [(column == base + (mp ^ x) * coords).astype(F32).astype(BF16) for x in range(count)]
+    return jnp.concatenate(places, axis=0)
+
+
+def slots_kernel(owners, where, owner_row, queries, *rest):
+    parts, outs = rest[:-owners], rest[-owners:]
     rows, columns = queries.shape
-    slots = out.shape[0]
-    owners = owner_row.shape[1] // rows
-    mp, me = where[0], where[1]
+    capacity = outs[0].shape[0]
+    slots = owners * capacity
+    me = where[1]
     row = lax.broadcasted_iota(jnp.int32, (owners * rows, rows), 0)
     mine = (row == me * rows + lax.broadcasted_iota(jnp.int32, (owners * rows, rows), 1)).astype(F32).astype(BF16)
-    named = owner_row[...].astype(F32).astype(BF16)
+    named = (owner_row[...] ^ me).astype(F32).astype(BF16)
     across = dot(named, mine)
     down = lax.dot_general(mine, named, (((0,), (1,)), ((), ())), preferred_element_type=F32)
     earlier = lax.broadcasted_iota(jnp.int32, (rows, rows), 0) < lax.broadcasted_iota(jnp.int32, (rows, rows), 1)
     rank = jnp.sum(jnp.where((down == across) & earlier, 1.0, 0.0), axis=0, keepdims=True)
-    slot = across * (slots // owners) + rank
+    slot = across * capacity + rank
     select = (lax.broadcasted_iota(jnp.int32, (slots, rows), 0).astype(F32) == slot).astype(F32).astype(BF16)
-    out[:, pl.ds(0, columns)] = dot(select, queries[...]).astype(BF16)
-    keyval = join_parts(mp, parts, parts[0].shape[0] - rows, rows)
-    out[:, pl.ds(columns, out.shape[1] - columns)] = dot(select, keyval).astype(BF16)
-
-
-def slots_of(where, owner_row, queries, parts, slots):
-    width = queries.shape[1] + 2 * (KV_HEADS // len(parts)) * HEAD_DIM
+    width = parts[0].shape[1]
+    images = [queries[...]] + [part[pl.ds(part.shape[0] - rows, rows), :] for part in parts]
+    chosen = dot(select, jnp.concatenate(images, axis=1))
+    for x, out in enumerate(outs):
+        out[...] = chosen[x * capacity : (x + 1) * capacity].astype(BF16)
+
+
+def slots_of(where, owner_row, queries, parts, owners, capacity):
+    width = queries.shape[1] + len(parts) * parts[0].shape[1]
     return pl.pallas_call(
-        slots_kernel,
-        out_shape=jax.ShapeDtypeStruct((slots, width), BF16),
+        functools.partial(slots_kernel, owners),
+        out_shape=[jax.ShapeDtypeStruct((capacity, width), BF16)] * owners,
         in_specs=[SMEM] + [VMEM] * (2 + len(parts)),
-        out_specs=VMEM,
+        out_specs=[VMEM] * owners,
         compiler_params=params(8),
         name="slots",
     )(where, owner_row, queries, *parts)
 
 
-def attend(blocks, first, doc_row, doc_column, windows, q_all, kv_all, out):
+def attend(blocks, first, doc_row, queries, kv_all, out):
     q_first, k_first, out_first = first
-    heads = q_all.shape[1] // HEAD_DIM
     groups = kv_all.shape[1] // (2 * HEAD_DIM)
-    shared = heads // groups
+    per_half = groups // len(queries)
+    shared = queries[0].shape[1] // HEAD_DIM // per_half
     block = DOC_MAX
-    seq = doc_row.shape[1]
     scale = 1.0 / math.sqrt(HEAD_DIM)
     docs = doc_row[...].astype(F32)
-    for b in range(seq // block):
-        k0 = max(0, b - 1) * block
-        windows[pl.ds(b, 1), :] = docs[:, k0 : k0 + 2 * block]
-    eye = lax.broadcasted_iota(jnp.int32, (seq, seq), 0) == lax.broadcasted_iota(jnp.int32, (seq, seq), 1)
-    doc_column[...] = jnp.sum(jnp.where(eye, docs, 0.0), axis=1, keepdims=True)
     row = lax.broadcasted_iota(jnp.int32, (block, 2 * block), 0)
     column = lax.broadcasted_iota(jnp.int32, (block, 2 * block), 1)
-
-    @pl.loop(blocks[0], blocks[1])
-    def _(b):
-        q0 = pl.multiple_of(b * block, block)
-        k0 = pl.multiple_of(jnp.maximum(b - 1, 0) * block, block)
-        allowed = (doc_column[pl.ds(q0, block), :] == windows[pl.ds(b, 1), :]) & (k0 + column <= q0 + row)
+    for b in range(*blocks):
+        q0 = b * block
+        k0 = max(0, b - 1) * block
+        k_doc = docs[:, k0 : k0 + 2 * block]
+        q_doc = jnp.sum(jnp.where(k0 + column == q0 + row, k_doc, 0.0), axis=1, keepdims=True)
+        allowed = (q_doc == k_doc) & (k0 + column <= q0 + row)
         penalty = jnp.concatenate([jnp.where(allowed, 0.0, -1e30)] * shared, axis=0)
         for g in range(groups):
             keys = kv_all[pl.ds(k0 - k_first, 2 * block), tile(g, HEAD_DIM)]
             values = kv_all[pl.ds(k0 - k_first, 2 * block), tile(groups + g, HEAD_DIM)]
-            columns = [tile(g * shared + h, HEAD_DIM) for h in range(shared)]
-            q = jnp.concatenate([q_all[pl.ds(q0 - q_first, block), c] for c in columns], axis=0)
+            source = queries[g // per_half]
+            columns = [tile((g % per_half) * shared + h, HEAD_DIM) for h in range(shared)]
+            q = jnp.concatenate([source[pl.ds(q0 - q_first, block), c] for c in columns], axis=0)
             scores = lax.dot_general(q, keys, (((1,), (1,)), ((), ())), preferred_element_type=F32) * scale
             scores = jnp.where(penalty < 0.0, penalty, scores)
             weights = jnp.exp(scores - jnp.max(scores, axis=-1, keepdims=True))
             probs = (weights * (1.0 / jnp.sum(weights, axis=-1, keepdims=True))).astype(BF16)
             result = dot(probs, values).astype(BF16)
-            for h, c in enumerate(columns):
-                out[pl.ds(q0 - out_first, block), c] = result[h * block : (h + 1) * block]
-
-
-def late_kernel(early, where, doc_row, queries, *rest):
+            for h in range(shared):
+                out[pl.ds(q0 - out_first, block), tile(g * shared + h, HEAD_DIM)] = result[h * block : (h + 1) * block]
+        yield b
+
+
+def late_kernel(early, owners, where, owner_row, doc_row, first_half, second_half, *rest):
     parts = rest[:-4]
-    out, kv_all, doc_column, windows = rest[-4:]
-    seq = queries.shape[0]
-    first = early - DOC_MAX
-    kv_all[...] = join_parts(where[0], parts, first, seq - first)
-    blocks = (early // DOC_MAX, seq // DOC_MAX)
-    attend(blocks, (0, first, 0), doc_row, doc_column, windows, queries, kv_all, out)
-
-
-def early_kernel(early, owners, where, owner_row, doc_row, queries, arrived, *rest):
-    parts = rest[:-8]
-    _, out, q_all, kv_all, result, doc_column, windows, sem = rest[-8:]
+    out, kv_all, join, place = rest[-4:]
     mp, me = where[0], where[1]
-    columns = queries.shape[1]
-    slots = arrived.shape[0]
+    seq = first_half.shape[0]
+    join[...] = join_matrix(mp, len(parts), parts[0].shape[1])
+    sent = jnp.concatenate([part[pl.ds(0, seq), :] for part in parts], axis=1)
+    kv_all[...] = dot(sent, join[...]).astype(BF16)
+    slots = place.shape[0]
     capacity = slots // owners
     named = (owner_row[...] == me).astype(F32).astype(BF16)
     total = owner_row.shape[1]
     source = lax.broadcasted_iota(jnp.int32, (total, slots), 0) // (total // owners)
-    block = lax.broadcasted_iota(jnp.int32, (total, slots), 1) // capacity
+    block = (lax.broadcasted_iota(jnp.int32, (total, slots), 1) // capacity) ^ me
     here = dot(named, (source == block).astype(F32).astype(BF16))
     offset = dot(named, (source < block).astype(F32).astype(BF16))
     index = (lax.broadcasted_iota(jnp.int32, (1, slots), 1) % capacity).astype(F32)
     target = jnp.where(index < here, offset + index, -1.0)
     position = lax.broadcasted_iota(jnp.int32, (slots, slots), 0).astype(F32)
-    place = (position == target).astype(F32).astype(BF16)
-    placed = dot(place, arrived[...]).astype(BF16)
-    count = jnp.sum(named.astype(F32), axis=1, keepdims=True)
-    is_image = lax.broadcasted_iota(jnp.int32, (slots, 1), 0).astype(F32) < count
-
-    keyval = join_parts(mp, parts, 0, early)
-    kv_all[...] = keyval
-    kv_all[pl.ds(0, slots), :] = jnp.where(is_image, placed[:, columns:], keyval[:slots])
-    q_all[...] = queries[pl.ds(0, early), :]
-    q_all[pl.ds(0, slots), :] = jnp.where(is_image, placed[:, :columns], queries[pl.ds(0, slots), :])
-    attend((0, early // DOC_MAX), (0, 0, 0), doc_row, doc_column, windows, q_all, kv_all, result)
-    copy = pltpu.make_async_copy(result, out.at[pl.ds(0, early)], sem)
-    copy.start()
-    copy.wait()
-
-
-def attention(where, owner_row, documents, queries, parts, owners, slots):
-    seq, columns = queries.shape
-    width = 2 * (KV_HEADS // len(parts)) * HEAD_DIM
+    place[...] = (position == target).astype(F32).astype(BF16)
+    blocks = (early // DOC_MAX, seq // DOC_MAX)
+    for _ in attend(blocks, (0, 0, early), doc_row, (first_half, second_half), kv_all, out):
+        pass
+
+
+def early_kernel(early, doc_row, first_half, second_half, keyval, join, place, *rest):
+    arrived = rest[:-7]
+    late, out, first, second, kv_all, result, sem = rest[-7:]
+    slots = place.shape[0]
+    copies = [pltpu.make_async_copy(late, out.at[pl.ds(early, late.shape[0])], sem.at[0])]
+    copies[0].start()
+    half = first_half.shape[1]
+    together = jnp.concatenate([rows[...].astype(F32) for rows in arrived], axis=0).astype(BF16)
+    placed = dot(place[...], together).astype(BF16)
+    is_image = jnp.sum(place[...].astype(F32), axis=1, keepdims=True) > 0.5
+    image_keyval = dot(placed[:, 2 * half :], join[...]).astype(BF16)
+    kv_all[...] = keyval[pl.ds(0, early), :]
+    kv_all[pl.ds(0, slots), :] = jnp.where(is_image, image_keyval, keyval[pl.ds(0, slots), :])
+    for i, (source, target) in enumerate(((first_half, first), (second_half, second))):
+        target[...] = source[pl.ds(0, early), :]
+        target[pl.ds(0, slots), :] = jnp.where(
+            is_image, placed[:, i * half : (i + 1) * half], source[pl.ds(0, slots), :]
+        )
+    for b in attend((0, early // DOC_MAX), (0, 0, 0), doc_row, (first, second), kv_all, result):
+        here = pl.ds(b * DOC_MAX, DOC_MAX)
+        copies.append(pltpu.make_async_copy(result.at[here], out.at[here], sem.at[b + 1]))
+        copies[-1].start()
+    for copy in copies:
+        copy.wait()
+
+
+def attention(where, owner_row, documents, halves, parts, arrived, owners, slots, columns):
+    seq = documents.shape[1]
+    full = 2 * (KV_HEADS // len(parts)) * HEAD_DIM
     early = min(seq, -(-slots // DOC_MAX) * DOC_MAX + DOC_MAX)
-    shape = jax.ShapeDtypeStruct((seq, columns), BF16)
-    docs = [pltpu.VMEM((seq, 1), F32), pltpu.VMEM((seq // DOC_MAX, 2 * DOC_MAX), F32)]
-
-    def late(queries):
-        return pl.pallas_call(
-            functools.partial(late_kernel, early),
-            out_shape=shape,
-            in_specs=[SMEM] + [VMEM] * (2 + len(parts)),
-            out_specs=VMEM,
-            scratch_shapes=[pltpu.VMEM((seq - early + DOC_MAX, width), BF16)] + docs,
-            compiler_params=params(12),
-            cost_estimate=cost(4 * (seq - early) * columns * 2 * DOC_MAX, 4 * seq * columns),
-            name="attention_late",
-        )(where, documents, queries, *parts)
-
-    def final(arrived, before):
-        return pl.pallas_call(
-            functools.partial(early_kernel, early, owners),
-            out_shape=shape,
-            in_specs=[SMEM] + [VMEM] * (4 + len(parts)) + [ANY],
-            out_specs=ANY,
-            scratch_shapes=[
-                pltpu.VMEM((early, columns), BF16),
-                pltpu.VMEM((early, width), BF16),
-                pltpu.VMEM((early, columns), BF16),
-            ]
-            + docs
-            + [pltpu.SemaphoreType.DMA],
-            input_output_aliases={5 + len(parts): 0},
-            compiler_params=params(12),
-            cost_estimate=cost(4 * early * columns * 2 * DOC_MAX, 4 * seq * columns),
-            name="attention_early",
-        )(where, owner_row, documents, queries, arrived, *parts, before)
-
-    return late, final
+    out, keyval, join, place = pl.pallas_call(
+        functools.partial(late_kernel, early, owners),
+        out_shape=[
+            pltpu.VMEM((seq - early, columns), BF16),
+            jax.ShapeDtypeStruct((seq, full), BF16),
+            jax.ShapeDtypeStruct((len(parts) * parts[0].shape[1], full), BF16),
+            jax.ShapeDtypeStruct((slots, slots), BF16),
+        ],
+        in_specs=[SMEM] + [VMEM] * (4 + len(parts)),
+        out_specs=[VMEM] * 4,
+        compiler_params=params(12),
+        cost_estimate=cost(4 * (seq - early) * columns * 2 * DOC_MAX, 4 * seq * columns),
+        name="attention_late",
+    )(where, owner_row, documents, *halves, *parts)
+    return pl.pallas_call(
+        functools.partial(early_kernel, early),
+        out_shape=jax.ShapeDtypeStruct((seq, columns), BF16),
+        in_specs=[VMEM] * (7 + owners),
+        out_specs=HBM,
+        scratch_shapes=[pltpu.VMEM((early, columns // 2), BF16)] * 2
+        + [pltpu.VMEM((early, full), BF16), pltpu.VMEM((early, columns), BF16), pltpu.SemaphoreType.DMA((1 + early // DOC_MAX,))],
+        compiler_params=params(12),
+        cost_estimate=cost(4 * early * columns * 2 * DOC_MAX, 4 * seq * columns),
+        name="attention_early",
+    )(documents, *halves, keyval, join, place, *arrived(out), in_vmem(out))
 
 
 def after(x, *others):
@@ -549,7 +539,7 @@
         text_embed[0], rms_gain[None, :], rows,
     )
     own = (keep.astype(F32) + exchange(send, count, 1).astype(F32)).astype(BF16)
-    weight, ready = weights_ahead(after(w_keyval, own), w_query, w_query.shape[1] // 4)
+    weight, ready = weights_ahead(after(w_keyval, send), w_query, w_query.shape[1] // 4)
     bit = 2
     while bit < count:
         other = after(exchange(own, count, bit), weight)
@@ -557,16 +547,22 @@
         bit *= 2
     sibling = exchange(own, count, 1)
 
+    columns = w_query.shape[1]
     rows_all, parts = keyval_parts(where, text, own, sibling, rms_gain[None, :], weight, keyval_bias, count)
     parts = [parts[0]] + [exchange(parts[x], count, x) for x in range(1, count)]
-    text_queries, image_queries = query_rows(rows_all, text.shape[0], ready, w_query, query_bias)
-    outgoing = slots_of(where, owner_row, image_queries, parts, owners * capacity)
-    arrived = lax.all_to_all(
-        outgoing.reshape(owners, capacity, -1), ("group", "dp"), split_axis=0, concat_axis=0, tiled=True
-    ).reshape(owners * capacity, -1)
-    late, final = attention(where, owner_row, doc_ids, text_queries, parts, owners, owners * capacity)
-    before = late(after(text_queries, outgoing))
-    return final(after(arrived, before), before)[None]
+    *halves, image_queries = query_rows(rows_all, text.shape[0], ready, w_query, query_bias[None, :])
+    outgoing = slots_of(where, owner_row, image_queries, parts, owners, capacity)
+
+    def arrived(done):
+        rows = [
+            lax.ppermute(outgoing[x], ("group", "dp"), [(i, i ^ x) for i in range(owners)]) for x in range(1, owners)
+        ]
+        return lax.optimization_barrier((outgoing[0], *rows, done))[:-1]
+
+    halves = [after(half, outgoing[0]) for half in halves]
+    return attention(
+        where, owner_row, doc_ids, halves, parts, arrived, owners, owners * capacity, columns
+    )[None]
 
 
 def general(
@@ -696,6 +692,7 @@
     )
     out_specs = P(("group", "dp"), None, "mp")
     count = mesh.shape["mp"]
-    narrow = count < 2 or count > KV_HEADS or count & (count - 1)
+    owners = mesh.shape["group"] * mesh.shape["dp"]
+    narrow = count < 2 or count > KV_HEADS or count & (count - 1) or owners & (owners - 1)
     body = general if narrow else per_device
     return jax.shard_map(body, mesh=mesh, in_specs=in_specs, out_specs=out_specs, check_vma=False)

time: 68.7 us -> 66.3 us (0.965)
  starting transfers between devices: 11.3 us -> 17.4 us
  Pallas kernels: 46.1 us -> 40.8 us
  waiting for transfers between devices: 10.8 us -> 7.56 us
    ppermute x0 -> x7, starting transfers between devices: none -> 11.9 us  [arrived(): lax.ppermute(outgoing[x], ('group', 'dp'), [(i, i ^ x) for i in range(own...]
    all_to_all x1 -> x0, waiting for transfers between devices: 8.09 us -> none  [per_device(): lax.all_to_all(outgoing.reshape(owners, capacity, -1), ('group', 'dp'), s...]
    all_to_all x1 -> x0, starting transfers between devices: 5.8 us -> none  [per_device(): lax.all_to_all(outgoing.reshape(owners, capacity, -1), ('group', 'dp'), s...]
    pallas_call x3, Pallas kernels: 9.35 us -> 6.07 us  [the longest x1 2.78 us: attention(): pl.pallas_call(functools.partial(late_kernel, early, owners), out_shape=[...]
    ppermute x0 -> x7, waiting for transfers between devices: none -> 3.19 us  [arrived(): lax.ppermute(outgoing[x], ('group', 'dp'), [(i, i ^ x) for i in range(own...]
    pallas_call x1, Pallas kernels: 7.4 us -> 4.91 us  [weights_ahead(): pl.pallas_call(weights_kernel, out_shape=[pltpu.VMEM((depth, 2 * columns)...]
    ppermute x6, waiting for transfers between devices: 2.69 us -> 4.37 us  [exchange(): return lax.ppermute(x, 'mp', [(i, i ^ bit) for i in range(count)])]
  transfers between devices with their start and end apart: 7 -> 13, of which waited for: 3 -> 4; matrix products, arithmetic and copies ran while one was open for 0% -> 0% of each run, Pallas kernels for 33% -> 29%
where the time goes in v4:
time: 66.3 us; the launch traced here: 66.1 us
  Pallas kernels  40.8 us (62%)
  starting transfers between devices  17.4 us (26%)
  waiting for transfers between devices  7.56 us (11%)
    pallas_call x1, Pallas kernels, merger(): pl.pallas_call(merger_kernel, out_shape=[jax.ShapeDtypeStruct((rows, colu...  14.8 us
    ppermute x7, starting transfers between devices, arrived(): lax.ppermute(outgoing[x], ('group', 'dp'), [(i, i ^ x) for i in range(own...  11.9 us
    pallas_call x1, Pallas kernels, query_rows(): pl.pallas_call(query_kernel, out_shape=[jax.ShapeDtypeStruct((texts, colu...  11.2 us
    ppermute x6, starting transfers between devices, exchange(): return lax.ppermute(x, 'mp', [(i, i ^ bit) for i in range(count)])  5.53 us
    pallas_call x1, Pallas kernels, weights_ahead(): pl.pallas_call(weights_kernel, out_shape=[pltpu.VMEM((depth, 2 * columns)...  4.91 us
    ppermute x6, waiting for transfers between devices, exchange(): return lax.ppermute(x, 'mp', [(i, i ^ bit) for i in range(count)])  4.37 us
    pallas_call x1, Pallas kernels, keyval_parts(): pl.pallas_call(keyval_kernel, out_shape=[pltpu.VMEM((rows, depth), BF16)]...  3.82 us
    ppermute x7, waiting for transfers between devices, arrived(): lax.ppermute(outgoing[x], ('group', 'dp'), [(i, i ^ x) for i in range(own...  3.19 us
  transfers between devices with their start and end apart: 13, of which 4 were waited for; matrix products, arithmetic and copies ran while one was open for 0% of the time, Pallas kernels for 29%

profile of v4, /device:TPU:0, one launch (start us, length us, event | category | flops | bytes accessed | tf_op | source)
XLA Modules:
  0.0 66.1 jit_solution(6024180166017072195)
XLA Ops:
  0.0 0.1 pad_add_fusion.where
  0.1 14.8 %merger.1 = (bf16[32,4096]{1,0:T(8,128)(2,1)S(1)}, bf16[32,4096]{1,0:T(8,128)(2,1)S(1)}, bf16[256,8192]{1,0:T(8,128)(2,1)S(1)}) custom-call(s32[2]{0:T(128)S(1)} %pad_add_fusion.where, bf16[128,1280]{1,0:T(8,128)(2,1)} %bitcast.14, f32[1280]{0:T(1024)} %gain_in.1, f32[1280]{0:T(1024)} %bias_in.1, bf16[5120,1280]{1,0:T(8,128)(2,1)} %up.1, f32[1280]{0:T(1024)} %up_bias_in.1, ...), custom_call_target="tpu_custom_call" | custom-call | flops 1090519040 | bytes 34078720 | tf_op jit(solution)/shard_map/merger/pallas_call | solution.py:176
  14.8 0.5 collective-permute-start
  15.4 1.2 %collective-permute-done = bf16[32,4096]{1,0:T(8,128)(2,1)S(1)} collective-permute-done((bf16[32,4096]{1,0:T(8,128)(2,1)S(1)}, bf16[32,4096]{1,0:T(8,128)(2,1)S(1)}, u32[]{:S(2)}, u32[]{:S(2)}) %collective-permute-start) | collective-permute-done | bytes 262176 | tf_op jit(solution)/shard_map/ppermute | solution.py:509
  16.5 0.1 add_convert_fusion.1
  16.6 0.0 copy-start.1
  16.6 0.0 copy-start.5
  16.6 3.0 %collective-permute-start.1 = (bf16[32,4096]{1,0:T(8,128)(2,1)S(1)}, bf16[32,4096]{1,0:T(8,128)(2,1)S(1)}, u32[]{:S(2)}, u32[]{:S(2)}) collective-permute-start(bf16[32,4096]{1,0:T(8,128)(2,1)S(1)} %add_convert_fusion.1), channel_id=1, source_target_pairs={{0,2},{1,3},{2,0},{3,1},{4,6},{5,7},{6,4},{7,5},{8,10},{9,11},{10,... | collective-permute-start | bytes 786440 | tf_op jit(solution)/shard_map/ppermute | solution.py:509
  19.6 4.9 %weights_ahead.1 = (bf16[8192,512]{1,0:T(8,128)(2,1)S(1)}, bf16[8192,512]{1,0:T(8,128)(2,1)S(1)}) custom-call(bf16[8192,2,256]{2,1,0:T(2,128)(2,1)S(1)} %copy-done, bf16[8192,2048]{1,0:T(8,128)(2,1)} %weight.1), custom_call_target="tpu_custom_call" | custom-call | flops 2147483648 | bytes 16777216 | tf_op jit(solution)/shard_map/weights_ahead/pallas_call | solution.py:239
  24.5 0.0 copy-start.2
  24.5 1.7 %collective-permute-done.1 = bf16[32,4096]{1,0:T(8,128)(2,1)S(1)} collective-permute-done((bf16[32,4096]{1,0:T(8,128)(2,1)S(1)}, bf16[32,4096]{1,0:T(8,128)(2,1)S(1)}, u32[]{:S(2)}, u32[]{:S(2)}) %collective-permute-start.1) | collective-permute-done | bytes 262176 | tf_op jit(solution)/shard_map/ppermute | solution.py:509
  26.2 0.1 add_convert_fusion.own
  26.2 0.1 collective-permute-start.2
  26.3 1.5 %collective-permute-done.2.sibling = bf16[32,4096]{1,0:T(8,128)(2,1)S(1)} collective-permute-done((bf16[32,4096]{1,0:T(8,128)(2,1)S(1)}, bf16[32,4096]{1,0:T(8,128)(2,1)S(1)}, u32[]{:S(2)}, u32[]{:S(2)}) %collective-permute-start.2) | collective-permute-done | bytes 262176 | tf_op jit(solution)/shard_map/ppermute | solution.py:509
  27.9 3.8 %keyval.2 = (bf16[288,8192]{1,0:T(8,128)(2,1)S(1)}, bf16[288,128]{1,0:T(8,128)(2,1)S(1)}, bf16[288,128]{1,0:T(8,128)(2,1)S(1)}, bf16[288,128]{1,0:T(8,128)(2,1)S(1)}, bf16[288,128]{1,0:T(8,128)(2,1)S(1)}) custom-call(s32[2]{0:T(128)S(1)} %pad_add_fusion.where, bf16[256,8192]{1,0:T(8,128)(2,1)S(1)} %get-tuple-element.42.text, ...), custom_call_target="tpu_custom_call" | custom-call | flops 2415919104 | bytes 8388608 | tf_op jit(solution)/shard_map/keyval/pallas_call | solution.py:287
  31.7 0.2 collective-permute-start.3
  31.9 1.8 %collective-permute-start.4 = (bf16[288,128]{1,0:T(8,128)(2,1)S(1)}, bf16[288,128]{1,0:T(8,128)(2,1)S(1)}, u32[]{:S(2)}, u32[]{:S(2)}) collective-permute-start(bf16[288,128]{1,0:T(8,128)(2,1)S(1)} %get-tuple-element.54), channel_id=1, source_target_pairs={{0,2},{1,3},{2,0},{3,1},{4,6},{5,7},{6,4},{7,5},{8,10},{9,11},{10,... | collective-permute-start | bytes 221192 | tf_op jit(solution)/shard_map/ppermute | solution.py:509
  33.7 11.2 %query.3 = (bf16[256,1024]{1,0:T(8,128)(2,1)S(1)}, bf16[256,1024]{1,0:T(8,128)(2,1)S(1)}, bf16[32,2048]{1,0:T(8,128)(2,1)S(1)}) custom-call(bf16[288,8192]{1,0:T(8,128)(2,1)S(1)} %get-tuple-element.48.rows_all, bf16[8192,512]{1,0:T(8,128)(2,1)S(1)} %get-tuple-element.49.ready, bf16[8192,2048]{1,0:T(8,128)(2,1)} %weight.1, f32[1,2048]{1,0:T(1,128)S(1)} %bitcast.10), custom_call_target="tpu_custom_call" | custom-call | flops 9663676416 | bytes 33554432 | tf_op jit(solution)/shard_map/query/pallas_call | solution.py:332
  44.9 0.0 collective-permute-done.3.rest_1_
  44.9 0.0 collective-permute-done.4.rest_2_
  44.9 1.0 %slots.1 = (bf16[8,2560]{1,0:T(8,128)(2,1)S(1)}, bf16[8,2560]{1,0:T(8,128)(2,1)S(1)}, bf16[8,2560]{1,0:T(8,128)(2,1)S(1)}, bf16[8,2560]{1,0:T(8,128)(2,1)S(1)}, ...) custom-call(s32[2]{0:T(128)S(1)} %pad_add_fusion.where, ...), custom_call_target="tpu_custom_call" | custom-call | tf_op jit(solution)/shard_map/slots/pallas_call | solution.py:379
  46.0 1.8 %collective-permute-start.6 = (bf16[8,2560]{1,0:T(8,128)(2,1)S(1)}, bf16[8,2560]{1,0:T(8,128)(2,1)S(1)}, u32[]{:S(2)}, u32[]{:S(2)}) collective-permute-start(bf16[8,2560]{1,0:T(8,128)(2,1)S(1)} %get-tuple-element.63), channel_id=1, source_target_pairs={{0,4},{4,0},{8,12},{12,8},{16,20},{20,16},{24,28},{28,24},{1,5},{5... | collective-permute-start | bytes 122888 | tf_op jit(solution)/shard_map/ppermute | solution.py:558
  47.8 2.6 %collective-permute-start.7 = (bf16[8,2560]{1,0:T(8,128)(2,1)S(1)}, bf16[8,2560]{1,0:T(8,128)(2,1)S(1)}, u32[]{:S(2)}, u32[]{:S(2)}) collective-permute-start(bf16[8,2560]{1,0:T(8,128)(2,1)S(1)} %get-tuple-element.64), channel_id=1, source_target_pairs={{0,8},{4,12},{8,0},{12,4},{16,24},{20,28},{24,16},{28,20},{1,9},{5... | collective-permute-start | bytes 122888 | tf_op jit(solution)/shard_map/ppermute | solution.py:558
  50.4 0.1 collective-permute-start.8
  50.4 1.6 %collective-permute-start.9 = (bf16[8,2560]{1,0:T(8,128)(2,1)S(1)}, bf16[8,2560]{1,0:T(8,128)(2,1)S(1)}, u32[]{:S(2)}, u32[]{:S(2)}) collective-permute-start(bf16[8,2560]{1,0:T(8,128)(2,1)S(1)} %get-tuple-element.66), channel_id=1, source_target_pairs={{0,16},{4,20},{8,24},{12,28},{16,0},{20,4},{24,8},{28,12},{1,17},{... | collective-permute-start | bytes 122888 | tf_op jit(solution)/shard_map/ppermute | solution.py:558
  52.1 0.7 collective-permute-start.10
  52.7 4.4 %collective-permute-start.11 = (bf16[8,2560]{1,0:T(8,128)(2,1)S(1)}, bf16[8,2560]{1,0:T(8,128)(2,1)S(1)}, u32[]{:S(2)}, u32[]{:S(2)}) collective-permute-start(bf16[8,2560]{1,0:T(8,128)(2,1)S(1)} %get-tuple-element.68), channel_id=1, source_target_pairs={{0,24},{4,28},{8,16},{12,20},{16,8},{20,12},{24,0},{28,4},{1,25},{... | collective-permute-start | bytes 122888 | tf_op jit(solution)/shard_map/ppermute | solution.py:558
  57.2 0.7 %collective-permute-start.12 = (bf16[8,2560]{1,0:T(8,128)(2,1)S(1)}, bf16[8,2560]{1,0:T(8,128)(2,1)S(1)}, u32[]{:S(2)}, u32[]{:S(2)}) collective-permute-start(bf16[8,2560]{1,0:T(8,128)(2,1)S(1)} %get-tuple-element.69), channel_id=1, source_target_pairs={{0,28},{4,24},{8,20},{12,16},{16,12},{20,8},{24,4},{28,0},{1,29},{... | collective-permute-start | bytes 122888 | tf_op jit(solution)/shard_map/ppermute | solution.py:558
  57.9 2.8 %attention_late.1 = (bf16[128,2048]{1,0:T(8,128)(2,1)S(1)}, bf16[256,512]{1,0:T(8,128)(2,1)S(1)}, bf16[512,512]{1,0:T(8,128)(2,1)S(1)}, bf16[64,64]{1,0:T(8,128)(2,1)S(1)}) custom-call(s32[2]{0:T(128)S(1)} %pad_add_fusion.where, s32[1,256]{1,0:T(1,128)S(1)} %bitcast.12, s32[1,256]{1,0:T(1,128)S(1)} %copy-done.4, ...), custom_call_target="tpu_custom_call" | custom-call | flops 134217728 | bytes 2097152 | tf_op jit(solution)/shard_map/attention_late/pallas_call | solution.py:477
  60.7 0.0 collective-permute-done.8.rest_3_
  60.7 3.2 %collective-permute-done.12.rest_7_ = bf16[8,2560]{1,0:T(8,128)(2,1)S(1)} collective-permute-done((bf16[8,2560]{1,0:T(8,128)(2,1)S(1)}, bf16[8,2560]{1,0:T(8,128)(2,1)S(1)}, u32[]{:S(2)}, u32[]{:S(2)}) %collective-permute-start.12) | collective-permute-done | bytes 40992 | tf_op jit(solution)/shard_map/ppermute | solution.py:558
  63.9 2.3 %attention_early.1 = bf16[256,2048]{1,0:T(8,128)(2,1)} custom-call(s32[1,256]{1,0:T(1,128)S(1)} %copy-done.4, bf16[256,1024]{1,0:T(8,128)(2,1)S(1)} %get-tuple-element.57.first_half, bf16[256,1024]{1,0:T(8,128)(2,1)S(1)} %get-tuple-element.59.second_half, bf16[256,512]{1,0:T(8,128)(2,1)S(1)} %get-tuple-element.60.keyval, ...), custom_call_target="tpu_custom_call" | custom-call | flops 134217728 | bytes 2097152 | tf_op jit(solution)/shard_map/attention_early/pallas_call | solution.py:491
  (16 shorter events, 0.0 us)
Async XLA Ops:
  0.1 19.5 %copy-start = (bf16[8192,2,256]{2,1,0:T(2,128)(2,1)S(1)}, bf16[8192,2,256]{2,1,0:T(2,128)(2,1)}, u32[]{:S(2)}) copy-start(bf16[8192,2,256]{2,1,0:T(2,128)(2,1)} %keyval.1) | copy-start | bytes 25165828
  14.8 1.7 %collective-permute-start = (bf16[32,4096]{1,0:T(8,128)(2,1)S(1)}, bf16[32,4096]{1,0:T(8,128)(2,1)S(1)}, u32[]{:S(2)}, u32[]{:S(2)}) collective-permute-start(bf16[32,4096]{1,0:T(8,128)(2,1)S(1)} %get-tuple-element.44), channel_id=1, source_target_pairs={{0,1},{1,0},{2,3},{3,2},{4,5},{5,4},{6,7},{7,6},{8,9},{9,8},{10,11... | collective-permute-start | bytes 786440 | tf_op jit(solution)/shard_map/ppermute | solution.py:509
  16.6 11.3 %copy-start.1 = (f32[8192]{0:T(1024)S(1)}, f32[8192]{0:T(1024)}, u32[]{:S(2)}) copy-start(f32[8192]{0:T(1024)} %param.25) | copy-start | bytes 98308
  16.6 11.2 %copy-start.5 = (f32[2,256]{1,0:T(2,128)S(1)}, f32[2,256]{1,0:T(2,128)}, u32[]{:S(2)}) copy-start(f32[2,256]{1,0:T(2,128)} %bias.1) | copy-start | bytes 6148
  16.6 9.6 %collective-permute-start.1 = (bf16[32,4096]{1,0:T(8,128)(2,1)S(1)}, bf16[32,4096]{1,0:T(8,128)(2,1)S(1)}, u32[]{:S(2)}, u32[]{:S(2)}) collective-permute-start(bf16[32,4096]{1,0:T(8,128)(2,1)S(1)} %add_convert_fusion.1), channel_id=1, source_target_pairs={{0,2},{1,3},{2,0},{3,1},{4,6},{5,7},{6,4},{7,5},{8,10},{9,11},{10,... | collective-permute-start | bytes 786440 | tf_op jit(solution)/shard_map/ppermute | solution.py:509
  24.5 9.2 %copy-start.2 = (f32[2048]{0:T(1024)S(1)}, f32[2048]{0:T(1024)}, u32[]{:S(2)}) copy-start(f32[2048]{0:T(1024)} %param.27) | copy-start | bytes 24580
  26.2 1.6 %collective-permute-start.2 = (bf16[32,4096]{1,0:T(8,128)(2,1)S(1)}, bf16[32,4096]{1,0:T(8,128)(2,1)S(1)}, u32[]{:S(2)}, u32[]{:S(2)}) collective-permute-start(bf16[32,4096]{1,0:T(8,128)(2,1)S(1)} %add_convert_fusion.own), channel_id=1, source_target_pairs={{0,1},{1,0},{2,3},{3,2},{4,5},{5,4},{6,7},{7,6},{8,9},{9,8},{10,11... | collective-permute-start | bytes 786440 | tf_op jit(solution)/shard_map/ppermute | solution.py:509
  31.7 13.2 %collective-permute-start.3 = (bf16[288,128]{1,0:T(8,128)(2,1)S(1)}, bf16[288,128]{1,0:T(8,128)(2,1)S(1)}, u32[]{:S(2)}, u32[]{:S(2)}) collective-permute-start(bf16[288,128]{1,0:T(8,128)(2,1)S(1)} %get-tuple-element.53), channel_id=1, source_target_pairs={{0,1},{1,0},{2,3},{3,2},{4,5},{5,4},{6,7},{7,6},{8,9},{9,8},{10,11... | collective-permute-start | bytes 221192 | tf_op jit(solution)/shard_map/ppermute | solution.py:509
  31.9 13.0 %collective-permute-start.4 = (bf16[288,128]{1,0:T(8,128)(2,1)S(1)}, bf16[288,128]{1,0:T(8,128)(2,1)S(1)}, u32[]{:S(2)}, u32[]{:S(2)}) collective-permute-start(bf16[288,128]{1,0:T(8,128)(2,1)S(1)} %get-tuple-element.54), channel_id=1, source_target_pairs={{0,2},{1,3},{2,0},{3,1},{4,6},{5,7},{6,4},{7,5},{8,10},{9,11},{10,... | collective-permute-start | bytes 221192 | tf_op jit(solution)/shard_map/ppermute | solution.py:509
  33.7 11.3 %collective-permute-start.5 = (bf16[288,128]{1,0:T(8,128)(2,1)S(1)}, bf16[288,128]{1,0:T(8,128)(2,1)S(1)}, u32[]{:S(2)}, u32[]{:S(2)}) collective-permute-start(bf16[288,128]{1,0:T(8,128)(2,1)S(1)} %get-tuple-element.55), channel_id=1, source_target_pairs={{0,3},{1,2},{2,1},{3,0},{4,7},{5,6},{6,5},{7,4},{8,11},{9,10},{10,... | collective-permute-start | bytes 221192 | tf_op jit(solution)/shard_map/ppermute | solution.py:509
  33.7 11.3 %copy-start.3 = (s32[256,1]{0,1:T(1,128)S(1)}, s32[256,1]{0,1:T(1,128)}, u32[]{:S(2)}) copy-start(s32[256,1]{0,1:T(1,128)} %param.22) | copy-start | bytes 3076
  33.7 24.2 %copy-start.4 = (s32[1,256]{1,0:T(1,128)S(1)}, s32[1,256]{1,0:T(1,128)}, u32[]{:S(2)}) copy-start(s32[1,256]{1,0:T(1,128)} %doc_row.3) | copy-start | bytes 3076
  46.0 6.8 %collective-permute-start.6 = (bf16[8,2560]{1,0:T(8,128)(2,1)S(1)}, bf16[8,2560]{1,0:T(8,128)(2,1)S(1)}, u32[]{:S(2)}, u32[]{:S(2)}) collective-permute-start(bf16[8,2560]{1,0:T(8,128)(2,1)S(1)} %get-tuple-element.63), channel_id=1, source_target_pairs={{0,4},{4,0},{8,12},{12,8},{16,20},{20,16},{24,28},{28,24},{1,5},{5... | collective-permute-start | bytes 122888 | tf_op jit(solution)/shard_map/ppermute | solution.py:558
  47.8 9.4 %collective-permute-start.7 = (bf16[8,2560]{1,0:T(8,128)(2,1)S(1)}, bf16[8,2560]{1,0:T(8,128)(2,1)S(1)}, u32[]{:S(2)}, u32[]{:S(2)}) collective-permute-start(bf16[8,2560]{1,0:T(8,128)(2,1)S(1)} %get-tuple-element.64), channel_id=1, source_target_pairs={{0,8},{4,12},{8,0},{12,4},{16,24},{20,28},{24,16},{28,20},{1,9},{5... | collective-permute-start | bytes 122888 | tf_op jit(solution)/shard_map/ppermute | solution.py:558
  50.4 10.3 %collective-permute-start.8 = (bf16[8,2560]{1,0:T(8,128)(2,1)S(1)}, bf16[8,2560]{1,0:T(8,128)(2,1)S(1)}, u32[]{:S(2)}, u32[]{:S(2)}) collective-permute-start(bf16[8,2560]{1,0:T(8,128)(2,1)S(1)} %get-tuple-element.65), channel_id=1, source_target_pairs={{0,12},{4,8},{8,4},{12,0},{16,28},{20,24},{24,20},{28,16},{1,13},{... | collective-permute-start | bytes 122888 | tf_op jit(solution)/shard_map/ppermute | solution.py:558
  50.4 10.2 %collective-permute-start.9 = (bf16[8,2560]{1,0:T(8,128)(2,1)S(1)}, bf16[8,2560]{1,0:T(8,128)(2,1)S(1)}, u32[]{:S(2)}, u32[]{:S(2)}) collective-permute-start(bf16[8,2560]{1,0:T(8,128)(2,1)S(1)} %get-tuple-element.66), channel_id=1, source_target_pairs={{0,16},{4,20},{8,24},{12,28},{16,0},{20,4},{24,8},{28,12},{1,17},{... | collective-permute-start | bytes 122888 | tf_op jit(solution)/shard_map/ppermute | solution.py:558
  52.1 8.6 %collective-permute-start.10 = (bf16[8,2560]{1,0:T(8,128)(2,1)S(1)}, bf16[8,2560]{1,0:T(8,128)(2,1)S(1)}, u32[]{:S(2)}, u32[]{:S(2)}) collective-permute-start(bf16[8,2560]{1,0:T(8,128)(2,1)S(1)} %get-tuple-element.67), channel_id=1, source_target_pairs={{0,20},{4,16},{8,28},{12,24},{16,4},{20,0},{24,12},{28,8},{1,21},{... | collective-permute-start | bytes 122888 | tf_op jit(solution)/shard_map/ppermute | solution.py:558
  52.7 7.9 %collective-permute-start.11 = (bf16[8,2560]{1,0:T(8,128)(2,1)S(1)}, bf16[8,2560]{1,0:T(8,128)(2,1)S(1)}, u32[]{:S(2)}, u32[]{:S(2)}) collective-permute-start(bf16[8,2560]{1,0:T(8,128)(2,1)S(1)} %get-tuple-element.68), channel_id=1, source_target_pairs={{0,24},{4,28},{8,16},{12,20},{16,8},{20,12},{24,0},{28,4},{1,25},{... | collective-permute-start | bytes 122888 | tf_op jit(solution)/shard_map/ppermute | solution.py:558
  57.2 6.7 %collective-permute-start.12 = (bf16[8,2560]{1,0:T(8,128)(2,1)S(1)}, bf16[8,2560]{1,0:T(8,128)(2,1)S(1)}, u32[]{:S(2)}, u32[]{:S(2)}) collective-permute-start(bf16[8,2560]{1,0:T(8,128)(2,1)S(1)} %get-tuple-element.69), channel_id=1, source_target_pairs={{0,28},{4,24},{8,20},{12,16},{16,12},{20,8},{24,4},{28,0},{1,29},{... | collective-permute-start | bytes 122888 | tf_op jit(solution)/shard_map/ppermute | solution.py:558

commit v5 on v4

--- a/solution.py
+++ b/solution.py
@@ -444,14 +444,15 @@
         pass
 
 
-def early_kernel(early, doc_row, first_half, second_half, keyval, join, place, *rest):
+def early_kernel(early, order, doc_row, first_half, second_half, keyval, join, place, *rest):
     arrived = rest[:-7]
     late, out, first, second, kv_all, result, sem = rest[-7:]
     slots = place.shape[0]
     copies = [pltpu.make_async_copy(late, out.at[pl.ds(early, late.shape[0])], sem.at[0])]
     copies[0].start()
     half = first_half.shape[1]
-    together = jnp.concatenate([rows[...].astype(F32) for rows in arrived], axis=0).astype(BF16)
+    in_place = [arrived[order.index(x)][...].astype(F32) for x in range(len(order))]
+    together = jnp.concatenate(in_place, axis=0).astype(BF16)
     placed = dot(place[...], together).astype(BF16)
     is_image = jnp.sum(place[...].astype(F32), axis=1, keepdims=True) > 0.5
     image_keyval = dot(placed[:, 2 * half :], join[...]).astype(BF16)
@@ -470,7 +471,7 @@
         copy.wait()
 
 
-def attention(where, owner_row, documents, halves, parts, arrived, owners, slots, columns):
+def attention(where, owner_row, documents, halves, parts, arrived, order, owners, slots, columns):
     seq = documents.shape[1]
     full = 2 * (KV_HEADS // len(parts)) * HEAD_DIM
     early = min(seq, -(-slots // DOC_MAX) * DOC_MAX + DOC_MAX)
@@ -489,7 +490,7 @@
         name="attention_late",
     )(where, owner_row, documents, *halves, *parts)
     return pl.pallas_call(
-        functools.partial(early_kernel, early),
+        functools.partial(early_kernel, early, order),
         out_shape=jax.ShapeDtypeStruct((seq, columns), BF16),
         in_specs=[VMEM] * (7 + owners),
         out_specs=HBM,
@@ -533,6 +534,11 @@
     rows = row_owner.shape[0] // owners
     capacity = max(2, 2 * rows // owners)
     owner_row = row_owner.reshape(1, -1)
+    groups, line = lax.axis_size("group"), lax.axis_size("dp")
+
+    def far(x):
+        return max(abs(i % line - (i ^ x) % line) + (x >= line) for i in range(groups * line))
+
 
     send, keep, text = merger(
         where, patch_rows[0], ln_gain, ln_bias, merge_up, merge_up_bias, merge_down, merge_down_bias,
@@ -553,15 +559,15 @@
     *halves, image_queries = query_rows(rows_all, text.shape[0], ready, w_query, query_bias[None, :])
     outgoing = slots_of(where, owner_row, image_queries, parts, owners, capacity)
 
+    order = sorted(range(1, owners), key=far, reverse=True)
+
     def arrived(done):
-        rows = [
-            lax.ppermute(outgoing[x], ("group", "dp"), [(i, i ^ x) for i in range(owners)]) for x in range(1, owners)
-        ]
-        return lax.optimization_barrier((outgoing[0], *rows, done))[:-1]
+        rows = [lax.ppermute(outgoing[x], ("group", "dp"), [(i, i ^ x) for i in range(owners)]) for x in order]
+        return lax.optimization_barrier((*rows, outgoing[0], done))[:-1]
 
     halves = [after(half, outgoing[0]) for half in halves]
     return attention(
-        where, owner_row, doc_ids, halves, parts, arrived, owners, owners * capacity, columns
+        where, owner_row, doc_ids, halves, parts, arrived, [*order, 0], owners, owners * capacity, columns
     )[None]
 
 

time: 66.3 us -> 63.2 us (0.953)
  waiting for transfers between devices: 7.56 us -> 5.14 us
    ppermute x7, waiting for transfers between devices: 3.19 us -> 0.77 us  [arrived(): lax.ppermute(outgoing[x], ('group', 'dp'), [(i, i ^ x) for i in range(own...]
  transfers between devices with their start and end apart: 13 -> 13, of which waited for: 4 -> 4; matrix products, arithmetic and copies ran while one was open for 0% -> 0% of each run, Pallas kernels for 29% -> 30%
where the time goes in v5:
time: 63.2 us; the launch traced here: 63.1 us
  Pallas kernels  40.8 us (65%)
  starting transfers between devices  16.8 us (27%)
  waiting for transfers between devices  5.14 us (8%)
    pallas_call x1, Pallas kernels, merger(): pl.pallas_call(merger_kernel, out_shape=[jax.ShapeDtypeStruct((rows, colu...  14.8 us
    ppermute x7, starting transfers between devices, arrived(): lax.ppermute(outgoing[x], ('group', 'dp'), [(i, i ^ x) for i in range(own...  11.3 us
    pallas_call x1, Pallas kernels, query_rows(): pl.pallas_call(query_kernel, out_shape=[jax.ShapeDtypeStruct((texts, colu...  11.2 us
    ppermute x6, starting transfers between devices, exchange(): return lax.ppermute(x, 'mp', [(i, i ^ bit) for i in range(count)])  5.53 us
    pallas_call x1, Pallas kernels, weights_ahead(): pl.pallas_call(weights_kernel, out_shape=[pltpu.VMEM((depth, 2 * columns)...  4.91 us
    ppermute x6, waiting for transfers between devices, exchange(): return lax.ppermute(x, 'mp', [(i, i ^ bit) for i in range(count)])  4.37 us
    pallas_call x1, Pallas kernels, keyval_parts(): pl.pallas_call(keyval_kernel, out_shape=[pltpu.VMEM((rows, depth), BF16)]...  3.82 us
    pallas_call x1, Pallas kernels, attention(): pl.pallas_call(functools.partial(late_kernel, early, owners), out_shape=[...  2.78 us
  transfers between devices with their start and end apart: 13, of which 4 were waited for; matrix products, arithmetic and copies ran while one was open for 0% of the time, Pallas kernels for 30%

profile of v5, /device:TPU:0, one launch (start us, length us, event | category | flops | bytes accessed | tf_op | source)
XLA Modules:
  0.0 63.1 jit_solution(8706083568548529049)
XLA Ops:
  0.0 0.1 pad_add_fusion.where
  0.1 14.8 %merger.1 = (bf16[32,4096]{1,0:T(8,128)(2,1)S(1)}, bf16[32,4096]{1,0:T(8,128)(2,1)S(1)}, bf16[256,8192]{1,0:T(8,128)(2,1)S(1)}) custom-call(s32[2]{0:T(128)S(1)} %pad_add_fusion.where, bf16[128,1280]{1,0:T(8,128)(2,1)} %bitcast.14, f32[1280]{0:T(1024)} %gain_in.1, f32[1280]{0:T(1024)} %bias_in.1, bf16[5120,1280]{1,0:T(8,128)(2,1)} %up.1, f32[1280]{0:T(1024)} %up_bias_in.1, ...), custom_call_target="tpu_custom_call" | custom-call | flops 1090519040 | bytes 34078720 | tf_op jit(solution)/shard_map/merger/pallas_call | solution.py:176
  14.8 0.5 collective-permute-start
  15.4 1.2 %collective-permute-done = bf16[32,4096]{1,0:T(8,128)(2,1)S(1)} collective-permute-done((bf16[32,4096]{1,0:T(8,128)(2,1)S(1)}, bf16[32,4096]{1,0:T(8,128)(2,1)S(1)}, u32[]{:S(2)}, u32[]{:S(2)}) %collective-permute-start) | collective-permute-done | bytes 262176 | tf_op jit(solution)/shard_map/ppermute | solution.py:510
  16.5 0.1 add_convert_fusion.1
  16.6 0.0 copy-start.1
  16.6 0.0 copy-start.5
  16.6 3.0 %collective-permute-start.1 = (bf16[32,4096]{1,0:T(8,128)(2,1)S(1)}, bf16[32,4096]{1,0:T(8,128)(2,1)S(1)}, u32[]{:S(2)}, u32[]{:S(2)}) collective-permute-start(bf16[32,4096]{1,0:T(8,128)(2,1)S(1)} %add_convert_fusion.1), channel_id=1, source_target_pairs={{0,2},{1,3},{2,0},{3,1},{4,6},{5,7},{6,4},{7,5},{8,10},{9,11},{10,... | collective-permute-start | bytes 786440 | tf_op jit(solution)/shard_map/ppermute | solution.py:510
  19.6 4.9 %weights_ahead.1 = (bf16[8192,512]{1,0:T(8,128)(2,1)S(1)}, bf16[8192,512]{1,0:T(8,128)(2,1)S(1)}) custom-call(bf16[8192,2,256]{2,1,0:T(2,128)(2,1)S(1)} %copy-done, bf16[8192,2048]{1,0:T(8,128)(2,1)} %weight.1), custom_call_target="tpu_custom_call" | custom-call | flops 2147483648 | bytes 16777216 | tf_op jit(solution)/shard_map/weights_ahead/pallas_call | solution.py:239
  24.5 0.0 copy-start.2
  24.5 1.7 %collective-permute-done.1 = bf16[32,4096]{1,0:T(8,128)(2,1)S(1)} collective-permute-done((bf16[32,4096]{1,0:T(8,128)(2,1)S(1)}, bf16[32,4096]{1,0:T(8,128)(2,1)S(1)}, u32[]{:S(2)}, u32[]{:S(2)}) %collective-permute-start.1) | collective-permute-done | bytes 262176 | tf_op jit(solution)/shard_map/ppermute | solution.py:510
  26.2 0.1 add_convert_fusion.own
  26.2 0.1 collective-permute-start.2
  26.3 1.5 %collective-permute-done.2.sibling = bf16[32,4096]{1,0:T(8,128)(2,1)S(1)} collective-permute-done((bf16[32,4096]{1,0:T(8,128)(2,1)S(1)}, bf16[32,4096]{1,0:T(8,128)(2,1)S(1)}, u32[]{:S(2)}, u32[]{:S(2)}) %collective-permute-start.2) | collective-permute-done | bytes 262176 | tf_op jit(solution)/shard_map/ppermute | solution.py:510
  27.9 3.8 %keyval.2 = (bf16[288,8192]{1,0:T(8,128)(2,1)S(1)}, bf16[288,128]{1,0:T(8,128)(2,1)S(1)}, bf16[288,128]{1,0:T(8,128)(2,1)S(1)}, bf16[288,128]{1,0:T(8,128)(2,1)S(1)}, bf16[288,128]{1,0:T(8,128)(2,1)S(1)}) custom-call(s32[2]{0:T(128)S(1)} %pad_add_fusion.where, bf16[256,8192]{1,0:T(8,128)(2,1)S(1)} %get-tuple-element.42.text, ...), custom_call_target="tpu_custom_call" | custom-call | flops 2415919104 | bytes 8388608 | tf_op jit(solution)/shard_map/keyval/pallas_call | solution.py:287
  31.7 0.2 collective-permute-start.3
  31.9 1.8 %collective-permute-start.4 = (bf16[288,128]{1,0:T(8,128)(2,1)S(1)}, bf16[288,128]{1,0:T(8,128)(2,1)S(1)}, u32[]{:S(2)}, u32[]{:S(2)}) collective-permute-start(bf16[288,128]{1,0:T(8,128)(2,1)S(1)} %get-tuple-element.54), channel_id=1, source_target_pairs={{0,2},{1,3},{2,0},{3,1},{4,6},{5,7},{6,4},{7,5},{8,10},{9,11},{10,... | collective-permute-start | bytes 221192 | tf_op jit(solution)/shard_map/ppermute | solution.py:510
  33.7 11.2 %query.3 = (bf16[256,1024]{1,0:T(8,128)(2,1)S(1)}, bf16[256,1024]{1,0:T(8,128)(2,1)S(1)}, bf16[32,2048]{1,0:T(8,128)(2,1)S(1)}) custom-call(bf16[288,8192]{1,0:T(8,128)(2,1)S(1)} %get-tuple-element.48.rows_all, bf16[8192,512]{1,0:T(8,128)(2,1)S(1)} %get-tuple-element.49.ready, bf16[8192,2048]{1,0:T(8,128)(2,1)} %weight.1, f32[1,2048]{1,0:T(1,128)S(1)} %bitcast.10), custom_call_target="tpu_custom_call" | custom-call | flops 9663676416 | bytes 33554432 | tf_op jit(solution)/shard_map/query/pallas_call | solution.py:332
  44.9 0.0 collective-permute-done.3.rest_1_
  44.9 0.0 collective-permute-done.4.rest_2_
  44.9 1.0 %slots.1 = (bf16[8,2560]{1,0:T(8,128)(2,1)S(1)}, bf16[8,2560]{1,0:T(8,128)(2,1)S(1)}, bf16[8,2560]{1,0:T(8,128)(2,1)S(1)}, bf16[8,2560]{1,0:T(8,128)(2,1)S(1)}, ...) custom-call(s32[2]{0:T(128)S(1)} %pad_add_fusion.where, ...), custom_call_target="tpu_custom_call" | custom-call | tf_op jit(solution)/shard_map/slots/pallas_call | solution.py:379
  46.0 4.8 %collective-permute-start.6 = (bf16[8,2560]{1,0:T(8,128)(2,1)S(1)}, bf16[8,2560]{1,0:T(8,128)(2,1)S(1)}, u32[]{:S(2)}, u32[]{:S(2)}) collective-permute-start(bf16[8,2560]{1,0:T(8,128)(2,1)S(1)} %get-tuple-element.63), channel_id=1, source_target_pairs={{0,28},{4,24},{8,20},{12,16},{16,12},{20,8},{24,4},{28,0},{1,29},{... | collective-permute-start | bytes 122888 | tf_op jit(solution)/shard_map/ppermute | solution.py:565
  50.7 0.2 collective-permute-start.7
  51.0 0.8 %collective-permute-start.8 = (bf16[8,2560]{1,0:T(8,128)(2,1)S(1)}, bf16[8,2560]{1,0:T(8,128)(2,1)S(1)}, u32[]{:S(2)}, u32[]{:S(2)}) collective-permute-start(bf16[8,2560]{1,0:T(8,128)(2,1)S(1)} %get-tuple-element.65), channel_id=1, source_target_pairs={{0,24},{4,28},{8,16},{12,20},{16,8},{20,12},{24,0},{28,4},{1,25},{... | collective-permute-start | bytes 122888 | tf_op jit(solution)/shard_map/ppermute | solution.py:565
  51.7 2.0 %collective-permute-start.9 = (bf16[8,2560]{1,0:T(8,128)(2,1)S(1)}, bf16[8,2560]{1,0:T(8,128)(2,1)S(1)}, u32[]{:S(2)}, u32[]{:S(2)}) collective-permute-start(bf16[8,2560]{1,0:T(8,128)(2,1)S(1)} %get-tuple-element.66), channel_id=1, source_target_pairs={{0,8},{4,12},{8,0},{12,4},{16,24},{20,28},{24,16},{28,20},{1,9},{5... | collective-permute-start | bytes 122888 | tf_op jit(solution)/shard_map/ppermute | solution.py:565
  53.7 2.3 %collective-permute-start.10 = (bf16[8,2560]{1,0:T(8,128)(2,1)S(1)}, bf16[8,2560]{1,0:T(8,128)(2,1)S(1)}, u32[]{:S(2)}, u32[]{:S(2)}) collective-permute-start(bf16[8,2560]{1,0:T(8,128)(2,1)S(1)} %get-tuple-element.67), channel_id=1, source_target_pairs={{0,20},{4,16},{8,28},{12,24},{16,4},{20,0},{24,12},{28,8},{1,21},{... | collective-permute-start | bytes 122888 | tf_op jit(solution)/shard_map/ppermute | solution.py:565
  56.0 0.0 collective-permute-done.6.rest_0_
  56.0 0.8 %collective-permute-start.11 = (bf16[8,2560]{1,0:T(8,128)(2,1)S(1)}, bf16[8,2560]{1,0:T(8,128)(2,1)S(1)}, u32[]{:S(2)}, u32[]{:S(2)}) collective-permute-start(bf16[8,2560]{1,0:T(8,128)(2,1)S(1)} %get-tuple-element.68), channel_id=1, source_target_pairs={{0,4},{4,0},{8,12},{12,8},{16,20},{20,16},{24,28},{28,24},{1,5},{5... | collective-permute-start | bytes 122888 | tf_op jit(solution)/shard_map/ppermute | solution.py:565
  56.8 0.4 collective-permute-start.12
  57.2 2.8 %attention_late.1 = (bf16[128,2048]{1,0:T(8,128)(2,1)S(1)}, bf16[256,512]{1,0:T(8,128)(2,1)S(1)}, bf16[512,512]{1,0:T(8,128)(2,1)S(1)}, bf16[64,64]{1,0:T(8,128)(2,1)S(1)}) custom-call(s32[2]{0:T(128)S(1)} %pad_add_fusion.where, s32[1,256]{1,0:T(1,128)S(1)} %bitcast.12, s32[1,256]{1,0:T(1,128)S(1)} %copy-done.4, ...), custom_call_target="tpu_custom_call" | custom-call | flops 134217728 | bytes 2097152 | tf_op jit(solution)/shard_map/attention_late/pallas_call | solution.py:478
  60.1 0.8 %collective-permute-done.12.rest_6_ = bf16[8,2560]{1,0:T(8,128)(2,1)S(1)} collective-permute-done((bf16[8,2560]{1,0:T(8,128)(2,1)S(1)}, bf16[8,2560]{1,0:T(8,128)(2,1)S(1)}, u32[]{:S(2)}, u32[]{:S(2)}) %collective-permute-start.12) | collective-permute-done | bytes 40992 | tf_op jit(solution)/shard_map/ppermute | solution.py:565
  60.8 2.3 %attention_early.1 = bf16[256,2048]{1,0:T(8,128)(2,1)} custom-call(s32[1,256]{1,0:T(1,128)S(1)} %copy-done.4, bf16[256,1024]{1,0:T(8,128)(2,1)S(1)} %get-tuple-element.57.first_half, bf16[256,1024]{1,0:T(8,128)(2,1)S(1)} %get-tuple-element.59.second_half, bf16[256,512]{1,0:T(8,128)(2,1)S(1)} %get-tuple-element.60.keyval, ...), custom_call_target="tpu_custom_call" | custom-call | flops 134217728 | bytes 2097152 | tf_op jit(solution)/shard_map/attention_early/pallas_call | solution.py:492
  (16 shorter events, 0.0 us)
Async XLA Ops:
  0.1 19.5 %copy-start = (bf16[8192,2,256]{2,1,0:T(2,128)(2,1)S(1)}, bf16[8192,2,256]{2,1,0:T(2,128)(2,1)}, u32[]{:S(2)}) copy-start(bf16[8192,2,256]{2,1,0:T(2,128)(2,1)} %keyval.1) | copy-start | bytes 25165828
  14.8 1.7 %collective-permute-start = (bf16[32,4096]{1,0:T(8,128)(2,1)S(1)}, bf16[32,4096]{1,0:T(8,128)(2,1)S(1)}, u32[]{:S(2)}, u32[]{:S(2)}) collective-permute-start(bf16[32,4096]{1,0:T(8,128)(2,1)S(1)} %get-tuple-element.44), channel_id=1, source_target_pairs={{0,1},{1,0},{2,3},{3,2},{4,5},{5,4},{6,7},{7,6},{8,9},{9,8},{10,11... | collective-permute-start | bytes 786440 | tf_op jit(solution)/shard_map/ppermute | solution.py:510
  16.6 11.3 %copy-start.1 = (f32[8192]{0:T(1024)S(1)}, f32[8192]{0:T(1024)}, u32[]{:S(2)}) copy-start(f32[8192]{0:T(1024)} %param.25) | copy-start | bytes 98308
  16.6 11.2 %copy-start.5 = (f32[2,256]{1,0:T(2,128)S(1)}, f32[2,256]{1,0:T(2,128)}, u32[]{:S(2)}) copy-start(f32[2,256]{1,0:T(2,128)} %bias.1) | copy-start | bytes 6148
  16.6 9.6 %collective-permute-start.1 = (bf16[32,4096]{1,0:T(8,128)(2,1)S(1)}, bf16[32,4096]{1,0:T(8,128)(2,1)S(1)}, u32[]{:S(2)}, u32[]{:S(2)}) collective-permute-start(bf16[32,4096]{1,0:T(8,128)(2,1)S(1)} %add_convert_fusion.1), channel_id=1, source_target_pairs={{0,2},{1,3},{2,0},{3,1},{4,6},{5,7},{6,4},{7,5},{8,10},{9,11},{10,... | collective-permute-start | bytes 786440 | tf_op jit(solution)/shard_map/ppermute | solution.py:510
  24.5 9.2 %copy-start.2 = (f32[2048]{0:T(1024)S(1)}, f32[2048]{0:T(1024)}, u32[]{:S(2)}) copy-start(f32[2048]{0:T(1024)} %param.27) | copy-start | bytes 24580
  26.2 1.6 %collective-permute-start.2 = (bf16[32,4096]{1,0:T(8,128)(2,1)S(1)}, bf16[32,4096]{1,0:T(8,128)(2,1)S(1)}, u32[]{:S(2)}, u32[]{:S(2)}) collective-permute-start(bf16[32,4096]{1,0:T(8,128)(2,1)S(1)} %add_convert_fusion.own), channel_id=1, source_target_pairs={{0,1},{1,0},{2,3},{3,2},{4,5},{5,4},{6,7},{7,6},{8,9},{9,8},{10,11... | collective-permute-start | bytes 786440 | tf_op jit(solution)/shard_map/ppermute | solution.py:510
  31.7 13.2 %collective-permute-start.3 = (bf16[288,128]{1,0:T(8,128)(2,1)S(1)}, bf16[288,128]{1,0:T(8,128)(2,1)S(1)}, u32[]{:S(2)}, u32[]{:S(2)}) collective-permute-start(bf16[288,128]{1,0:T(8,128)(2,1)S(1)} %get-tuple-element.53), channel_id=1, source_target_pairs={{0,1},{1,0},{2,3},{3,2},{4,5},{5,4},{6,7},{7,6},{8,9},{9,8},{10,11... | collective-permute-start | bytes 221192 | tf_op jit(solution)/shard_map/ppermute | solution.py:510
  31.9 13.0 %collective-permute-start.4 = (bf16[288,128]{1,0:T(8,128)(2,1)S(1)}, bf16[288,128]{1,0:T(8,128)(2,1)S(1)}, u32[]{:S(2)}, u32[]{:S(2)}) collective-permute-start(bf16[288,128]{1,0:T(8,128)(2,1)S(1)} %get-tuple-element.54), channel_id=1, source_target_pairs={{0,2},{1,3},{2,0},{3,1},{4,6},{5,7},{6,4},{7,5},{8,10},{9,11},{10,... | collective-permute-start | bytes 221192 | tf_op jit(solution)/shard_map/ppermute | solution.py:510
  33.7 11.3 %collective-permute-start.5 = (bf16[288,128]{1,0:T(8,128)(2,1)S(1)}, bf16[288,128]{1,0:T(8,128)(2,1)S(1)}, u32[]{:S(2)}, u32[]{:S(2)}) collective-permute-start(bf16[288,128]{1,0:T(8,128)(2,1)S(1)} %get-tuple-element.55), channel_id=1, source_target_pairs={{0,3},{1,2},{2,1},{3,0},{4,7},{5,6},{6,5},{7,4},{8,11},{9,10},{10,... | collective-permute-start | bytes 221192 | tf_op jit(solution)/shard_map/ppermute | solution.py:510
  33.7 11.3 %copy-start.3 = (s32[256,1]{0,1:T(1,128)S(1)}, s32[256,1]{0,1:T(1,128)}, u32[]{:S(2)}) copy-start(s32[256,1]{0,1:T(1,128)} %param.22) | copy-start | bytes 3076
  33.7 23.6 %copy-start.4 = (s32[1,256]{1,0:T(1,128)S(1)}, s32[1,256]{1,0:T(1,128)}, u32[]{:S(2)}) copy-start(s32[1,256]{1,0:T(1,128)} %doc_row.3) | copy-start | bytes 3076
  46.0 10.1 %collective-permute-start.6 = (bf16[8,2560]{1,0:T(8,128)(2,1)S(1)}, bf16[8,2560]{1,0:T(8,128)(2,1)S(1)}, u32[]{:S(2)}, u32[]{:S(2)}) collective-permute-start(bf16[8,2560]{1,0:T(8,128)(2,1)S(1)} %get-tuple-element.63), channel_id=1, source_target_pairs={{0,28},{4,24},{8,20},{12,16},{16,12},{20,8},{24,4},{28,0},{1,29},{... | collective-permute-start | bytes 122888 | tf_op jit(solution)/shard_map/ppermute | solution.py:565
  50.7 6.1 %collective-permute-start.7 = (bf16[8,2560]{1,0:T(8,128)(2,1)S(1)}, bf16[8,2560]{1,0:T(8,128)(2,1)S(1)}, u32[]{:S(2)}, u32[]{:S(2)}) collective-permute-start(bf16[8,2560]{1,0:T(8,128)(2,1)S(1)} %get-tuple-element.64), channel_id=1, source_target_pairs={{0,12},{4,8},{8,4},{12,0},{16,28},{20,24},{24,20},{28,16},{1,13},{... | collective-permute-start | bytes 122888 | tf_op jit(solution)/shard_map/ppermute | solution.py:565
  51.0 9.1 %collective-permute-start.8 = (bf16[8,2560]{1,0:T(8,128)(2,1)S(1)}, bf16[8,2560]{1,0:T(8,128)(2,1)S(1)}, u32[]{:S(2)}, u32[]{:S(2)}) collective-permute-start(bf16[8,2560]{1,0:T(8,128)(2,1)S(1)} %get-tuple-element.65), channel_id=1, source_target_pairs={{0,24},{4,28},{8,16},{12,20},{16,8},{20,12},{24,0},{28,4},{1,25},{... | collective-permute-start | bytes 122888 | tf_op jit(solution)/shard_map/ppermute | solution.py:565
  51.7 8.3 %collective-permute-start.9 = (bf16[8,2560]{1,0:T(8,128)(2,1)S(1)}, bf16[8,2560]{1,0:T(8,128)(2,1)S(1)}, u32[]{:S(2)}, u32[]{:S(2)}) collective-permute-start(bf16[8,2560]{1,0:T(8,128)(2,1)S(1)} %get-tuple-element.66), channel_id=1, source_target_pairs={{0,8},{4,12},{8,0},{12,4},{16,24},{20,28},{24,16},{28,20},{1,9},{5... | collective-permute-start | bytes 122888 | tf_op jit(solution)/shard_map/ppermute | solution.py:565
  53.7 6.3 %collective-permute-start.10 = (bf16[8,2560]{1,0:T(8,128)(2,1)S(1)}, bf16[8,2560]{1,0:T(8,128)(2,1)S(1)}, u32[]{:S(2)}, u32[]{:S(2)}) collective-permute-start(bf16[8,2560]{1,0:T(8,128)(2,1)S(1)} %get-tuple-element.67), channel_id=1, source_target_pairs={{0,20},{4,16},{8,28},{12,24},{16,4},{20,0},{24,12},{28,8},{1,21},{... | collective-permute-start | bytes 122888 | tf_op jit(solution)/shard_map/ppermute | solution.py:565
  56.0 4.0 %collective-permute-start.11 = (bf16[8,2560]{1,0:T(8,128)(2,1)S(1)}, bf16[8,2560]{1,0:T(8,128)(2,1)S(1)}, u32[]{:S(2)}, u32[]{:S(2)}) collective-permute-start(bf16[8,2560]{1,0:T(8,128)(2,1)S(1)} %get-tuple-element.68), channel_id=1, source_target_pairs={{0,4},{4,0},{8,12},{12,8},{16,20},{20,16},{24,28},{28,24},{1,5},{5... | collective-permute-start | bytes 122888 | tf_op jit(solution)/shard_map/ppermute | solution.py:565
  56.8 4.0 %collective-permute-start.12 = (bf16[8,2560]{1,0:T(8,128)(2,1)S(1)}, bf16[8,2560]{1,0:T(8,128)(2,1)S(1)}, u32[]{:S(2)}, u32[]{:S(2)}) collective-permute-start(bf16[8,2560]{1,0:T(8,128)(2,1)S(1)} %get-tuple-element.69), channel_id=1, source_target_pairs={{0,16},{4,20},{8,24},{12,28},{16,0},{20,4},{24,8},{28,12},{1,17},{... | collective-permute-start | bytes 122888 | tf_op jit(solution)/shard_map/ppermute | solution.py:565

commit v6 on v5

--- a/solution.py
+++ b/solution.py
@@ -203,25 +203,80 @@
     )(where, *map(in_hbm, (patch, gain, bias, up, up_bias, down, down_bias, text, rms_gain)))
 
 
-def weights_kernel(keyval, query, out, query_out, sem):
+def owner_slots(owner_row, me, rows, capacity, slots):
+    total = owner_row.shape[1]
+    row = lax.broadcasted_iota(jnp.int32, (total, rows), 0)
+    mine = (row == me * rows + lax.broadcasted_iota(jnp.int32, (total, rows), 1)).astype(F32).astype(BF16)
+    named = (owner_row[...] ^ me).astype(F32).astype(BF16)
+    across = dot(named, mine)
+    down = lax.dot_general(mine, named, (((0,), (1,)), ((), ())), preferred_element_type=F32)
+    earlier = lax.broadcasted_iota(jnp.int32, (rows, rows), 0) < lax.broadcasted_iota(jnp.int32, (rows, rows), 1)
+    rank = jnp.sum(jnp.where((down == across) & earlier, 1.0, 0.0), axis=0, keepdims=True)
+    slot = across * capacity + rank
+    return (lax.broadcasted_iota(jnp.int32, (slots, rows), 0).astype(F32) == slot).astype(F32).astype(BF16)
+
+
+def slot_places(owner_row, me, owners, slots):
+    total = owner_row.shape[1]
+    capacity = slots // owners
+    named = (owner_row[...] == me).astype(F32).astype(BF16)
+    source = lax.broadcasted_iota(jnp.int32, (total, slots), 0) // (total // owners)
+    block = (lax.broadcasted_iota(jnp.int32, (total, slots), 1) // capacity) ^ me
+    here = dot(named, (source == block).astype(F32).astype(BF16))
+    offset = dot(named, (source < block).astype(F32).astype(BF16))
+    index = (lax.broadcasted_iota(jnp.int32, (1, slots), 1) % capacity).astype(F32)
+    target = jnp.where(index < here, offset + index, -1.0)
+    position = lax.broadcasted_iota(jnp.int32, (slots, slots), 0).astype(F32)
+    return (position == target).astype(F32).astype(BF16)
+
+
+def join_matrix(mp, count, width):
+    heads = KV_HEADS // count
+    coords = HEAD_DIM // count
+    full = 2 * heads * HEAD_DIM
+    column = lax.broadcasted_iota(jnp.int32, (width, full), 1)
+    row = lax.broadcasted_iota(jnp.int32, (width, full), 0)
+    base = (row // coords) * HEAD_DIM + row % coords
+    places = [(column == base + (mp ^ x) * coords).astype(F32).astype(BF16) for x in range(count)]
+    return jnp.concatenate(places, axis=0)
+
+
+def weights_kernel(owners, where, owner_row, keyval, query, out, query_out, select, place, join, buf, sem, query_sem):
     depth, _, columns = keyval.shape
     pieces = sem.shape[0]
     step = depth // pieces
-    width = query_out.shape[1]
+    together = step // 128
+
+    def copy(i):
+        return pltpu.make_async_copy(keyval.at[tile(i, step)], buf.at[tile(i, step)], sem.at[i])
+
+    for i in range(pieces):
+        copy(i).start()
+    part = depth // query_sem.shape[0]
     copies = [
-        pltpu.make_async_copy(query.at[pl.ds(i * step, step), pl.ds(0, width)], query_out.at[pl.ds(i * step, step)], sem.at[i])
-        for i in range(pieces)
+        pltpu.make_async_copy(
+            query.at[pl.ds(i * part, part), pl.ds(0, query_out.shape[1])],
+            query_out.at[pl.ds(i * part, part)],
+            query_sem.at[i],
+        )
+        for i in range(query_sem.shape[0])
     ]
-    for copy in copies:
-        copy.start()
-    pairs = keyval.reshape(2 * depth, columns)
+    for query_copy in copies:
+        query_copy.start()
+    mp, me = where[0], where[1]
+    slots, rows = select.shape
+    select[...] = owner_slots(owner_row, me, rows, slots // owners, slots)
+    place[...] = slot_places(owner_row, me, owners, slots)
+    count = KV_HEADS * HEAD_DIM // columns
+    join[...] = join_matrix(mp, count, join.shape[0] // count)
+    pairs = buf.reshape(2 * depth, columns)
     row = lax.broadcasted_iota(jnp.int32, (256, 256), 0)
     column = lax.broadcasted_iota(jnp.int32, (256, 256), 1)
     apart = (column == 2 * (row % 128) + row // 128).astype(F32).astype(BF16)
-    together = 8
-
-    @pl.loop(0, depth // (128 * together))
+
+    @pl.loop(0, pieces)
     def _(j):
+        copy(j).wait()
         blocks = [pairs[tile(j * together + n, 256), :] for n in range(together)]
         ordered = dot(apart, jnp.concatenate(blocks, axis=1)).astype(BF16)
         for n in range(together):
@@ -230,22 +285,29 @@
                     side * 128 : (side + 1) * 128, n * columns : (n + 1) * columns
                 ]
 
-    for copy in copies:
-        copy.wait()
-
-
-def weights_ahead(keyval, query, width):
+    for query_copy in copies:
+        query_copy.wait()
+
+
+def weights_ahead(where, owner_row, keyval, query, width, owners, slots):
     depth, _, columns = keyval.shape
+    rows = owner_row.shape[1] // owners
     return pl.pallas_call(
-        weights_kernel,
-        out_shape=[pltpu.VMEM((depth, 2 * columns), BF16), pltpu.VMEM((depth, width), BF16)],
-        in_specs=[VMEM, HBM],
-        out_specs=[VMEM, VMEM],
-        scratch_shapes=[pltpu.SemaphoreType.DMA((4,))],
-        compiler_params=params(8),
-        cost_estimate=cost(4 * depth * columns * 256, 4 * depth * columns + 2 * depth * width),
+        functools.partial(weights_kernel, owners),
+        out_shape=[
+            pltpu.VMEM((depth, 2 * columns), BF16),
+            pltpu.VMEM((depth, width), BF16),
+            jax.ShapeDtypeStruct((slots, rows), BF16),
+            jax.ShapeDtypeStruct((slots, slots), BF16),
+            jax.ShapeDtypeStruct((2 * columns, 2 * columns), BF16),
+        ],
+        in_specs=[SMEM, VMEM, HBM, HBM],
+        out_specs=[VMEM] * 5,
+        scratch_shapes=[pltpu.VMEM(keyval.shape, BF16), pltpu.SemaphoreType.DMA((8,)), pltpu.SemaphoreType.DMA((4,))],
+        compiler_params=params(16),
+        cost_estimate=cost(4 * depth * columns * 256, 4 * depth * columns),
         name="weights_ahead",
-    )(in_vmem(keyval), in_hbm(query))
+    )(where, owner_row, in_hbm(keyval), in_hbm(query))
 
 
 def keyval_kernel(where, text, own, sibling, gain, weight, bias, rows_all, *rest):
@@ -341,49 +403,27 @@
     )(in_vmem(rows_all), in_vmem(ready), in_hbm(weight), bias)
 
 
-def join_matrix(mp, count, width):
-    heads = KV_HEADS // count
-    coords = HEAD_DIM // count
-    full = 2 * heads * HEAD_DIM
-    column = lax.broadcasted_iota(jnp.int32, (width, full), 1)
-    row = lax.broadcasted_iota(jnp.int32, (width, full), 0)
-    base = (row // coords) * HEAD_DIM + row % coords
-    places = [(column == base + (mp ^ x) * coords).astype(F32).astype(BF16) for x in range(count)]
-    return jnp.concatenate(places, axis=0)
-
-
-def slots_kernel(owners, where, owner_row, queries, *rest):
+def slots_kernel(owners, select, queries, *rest):
     parts, outs = rest[:-owners], rest[-owners:]
-    rows, columns = queries.shape
+    rows = queries.shape[0]
     capacity = outs[0].shape[0]
-    slots = owners * capacity
-    me = where[1]
-    row = lax.broadcasted_iota(jnp.int32, (owners * rows, rows), 0)
-    mine = (row == me * rows + lax.broadcasted_iota(jnp.int32, (owners * rows, rows), 1)).astype(F32).astype(BF16)
-    named = (owner_row[...] ^ me).astype(F32).astype(BF16)
-    across = dot(named, mine)
-    down = lax.dot_general(mine, named, (((0,), (1,)), ((), ())), preferred_element_type=F32)
-    earlier = lax.broadcasted_iota(jnp.int32, (rows, rows), 0) < lax.broadcasted_iota(jnp.int32, (rows, rows), 1)
-    rank = jnp.sum(jnp.where((down == across) & earlier, 1.0, 0.0), axis=0, keepdims=True)
-    slot = across * capacity + rank
-    select = (lax.broadcasted_iota(jnp.int32, (slots, rows), 0).astype(F32) == slot).astype(F32).astype(BF16)
-    width = parts[0].shape[1]
     images = [queries[...]] + [part[pl.ds(part.shape[0] - rows, rows), :] for part in parts]
-    chosen = dot(select, jnp.concatenate(images, axis=1))
+    chosen = dot(select[...], jnp.concatenate(images, axis=1))
     for x, out in enumerate(outs):
         out[...] = chosen[x * capacity : (x + 1) * capacity].astype(BF16)
 
 
-def slots_of(where, owner_row, queries, parts, owners, capacity):
+def slots_of(select, queries, parts, owners):
     width = queries.shape[1] + len(parts) * parts[0].shape[1]
+    capacity = select.shape[0] // owners
     return pl.pallas_call(
         functools.partial(slots_kernel, owners),
         out_shape=[jax.ShapeDtypeStruct((capacity, width), BF16)] * owners,
-        in_specs=[SMEM] + [VMEM] * (2 + len(parts)),
+        in_specs=[VMEM] * (2 + len(parts)),
         out_specs=[VMEM] * owners,
         compiler_params=params(8),
         name="slots",
-    )(where, owner_row, queries, *parts)
+    )(select, queries, *parts)
 
 
 def attend(blocks, first, doc_row, queries, kv_all, out):
@@ -394,6 +434,7 @@
     block = DOC_MAX
     scale = 1.0 / math.sqrt(HEAD_DIM)
     docs = doc_row[...].astype(F32)
+    ones = jnp.ones((2 * block, HEAD_DIM), BF16)
     row = lax.broadcasted_iota(jnp.int32, (block, 2 * block), 0)
     column = lax.broadcasted_iota(jnp.int32, (block, 2 * block), 1)
     for b in range(*blocks):
@@ -412,33 +453,18 @@
             scores = lax.dot_general(q, keys, (((1,), (1,)), ((), ())), preferred_element_type=F32) * scale
             scores = jnp.where(penalty < 0.0, penalty, scores)
             weights = jnp.exp(scores - jnp.max(scores, axis=-1, keepdims=True))
-            probs = (weights * (1.0 / jnp.sum(weights, axis=-1, keepdims=True))).astype(BF16)
-            result = dot(probs, values).astype(BF16)
+            result = dot(weights.astype(BF16), jnp.concatenate([values, ones], axis=1))
+            result = (result[:, :HEAD_DIM] / result[:, HEAD_DIM:]).astype(BF16)
             for h in range(shared):
                 out[pl.ds(q0 - out_first, block), tile(g * shared + h, HEAD_DIM)] = result[h * block : (h + 1) * block]
         yield b
 
 
-def late_kernel(early, owners, where, owner_row, doc_row, first_half, second_half, *rest):
-    parts = rest[:-4]
-    out, kv_all, join, place = rest[-4:]
-    mp, me = where[0], where[1]
+def late_kernel(early, join, doc_row, first_half, second_half, *rest):
+    parts, out, kv_all = rest[:-2], rest[-2], rest[-1]
     seq = first_half.shape[0]
-    join[...] = join_matrix(mp, len(parts), parts[0].shape[1])
     sent = jnp.concatenate([part[pl.ds(0, seq), :] for part in parts], axis=1)
     kv_all[...] = dot(sent, join[...]).astype(BF16)
-    slots = place.shape[0]
-    capacity = slots // owners
-    named = (owner_row[...] == me).astype(F32).astype(BF16)
-    total = owner_row.shape[1]
-    source = lax.broadcasted_iota(jnp.int32, (total, slots), 0) // (total // owners)
-    block = (lax.broadcasted_iota(jnp.int32, (total, slots), 1) // capacity) ^ me
-    here = dot(named, (source == block).astype(F32).astype(BF16))
-    offset = dot(named, (source < block).astype(F32).astype(BF16))
-    index = (lax.broadcasted_iota(jnp.int32, (1, slots), 1) % capacity).astype(F32)
-    target = jnp.where(index < here, offset + index, -1.0)
-    position = lax.broadcasted_iota(jnp.int32, (slots, slots), 0).astype(F32)
-    place[...] = (position == target).astype(F32).astype(BF16)
     blocks = (early // DOC_MAX, seq // DOC_MAX)
     for _ in attend(blocks, (0, 0, early), doc_row, (first_half, second_half), kv_all, out):
         pass
@@ -471,24 +497,21 @@
         copy.wait()
 
 
-def attention(where, owner_row, documents, halves, parts, arrived, order, owners, slots, columns):
+def attention(join, place, documents, halves, parts, arrived, order, columns):
     seq = documents.shape[1]
-    full = 2 * (KV_HEADS // len(parts)) * HEAD_DIM
+    full = join.shape[1]
+    slots = place.shape[0]
+    owners = len(order)
     early = min(seq, -(-slots // DOC_MAX) * DOC_MAX + DOC_MAX)
-    out, keyval, join, place = pl.pallas_call(
-        functools.partial(late_kernel, early, owners),
-        out_shape=[
-            pltpu.VMEM((seq - early, columns), BF16),
-            jax.ShapeDtypeStruct((seq, full), BF16),
-            jax.ShapeDtypeStruct((len(parts) * parts[0].shape[1], full), BF16),
-            jax.ShapeDtypeStruct((slots, slots), BF16),
-        ],
-        in_specs=[SMEM] + [VMEM] * (4 + len(parts)),
-        out_specs=[VMEM] * 4,
+    out, keyval = pl.pallas_call(
+        functools.partial(late_kernel, early),
+        out_shape=[pltpu.VMEM((seq - early, columns), BF16), jax.ShapeDtypeStruct((seq, full), BF16)],
+        in_specs=[VMEM] * (4 + len(parts)),
+        out_specs=[VMEM] * 2,
         compiler_params=params(12),
         cost_estimate=cost(4 * (seq - early) * columns * 2 * DOC_MAX, 4 * seq * columns),
         name="attention_late",
-    )(where, owner_row, documents, *halves, *parts)
+    )(join, documents, *halves, *parts)
     return pl.pallas_call(
         functools.partial(early_kernel, early, order),
         out_shape=jax.ShapeDtypeStruct((seq, columns), BF16),
@@ -545,7 +568,10 @@
         text_embed[0], rms_gain[None, :], rows,
     )
     own = (keep.astype(F32) + exchange(send, count, 1).astype(F32)).astype(BF16)
-    weight, ready = weights_ahead(after(w_keyval, send), w_query, w_query.shape[1] // 4)
+    slots = owners * capacity
+    weight, ready, select, place, join = weights_ahead(
+        where, owner_row, after(w_keyval, own), w_query, w_query.shape[1] // 4, owners, slots
+    )
     bit = 2
     while bit < count:
         other = after(exchange(own, count, bit), weight)
@@ -557,7 +583,7 @@
     rows_all, parts = keyval_parts(where, text, own, sibling, rms_gain[None, :], weight, keyval_bias, count)
     parts = [parts[0]] + [exchange(parts[x], count, x) for x in range(1, count)]
     *halves, image_queries = query_rows(rows_all, text.shape[0], ready, w_query, query_bias[None, :])
-    outgoing = slots_of(where, owner_row, image_queries, parts, owners, capacity)
+    outgoing = slots_of(select, image_queries, parts, owners)
 
     order = sorted(range(1, owners), key=far, reverse=True)
 
@@ -566,9 +592,7 @@
         return lax.optimization_barrier((*rows, outgoing[0], done))[:-1]
 
     halves = [after(half, outgoing[0]) for half in halves]
-    return attention(
-        where, owner_row, doc_ids, halves, parts, arrived, [*order, 0], owners, owners * capacity, columns
-    )[None]
+    return attention(join, place, doc_ids, halves, parts, arrived, [*order, 0], columns)[None]
 
 
 def general(

time: 63.2 us -> 62.2 us (0.984)
  waiting for transfers between devices: 5.14 us -> 4.07 us
    ppermute x6, waiting for transfers between devices: 4.37 us -> 2.69 us  [exchange(): return lax.ppermute(x, 'mp', [(i, i ^ bit) for i in range(count)])]
    pallas_call x2, Pallas kernels: 7.69 us -> 8.99 us  [the longest x1 6.91 us: weights_ahead(): pl.pallas_call(functools.partial(weights_kernel, owners), out_shape=[pltp...]
    pallas_call x1, Pallas kernels: 1.02 us -> 0.21 us  [slots_of(): pl.pallas_call(functools.partial(slots_kernel, owners), out_shape=[jax.Sh...]
  transfers between devices with their start and end apart: 13 -> 13, of which waited for: 4 -> 5; matrix products, arithmetic and copies ran while one was open for 0% -> 0% of each run, Pallas kernels for 30% -> 33%
where the time goes in v6:
time: 62.2 us; the launch traced here: 62.1 us
  Pallas kernels  40.8 us (66%)
  starting transfers between devices  16.7 us (27%)
  waiting for transfers between devices  4.07 us (7%)
    pallas_call x1, Pallas kernels, merger(): pl.pallas_call(merger_kernel, out_shape=[jax.ShapeDtypeStruct((rows, colu...  14.3 us
    pallas_call x1, Pallas kernels, query_rows(): pl.pallas_call(query_kernel, out_shape=[jax.ShapeDtypeStruct((texts, colu...  11.2 us
    ppermute x7, starting transfers between devices, arrived(): lax.ppermute(outgoing[x], ('group', 'dp'), [(i, i ^ x) for i in range(own...  11.2 us
    pallas_call x1, Pallas kernels, weights_ahead(): pl.pallas_call(functools.partial(weights_kernel, owners), out_shape=[pltp...  6.91 us
    ppermute x6, starting transfers between devices, exchange(): return lax.ppermute(x, 'mp', [(i, i ^ bit) for i in range(count)])  5.47 us
    pallas_call x1, Pallas kernels, keyval_parts(): pl.pallas_call(keyval_kernel, out_shape=[pltpu.VMEM((rows, depth), BF16)]...  3.82 us
    ppermute x6, waiting for transfers between devices, exchange(): return lax.ppermute(x, 'mp', [(i, i ^ bit) for i in range(count)])  2.69 us
    pallas_call x1, Pallas kernels, attention(): pl.pallas_call(functools.partial(early_kernel, early, order), out_shape=j...  2.27 us
  transfers between devices with their start and end apart: 13, of which 5 were waited for; matrix products, arithmetic and copies ran while one was open for 0% of the time, Pallas kernels for 33%

profile of v6, /device:TPU:0, one launch (start us, length us, event | category | flops | bytes accessed | tf_op | source)
XLA Modules:
  0.0 62.1 jit_solution(1559144628618081093)
XLA Ops:
  0.0 0.1 pad_add_fusion.where
  0.1 14.3 %merger.1 = (bf16[32,4096]{1,0:T(8,128)(2,1)S(1)}, bf16[32,4096]{1,0:T(8,128)(2,1)S(1)}, bf16[256,8192]{1,0:T(8,128)(2,1)S(1)}) custom-call(s32[2]{0:T(128)S(1)} %pad_add_fusion.where, bf16[128,1280]{1,0:T(8,128)(2,1)} %bitcast.13, f32[1280]{0:T(1024)} %gain_in.1, f32[1280]{0:T(1024)} %bias_in.1, bf16[5120,1280]{1,0:T(8,128)(2,1)} %up.1, f32[1280]{0:T(1024)} %up_bias_in.1, ...), custom_call_target="tpu_custom_call" | custom-call | flops 1090519040 | bytes 34078720 | tf_op jit(solution)/shard_map/merger/pallas_call | solution.py:176
  14.4 0.5 collective-permute-start
  14.9 1.2 %collective-permute-done = bf16[32,4096]{1,0:T(8,128)(2,1)S(1)} collective-permute-done((bf16[32,4096]{1,0:T(8,128)(2,1)S(1)}, bf16[32,4096]{1,0:T(8,128)(2,1)S(1)}, u32[]{:S(2)}, u32[]{:S(2)}) %collective-permute-start) | collective-permute-done | bytes 262176 | tf_op jit(solution)/shard_map/ppermute | solution.py:533
  16.1 0.1 add_convert_fusion.1
  16.1 3.0 %collective-permute-start.1 = (bf16[32,4096]{1,0:T(8,128)(2,1)S(1)}, bf16[32,4096]{1,0:T(8,128)(2,1)S(1)}, u32[]{:S(2)}, u32[]{:S(2)}) collective-permute-start(bf16[32,4096]{1,0:T(8,128)(2,1)S(1)} %add_convert_fusion.1), channel_id=1, source_target_pairs={{0,2},{1,3},{2,0},{3,1},{4,6},{5,7},{6,4},{7,5},{8,10},{9,11},{10,... | collective-permute-start | bytes 786440 | tf_op jit(solution)/shard_map/ppermute | solution.py:533
  19.1 6.9 %weights_ahead.1 = (bf16[8192,512]{1,0:T(8,128)(2,1)S(1)}, bf16[8192,512]{1,0:T(8,128)(2,1)S(1)}, bf16[64,32]{1,0:T(8,128)(2,1)S(1)}, bf16[64,64]{1,0:T(8,128)(2,1)S(1)}, bf16[512,512]{1,0:T(8,128)(2,1)S(1)}) custom-call(s32[2]{0:T(128)S(1)} %pad_add_fusion.where, s32[1,256]{1,0:T(1,128)S(1)} %bitcast.11, bf16[8192,2,256]{2,1,0:T(2,128)(2,1)} %keyval.1, ...), custom_call_target="tpu_custom_call" | custom-call | flops 2147483648 | bytes 8388608 | tf_op jit(solution)/shard_map/weights_ahead/pallas_call | solution.py:295
  26.0 0.0 copy-start.1
  26.0 0.1 add_convert_fusion.own
  26.1 0.1 collective-permute-start.2
  26.2 1.5 %collective-permute-done.2.sibling = bf16[32,4096]{1,0:T(8,128)(2,1)S(1)} collective-permute-done((bf16[32,4096]{1,0:T(8,128)(2,1)S(1)}, bf16[32,4096]{1,0:T(8,128)(2,1)S(1)}, u32[]{:S(2)}, u32[]{:S(2)}) %collective-permute-start.2) | collective-permute-done | bytes 262176 | tf_op jit(solution)/shard_map/ppermute | solution.py:533
  27.7 3.8 %keyval.2 = (bf16[288,8192]{1,0:T(8,128)(2,1)S(1)}, bf16[288,128]{1,0:T(8,128)(2,1)S(1)}, bf16[288,128]{1,0:T(8,128)(2,1)S(1)}, bf16[288,128]{1,0:T(8,128)(2,1)S(1)}, bf16[288,128]{1,0:T(8,128)(2,1)S(1)}) custom-call(s32[2]{0:T(128)S(1)} %pad_add_fusion.where, bf16[256,8192]{1,0:T(8,128)(2,1)S(1)} %get-tuple-element.43.text, ...), custom_call_target="tpu_custom_call" | custom-call | flops 2415919104 | bytes 8388608 | tf_op jit(solution)/shard_map/keyval/pallas_call | solution.py:349
  31.5 0.2 collective-permute-start.3
  31.7 1.4 %collective-permute-start.4 = (bf16[288,128]{1,0:T(8,128)(2,1)S(1)}, bf16[288,128]{1,0:T(8,128)(2,1)S(1)}, u32[]{:S(2)}, u32[]{:S(2)}) collective-permute-start(bf16[288,128]{1,0:T(8,128)(2,1)S(1)} %get-tuple-element.56), channel_id=1, source_target_pairs={{0,2},{1,3},{2,0},{3,1},{4,6},{5,7},{6,4},{7,5},{8,10},{9,11},{10,... | collective-permute-start | bytes 221192 | tf_op jit(solution)/shard_map/ppermute | solution.py:533
  33.2 0.3 collective-permute-start.5
  33.5 11.2 %query.3 = (bf16[256,1024]{1,0:T(8,128)(2,1)S(1)}, bf16[256,1024]{1,0:T(8,128)(2,1)S(1)}, bf16[32,2048]{1,0:T(8,128)(2,1)S(1)}) custom-call(bf16[288,8192]{1,0:T(8,128)(2,1)S(1)} %get-tuple-element.49.rows_all, bf16[8192,512]{1,0:T(8,128)(2,1)S(1)} %get-tuple-element.50.ready, bf16[8192,2048]{1,0:T(8,128)(2,1)} %weight.1, f32[1,2048]{1,0:T(1,128)S(1)} %bitcast.10), custom_call_target="tpu_custom_call" | custom-call | flops 9663676416 | bytes 33554432 | tf_op jit(solution)/shard_map/query/pallas_call | solution.py:394
  44.7 0.0 collective-permute-done.3.rest_1_
  44.7 0.0 collective-permute-done.5.rest_3_
  44.7 0.2 slots.1
  44.9 4.6 %collective-permute-start.6 = (bf16[8,2560]{1,0:T(8,128)(2,1)S(1)}, bf16[8,2560]{1,0:T(8,128)(2,1)S(1)}, u32[]{:S(2)}, u32[]{:S(2)}) collective-permute-start(bf16[8,2560]{1,0:T(8,128)(2,1)S(1)} %get-tuple-element.65), channel_id=1, source_target_pairs={{0,28},{4,24},{8,20},{12,16},{16,12},{20,8},{24,4},{28,0},{1,29},{... | collective-permute-start | bytes 122888 | tf_op jit(solution)/shard_map/ppermute | solution.py:591
  49.5 0.2 collective-permute-start.7
  49.8 0.8 %collective-permute-start.8 = (bf16[8,2560]{1,0:T(8,128)(2,1)S(1)}, bf16[8,2560]{1,0:T(8,128)(2,1)S(1)}, u32[]{:S(2)}, u32[]{:S(2)}) collective-permute-start(bf16[8,2560]{1,0:T(8,128)(2,1)S(1)} %get-tuple-element.67), channel_id=1, source_target_pairs={{0,24},{4,28},{8,16},{12,20},{16,8},{20,12},{24,0},{28,4},{1,25},{... | collective-permute-start | bytes 122888 | tf_op jit(solution)/shard_map/ppermute | solution.py:591
  50.5 2.1 %collective-permute-start.9 = (bf16[8,2560]{1,0:T(8,128)(2,1)S(1)}, bf16[8,2560]{1,0:T(8,128)(2,1)S(1)}, u32[]{:S(2)}, u32[]{:S(2)}) collective-permute-start(bf16[8,2560]{1,0:T(8,128)(2,1)S(1)} %get-tuple-element.68), channel_id=1, source_target_pairs={{0,8},{4,12},{8,0},{12,4},{16,24},{20,28},{24,16},{28,20},{1,9},{5... | collective-permute-start | bytes 122888 | tf_op jit(solution)/shard_map/ppermute | solution.py:591
  52.7 2.2 %collective-permute-start.10 = (bf16[8,2560]{1,0:T(8,128)(2,1)S(1)}, bf16[8,2560]{1,0:T(8,128)(2,1)S(1)}, u32[]{:S(2)}, u32[]{:S(2)}) collective-permute-start(bf16[8,2560]{1,0:T(8,128)(2,1)S(1)} %get-tuple-element.69), channel_id=1, source_target_pairs={{0,20},{4,16},{8,28},{12,24},{16,4},{20,0},{24,12},{28,8},{1,21},{... | collective-permute-start | bytes 122888 | tf_op jit(solution)/shard_map/ppermute | solution.py:591
  54.8 0.0 collective-permute-done.6.rest_0_
  54.8 0.8 %collective-permute-start.11 = (bf16[8,2560]{1,0:T(8,128)(2,1)S(1)}, bf16[8,2560]{1,0:T(8,128)(2,1)S(1)}, u32[]{:S(2)}, u32[]{:S(2)}) collective-permute-start(bf16[8,2560]{1,0:T(8,128)(2,1)S(1)} %get-tuple-element.70), channel_id=1, source_target_pairs={{0,4},{4,0},{8,12},{12,8},{16,20},{20,16},{24,28},{28,24},{1,5},{5... | collective-permute-start | bytes 122888 | tf_op jit(solution)/shard_map/ppermute | solution.py:591
  55.6 0.5 collective-permute-start.12
  56.2 2.1 %attention_late.1 = (bf16[128,2048]{1,0:T(8,128)(2,1)S(1)}, bf16[256,512]{1,0:T(8,128)(2,1)S(1)}) custom-call(bf16[512,512]{1,0:T(8,128)(2,1)S(1)} %get-tuple-element.62.join, s32[1,256]{1,0:T(1,128)S(1)} %copy-done.2, bf16[256,1024]{1,0:T(8,128)(2,1)S(1)} %get-tuple-element.59.first_half, bf16[256,1024]{1,0:T(8,128)(2,1)S(1)} %get-tuple-element.61.second_half, ...), custom_call_target="tpu_custom_call" | custom-call | flops 134217728 | bytes 2097152 | tf_op jit(solution)/shard_map/attention_late/pallas_call | solution.py:506
  58.3 0.3 collective-permute-done.10.rest_4_
  58.6 0.2 collective-permute-done.11.rest_5_
  58.8 0.8 %collective-permute-done.12.rest_6_ = bf16[8,2560]{1,0:T(8,128)(2,1)S(1)} collective-permute-done((bf16[8,2560]{1,0:T(8,128)(2,1)S(1)}, bf16[8,2560]{1,0:T(8,128)(2,1)S(1)}, u32[]{:S(2)}, u32[]{:S(2)}) %collective-permute-start.12) | collective-permute-done | bytes 40992 | tf_op jit(solution)/shard_map/ppermute | solution.py:591
  59.6 2.3 %attention_early.1 = bf16[256,2048]{1,0:T(8,128)(2,1)} custom-call(s32[1,256]{1,0:T(1,128)S(1)} %copy-done.2, bf16[256,1024]{1,0:T(8,128)(2,1)S(1)} %get-tuple-element.59.first_half, bf16[256,1024]{1,0:T(8,128)(2,1)S(1)} %get-tuple-element.61.second_half, bf16[256,512]{1,0:T(8,128)(2,1)S(1)} %get-tuple-element.63.keyval, ...), custom_call_target="tpu_custom_call" | custom-call | flops 134217728 | bytes 2097152 | tf_op jit(solution)/shard_map/attention_early/pallas_call | solution.py:515
  (14 shorter events, 0.0 us)
Async XLA Ops:
  0.1 19.0 %copy-start.4 = (s32[256,1]{0,1:T(1,128)S(1)}, s32[256,1]{0,1:T(1,128)}, u32[]{:S(2)}) copy-start(s32[256,1]{0,1:T(1,128)} %param.22) | copy-start | bytes 3076
  14.4 1.7 %collective-permute-start = (bf16[32,4096]{1,0:T(8,128)(2,1)S(1)}, bf16[32,4096]{1,0:T(8,128)(2,1)S(1)}, u32[]{:S(2)}, u32[]{:S(2)}) collective-permute-start(bf16[32,4096]{1,0:T(8,128)(2,1)S(1)} %get-tuple-element.45), channel_id=1, source_target_pairs={{0,1},{1,0},{2,3},{3,2},{4,5},{5,4},{6,7},{7,6},{8,9},{9,8},{10,11... | collective-permute-start | bytes 786440 | tf_op jit(solution)/shard_map/ppermute | solution.py:533
  16.1 9.9 %collective-permute-start.1 = (bf16[32,4096]{1,0:T(8,128)(2,1)S(1)}, bf16[32,4096]{1,0:T(8,128)(2,1)S(1)}, u32[]{:S(2)}, u32[]{:S(2)}) collective-permute-start(bf16[32,4096]{1,0:T(8,128)(2,1)S(1)} %add_convert_fusion.1), channel_id=1, source_target_pairs={{0,2},{1,3},{2,0},{3,1},{4,6},{5,7},{6,4},{7,5},{8,10},{9,11},{10,... | collective-permute-start | bytes 786440 | tf_op jit(solution)/shard_map/ppermute | solution.py:533
  19.1 8.6 %copy-start = (f32[8192]{0:T(1024)S(1)}, f32[8192]{0:T(1024)}, u32[]{:S(2)}) copy-start(f32[8192]{0:T(1024)} %param.25) | copy-start | bytes 98308
  19.1 8.6 %copy-start.3 = (f32[2,256]{1,0:T(2,128)S(1)}, f32[2,256]{1,0:T(2,128)}, u32[]{:S(2)}) copy-start(f32[2,256]{1,0:T(2,128)} %bias.1) | copy-start | bytes 6148
  26.0 7.4 %copy-start.1 = (f32[2048]{0:T(1024)S(1)}, f32[2048]{0:T(1024)}, u32[]{:S(2)}) copy-start(f32[2048]{0:T(1024)} %param.27) | copy-start | bytes 24580
  26.1 1.6 %collective-permute-start.2 = (bf16[32,4096]{1,0:T(8,128)(2,1)S(1)}, bf16[32,4096]{1,0:T(8,128)(2,1)S(1)}, u32[]{:S(2)}, u32[]{:S(2)}) collective-permute-start(bf16[32,4096]{1,0:T(8,128)(2,1)S(1)} %add_convert_fusion.own), channel_id=1, source_target_pairs={{0,1},{1,0},{2,3},{3,2},{4,5},{5,4},{6,7},{7,6},{8,9},{9,8},{10,11... | collective-permute-start | bytes 786440 | tf_op jit(solution)/shard_map/ppermute | solution.py:533
  31.5 13.2 %collective-permute-start.3 = (bf16[288,128]{1,0:T(8,128)(2,1)S(1)}, bf16[288,128]{1,0:T(8,128)(2,1)S(1)}, u32[]{:S(2)}, u32[]{:S(2)}) collective-permute-start(bf16[288,128]{1,0:T(8,128)(2,1)S(1)} %get-tuple-element.55), channel_id=1, source_target_pairs={{0,1},{1,0},{2,3},{3,2},{4,5},{5,4},{6,7},{7,6},{8,9},{9,8},{10,11... | collective-permute-start | bytes 221192 | tf_op jit(solution)/shard_map/ppermute | solution.py:533
  31.7 13.0 %collective-permute-start.4 = (bf16[288,128]{1,0:T(8,128)(2,1)S(1)}, bf16[288,128]{1,0:T(8,128)(2,1)S(1)}, u32[]{:S(2)}, u32[]{:S(2)}) collective-permute-start(bf16[288,128]{1,0:T(8,128)(2,1)S(1)} %get-tuple-element.56), channel_id=1, source_target_pairs={{0,2},{1,3},{2,0},{3,1},{4,6},{5,7},{6,4},{7,5},{8,10},{9,11},{10,... | collective-permute-start | bytes 221192 | tf_op jit(solution)/shard_map/ppermute | solution.py:533
  33.2 11.6 %collective-permute-start.5 = (bf16[288,128]{1,0:T(8,128)(2,1)S(1)}, bf16[288,128]{1,0:T(8,128)(2,1)S(1)}, u32[]{:S(2)}, u32[]{:S(2)}) collective-permute-start(bf16[288,128]{1,0:T(8,128)(2,1)S(1)} %get-tuple-element.57), channel_id=1, source_target_pairs={{0,3},{1,2},{2,1},{3,0},{4,7},{5,6},{6,5},{7,4},{8,11},{9,10},{10,... | collective-permute-start | bytes 221192 | tf_op jit(solution)/shard_map/ppermute | solution.py:533
  33.5 22.7 %copy-start.2 = (s32[1,256]{1,0:T(1,128)S(1)}, s32[1,256]{1,0:T(1,128)}, u32[]{:S(2)}) copy-start(s32[1,256]{1,0:T(1,128)} %doc_row.3) | copy-start | bytes 3076
  44.9 9.9 %collective-permute-start.6 = (bf16[8,2560]{1,0:T(8,128)(2,1)S(1)}, bf16[8,2560]{1,0:T(8,128)(2,1)S(1)}, u32[]{:S(2)}, u32[]{:S(2)}) collective-permute-start(bf16[8,2560]{1,0:T(8,128)(2,1)S(1)} %get-tuple-element.65), channel_id=1, source_target_pairs={{0,28},{4,24},{8,20},{12,16},{16,12},{20,8},{24,4},{28,0},{1,29},{... | collective-permute-start | bytes 122888 | tf_op jit(solution)/shard_map/ppermute | solution.py:591
  49.5 6.1 %collective-permute-start.7 = (bf16[8,2560]{1,0:T(8,128)(2,1)S(1)}, bf16[8,2560]{1,0:T(8,128)(2,1)S(1)}, u32[]{:S(2)}, u32[]{:S(2)}) collective-permute-start(bf16[8,2560]{1,0:T(8,128)(2,1)S(1)} %get-tuple-element.66), channel_id=1, source_target_pairs={{0,12},{4,8},{8,4},{12,0},{16,28},{20,24},{24,20},{28,16},{1,13},{... | collective-permute-start | bytes 122888 | tf_op jit(solution)/shard_map/ppermute | solution.py:591
  49.8 8.5 %collective-permute-start.8 = (bf16[8,2560]{1,0:T(8,128)(2,1)S(1)}, bf16[8,2560]{1,0:T(8,128)(2,1)S(1)}, u32[]{:S(2)}, u32[]{:S(2)}) collective-permute-start(bf16[8,2560]{1,0:T(8,128)(2,1)S(1)} %get-tuple-element.67), channel_id=1, source_target_pairs={{0,24},{4,28},{8,16},{12,20},{16,8},{20,12},{24,0},{28,4},{1,25},{... | collective-permute-start | bytes 122888 | tf_op jit(solution)/shard_map/ppermute | solution.py:591
  50.5 7.7 %collective-permute-start.9 = (bf16[8,2560]{1,0:T(8,128)(2,1)S(1)}, bf16[8,2560]{1,0:T(8,128)(2,1)S(1)}, u32[]{:S(2)}, u32[]{:S(2)}) collective-permute-start(bf16[8,2560]{1,0:T(8,128)(2,1)S(1)} %get-tuple-element.68), channel_id=1, source_target_pairs={{0,8},{4,12},{8,0},{12,4},{16,24},{20,28},{24,16},{28,20},{1,9},{5... | collective-permute-start | bytes 122888 | tf_op jit(solution)/shard_map/ppermute | solution.py:591
  52.7 5.9 %collective-permute-start.10 = (bf16[8,2560]{1,0:T(8,128)(2,1)S(1)}, bf16[8,2560]{1,0:T(8,128)(2,1)S(1)}, u32[]{:S(2)}, u32[]{:S(2)}) collective-permute-start(bf16[8,2560]{1,0:T(8,128)(2,1)S(1)} %get-tuple-element.69), channel_id=1, source_target_pairs={{0,20},{4,16},{8,28},{12,24},{16,4},{20,0},{24,12},{28,8},{1,21},{... | collective-permute-start | bytes 122888 | tf_op jit(solution)/shard_map/ppermute | solution.py:591
  54.8 4.0 %collective-permute-start.11 = (bf16[8,2560]{1,0:T(8,128)(2,1)S(1)}, bf16[8,2560]{1,0:T(8,128)(2,1)S(1)}, u32[]{:S(2)}, u32[]{:S(2)}) collective-permute-start(bf16[8,2560]{1,0:T(8,128)(2,1)S(1)} %get-tuple-element.70), channel_id=1, source_target_pairs={{0,4},{4,0},{8,12},{12,8},{16,20},{20,16},{24,28},{28,24},{1,5},{5... | collective-permute-start | bytes 122888 | tf_op jit(solution)/shard_map/ppermute | solution.py:591
  55.6 4.0 %collective-permute-start.12 = (bf16[8,2560]{1,0:T(8,128)(2,1)S(1)}, bf16[8,2560]{1,0:T(8,128)(2,1)S(1)}, u32[]{:S(2)}, u32[]{:S(2)}) collective-permute-start(bf16[8,2560]{1,0:T(8,128)(2,1)S(1)} %get-tuple-element.71), channel_id=1, source_target_pairs={{0,16},{4,20},{8,24},{12,28},{16,0},{20,4},{24,8},{28,12},{1,17},{... | collective-permute-start | bytes 122888 | tf_op jit(solution)/shard_map/ppermute | solution.py:591

commit v7 on v6

--- a/solution.py
+++ b/solution.py
@@ -310,23 +310,32 @@
     )(where, owner_row, in_hbm(keyval), in_hbm(query))
 
 
-def keyval_kernel(where, text, own, sibling, gain, weight, bias, rows_all, *rest):
+def keyval_own_kernel(where, text, own, gain, weight, rows_all, sums):
+    texts, half = text.shape[0], own.shape[1]
+    here = pl.ds(pl.multiple_of((where[0] % 2) * half, half), half)
+    rows_all[pl.ds(0, texts), :] = text[...]
+    rows_all[pl.ds(texts, own.shape[0]), here] = (own[...].astype(F32) * gain[:, here]).astype(BF16)
+    sums[...] = dot(rows_all[:, here], weight[here, :])
+
+
+def keyval_kernel(where, _, sums_in, own, sibling, gain, weight, bias, rows_all, scale_out, *rest):
     parts, keyval = rest[:-1], rest[-1]
-    texts, images = text.shape[0], own.shape[0]
+    images, half = own.shape
+    texts = rows_all.shape[0] - images
     mp = where[0]
-    half = own.shape[1]
-    mine = mp % 2
+    here = pl.ds(pl.multiple_of((1 - mp % 2) * half, half), half)
     first, second = own[...].astype(F32), sibling[...].astype(F32)
+    rows_all[pl.ds(texts, images), here] = (second * gain[:, here]).astype(BF16)
     squares = jnp.sum(first * first, axis=-1, keepdims=True) + jnp.sum(second * second, axis=-1, keepdims=True)
     scale = lax.rsqrt(squares / (2 * half) + 1e-06)
-    for values, which in ((first, mine), (second, 1 - mine)):
-        here = pl.ds(pl.multiple_of(which * half, half), half)
-        rows_all[pl.ds(texts, images), here] = (values * scale * gain[:, here]).astype(BF16)
-    rows_all[pl.ds(0, texts), :] = text[...]
+    scale_out[...] = jnp.broadcast_to(scale, scale_out.shape)
     columns = weight.shape[1] // 2
-    sums = dot(rows_all[...], weight[...])
+    sums = sums_in[...] + dot(rows_all[:, here], weight[here, :])
     for t in range(2):
-        keyval[t] = (sums[:, t * columns : (t + 1) * columns] + bias[pl.ds(t, 1), :]).astype(BF16)
+        side = slice(t * columns, (t + 1) * columns)
+        add = bias[pl.ds(t, 1), :]
+        keyval[t, pl.ds(0, texts), :] = (sums[:texts, side] + add).astype(BF16)
+        keyval[t, pl.ds(texts, images), :] = (sums[texts:, side] * scale + add).astype(BF16)
 
     count = len(parts)
     width = parts[0].shape[1]
@@ -344,23 +353,35 @@
 def keyval_parts(where, text, own, sibling, gain, weight, bias, count):
     texts, depth = text.shape
     columns = weight.shape[1] // 2
-    rows = texts + own.shape[0]
+    images = own.shape[0]
+    rows = texts + images
     width = 2 * columns // count
+    weight = in_vmem(weight)
+    rows_all, sums = pl.pallas_call(
+        keyval_own_kernel,
+        out_shape=[pltpu.VMEM((rows, depth), BF16), pltpu.VMEM((rows, 2 * columns), F32)],
+        in_specs=[SMEM, VMEM, VMEM, VMEM, VMEM],
+        out_specs=[VMEM] * 2,
+        compiler_params=params(8),
+        cost_estimate=cost(2 * rows * depth * columns, 2 * depth * columns),
+        name="keyval_own",
+    )(where, in_vmem(text), own, gain, weight)
     outs = pl.pallas_call(
         keyval_kernel,
-        out_shape=[pltpu.VMEM((rows, depth), BF16)]
+        out_shape=[pltpu.VMEM((rows, depth), BF16), jax.ShapeDtypeStruct((images, 128), F32)]
         + [jax.ShapeDtypeStruct((rows, width), BF16)] * count,
-        in_specs=[SMEM, VMEM, VMEM, VMEM, VMEM, VMEM, VMEM],
-        out_specs=[VMEM] * (1 + count),
+        in_specs=[SMEM] + [VMEM] * 7,
+        out_specs=[VMEM] * (2 + count),
         scratch_shapes=[pltpu.VMEM((2, rows, columns), BF16)],
+        input_output_aliases={1: 0},
         compiler_params=params(8),
-        cost_estimate=cost(4 * rows * depth * columns, 4 * depth * columns),
+        cost_estimate=cost(2 * rows * depth * columns, 2 * depth * columns),
         name="keyval",
-    )(where, in_vmem(text), own, sibling, gain, in_vmem(weight), bias)
-    return outs[0], outs[1:]
-
-
-def query_kernel(rows_all, ready, weight, bias, first_half, second_half, image_out, buf, sem):
+    )(where, in_vmem(rows_all), in_vmem(sums), own, after(sibling, sums), gain, weight, bias)
+    return outs[0], outs[1], outs[2:]
+
+
+def query_kernel(rows_all, scale, ready, weight, bias, first_half, second_half, image_out, buf, sem):
     width = ready.shape[1]
     texts, half = first_half.shape
     later = buf.shape[0]
@@ -369,9 +390,10 @@
         return pltpu.make_async_copy(weight.at[:, tile(i + 1, width)], buf.at[i], sem.at[i])
 
     def columns(i, weights, text_out, offset):
-        out = (dot(rows_all[...], weights) + bias[:, tile(i, width)]).astype(BF16)
-        text_out[:, pl.ds(i * width - offset, width)] = out[:texts]
-        image_out[:, tile(i, width)] = out[texts:]
+        out = dot(rows_all[...], weights)
+        add = bias[:, tile(i, width)]
+        text_out[:, pl.ds(i * width - offset, width)] = (out[:texts] + add).astype(BF16)
+        image_out[:, tile(i, width)] = (out[texts:] * scale[:, :1] + add).astype(BF16)
 
     begin(copy, 2)
     columns(0, ready[...], first_half, 0)
@@ -385,7 +407,7 @@
             columns(i, buf[i - 1], second_half, half)
 
 
-def query_rows(rows_all, texts, ready, weight, bias):
+def query_rows(rows_all, scale, texts, ready, weight, bias):
     depth = rows_all.shape[1]
     images = rows_all.shape[0] - texts
     columns = weight.shape[1]
@@ -394,13 +416,13 @@
     return pl.pallas_call(
         query_kernel,
         out_shape=[jax.ShapeDtypeStruct((texts, columns // 2), BF16)] * 2 + [jax.ShapeDtypeStruct((images, columns), BF16)],
-        in_specs=[VMEM, VMEM, HBM, VMEM],
+        in_specs=[VMEM, VMEM, VMEM, HBM, VMEM],
         out_specs=[VMEM] * 3,
         scratch_shapes=[pltpu.VMEM((later, depth, width), BF16), pltpu.SemaphoreType.DMA((later,))],
         compiler_params=params(30),
         cost_estimate=cost(2 * (texts + images) * depth * columns, 2 * depth * columns),
         name="query",
-    )(in_vmem(rows_all), in_vmem(ready), in_hbm(weight), bias)
+    )(in_vmem(rows_all), scale, in_vmem(ready), in_hbm(weight), bias)
 
 
 def slots_kernel(owners, select, queries, *rest):
@@ -580,9 +602,9 @@
     sibling = exchange(own, count, 1)
 
     columns = w_query.shape[1]
-    rows_all, parts = keyval_parts(where, text, own, sibling, rms_gain[None, :], weight, keyval_bias, count)
+    rows_all, scale, parts = keyval_parts(where, text, own, sibling, rms_gain[None, :], weight, keyval_bias, count)
     parts = [parts[0]] + [exchange(parts[x], count, x) for x in range(1, count)]
-    *halves, image_queries = query_rows(rows_all, text.shape[0], ready, w_query, query_bias[None, :])
+    *halves, image_queries = query_rows(rows_all, scale, text.shape[0], ready, w_query, query_bias[None, :])
     outgoing = slots_of(select, image_queries, parts, owners)
 
     order = sorted(range(1, owners), key=far, reverse=True)

time: 62.2 us -> 61.6 us (level)
  waiting for transfers between devices: 4.07 us -> 2.72 us
  Pallas kernels: 40.8 us -> 41.5 us
    ppermute x6, waiting for transfers between devices: 2.69 us -> 1.18 us  [exchange(): return lax.ppermute(x, 'mp', [(i, i ^ bit) for i in range(count)])]
    pallas_call x1 -> x2, Pallas kernels: 3.82 us -> 4.4 us  [the longest x1 2.39 us: keyval_parts(): pl.pallas_call(keyval_kernel, out_shape=[pltpu.VMEM((rows, depth), BF16),...]
  transfers between devices with their start and end apart: 13 -> 13, of which waited for: 5 -> 4; matrix products, arithmetic and copies ran while one was open for 0% -> 0% of each run, Pallas kernels for 33% -> 36%
where the time goes in v7:
time: 61.6 us; the launch traced here: 61.5 us
  Pallas kernels  41.5 us (67%)
  starting transfers between devices  16.7 us (27%)
  waiting for transfers between devices  2.72 us (4%)
    pallas_call x1, Pallas kernels, merger(): pl.pallas_call(merger_kernel, out_shape=[jax.ShapeDtypeStruct((rows, colu...  14.3 us
    pallas_call x1, Pallas kernels, query_rows(): pl.pallas_call(query_kernel, out_shape=[jax.ShapeDtypeStruct((texts, colu...  11.3 us
    ppermute x7, starting transfers between devices, arrived(): lax.ppermute(outgoing[x], ('group', 'dp'), [(i, i ^ x) for i in range(own...  11.2 us
    pallas_call x1, Pallas kernels, weights_ahead(): pl.pallas_call(functools.partial(weights_kernel, owners), out_shape=[pltp...  6.91 us
    ppermute x6, starting transfers between devices, exchange(): return lax.ppermute(x, 'mp', [(i, i ^ bit) for i in range(count)])  5.54 us
    pallas_call x1, Pallas kernels, keyval_parts(): pl.pallas_call(keyval_kernel, out_shape=[pltpu.VMEM((rows, depth), BF16),...  2.39 us
    pallas_call x1, Pallas kernels, attention(): pl.pallas_call(functools.partial(early_kernel, early, order), out_shape=j...  2.28 us
    pallas_call x1, Pallas kernels, attention(): pl.pallas_call(functools.partial(late_kernel, early), out_shape=[pltpu.VM...  2.08 us
  transfers between devices with their start and end apart: 13, of which 4 were waited for; matrix products, arithmetic and copies ran while one was open for 0% of the time, Pallas kernels for 36%

profile of v7, /device:TPU:0, one launch (start us, length us, event | category | flops | bytes accessed | tf_op | source)
XLA Modules:
  0.0 61.5 jit_solution(7804550976702578987)
XLA Ops:
  0.0 0.1 pad_add_fusion.where
  0.1 14.3 %merger.1 = (bf16[32,4096]{1,0:T(8,128)(2,1)S(1)}, bf16[32,4096]{1,0:T(8,128)(2,1)S(1)}, bf16[256,8192]{1,0:T(8,128)(2,1)S(1)}) custom-call(s32[2]{0:T(128)S(1)} %pad_add_fusion.where, bf16[128,1280]{1,0:T(8,128)(2,1)} %bitcast.14, f32[1280]{0:T(1024)} %gain_in.1, f32[1280]{0:T(1024)} %bias_in.1, bf16[5120,1280]{1,0:T(8,128)(2,1)} %up.1, f32[1280]{0:T(1024)} %up_bias_in.1, ...), custom_call_target="tpu_custom_call" | custom-call | flops 1090519040 | bytes 34078720 | tf_op jit(solution)/shard_map/merger/pallas_call | solution.py:176
  14.4 0.5 collective-permute-start
  14.9 1.2 %collective-permute-done = bf16[32,4096]{1,0:T(8,128)(2,1)S(1)} collective-permute-done((bf16[32,4096]{1,0:T(8,128)(2,1)S(1)}, bf16[32,4096]{1,0:T(8,128)(2,1)S(1)}, u32[]{:S(2)}, u32[]{:S(2)}) %collective-permute-start) | collective-permute-done | bytes 262176 | tf_op jit(solution)/shard_map/ppermute | solution.py:555
  16.1 0.1 add_convert_fusion.1
  16.1 3.0 %collective-permute-start.1 = (bf16[32,4096]{1,0:T(8,128)(2,1)S(1)}, bf16[32,4096]{1,0:T(8,128)(2,1)S(1)}, u32[]{:S(2)}, u32[]{:S(2)}) collective-permute-start(bf16[32,4096]{1,0:T(8,128)(2,1)S(1)} %add_convert_fusion.1), channel_id=1, source_target_pairs={{0,2},{1,3},{2,0},{3,1},{4,6},{5,7},{6,4},{7,5},{8,10},{9,11},{10,... | collective-permute-start | bytes 786440 | tf_op jit(solution)/shard_map/ppermute | solution.py:555
  19.1 6.9 %weights_ahead.1 = (bf16[8192,512]{1,0:T(8,128)(2,1)S(1)}, bf16[8192,512]{1,0:T(8,128)(2,1)S(1)}, bf16[64,32]{1,0:T(8,128)(2,1)S(1)}, bf16[64,64]{1,0:T(8,128)(2,1)S(1)}, bf16[512,512]{1,0:T(8,128)(2,1)S(1)}) custom-call(s32[2]{0:T(128)S(1)} %pad_add_fusion.where, s32[1,256]{1,0:T(1,128)S(1)} %bitcast.12, bf16[8192,2,256]{2,1,0:T(2,128)(2,1)} %keyval.1, ...), custom_call_target="tpu_custom_call" | custom-call | flops 2147483648 | bytes 8388608 | tf_op jit(solution)/shard_map/weights_ahead/pallas_call | solution.py:295
  26.0 0.0 copy-start.3
  26.0 0.0 collective-permute-done.1
  26.0 0.1 add_convert_fusion.own
  26.1 0.1 collective-permute-start.2
  26.2 2.0 %keyval_own.1 = (bf16[288,8192]{1,0:T(8,128)(2,1)S(1)}, f32[288,512]{1,0:T(8,128)S(1)}) custom-call(s32[2]{0:T(128)S(1)} %pad_add_fusion.where, bf16[256,8192]{1,0:T(8,128)(2,1)S(1)} %get-tuple-element.47.text, bf16[32,4096]{1,0:T(8,128)(2,1)S(1)} %add_convert_fusion.own, f32[1,8192]{1,0:T(1,128)S(1)} %bitcast.9, bf16[8192,512]{1,0:T(8,128)(2,1)S(1)} %get-tuple-element.51.weight), custom_call_target="tpu_custom_call" | custom-call | flops 1207959552 | bytes 4194304 | tf_op jit(solution)/shard_map/keyval_own/pallas_call | solution.py:360
  28.2 0.0 copy-start.1
  28.2 0.0 collective-permute-done.2.sibling
  28.3 2.4 %keyval.2 = (bf16[288,8192]{1,0:T(8,128)(2,1)S(1)}, f32[32,128]{1,0:T(8,128)S(1)}, bf16[288,128]{1,0:T(8,128)(2,1)S(1)}, bf16[288,128]{1,0:T(8,128)(2,1)S(1)}, b...) custom-call(s32[2]{0:T(128)S(1)} %pad_add_fusion.where, ...), custom_call_target="tpu_custom_call", output_to_operand_aliasing={{0}: (1, {})} | custom-call | flops 1207959552 | bytes 4194304 | tf_op jit(solution)/shard_map/keyval/pallas_call | solution.py:369
  30.6 0.6 collective-permute-start.3
  31.2 1.4 %collective-permute-start.4 = (bf16[288,128]{1,0:T(8,128)(2,1)S(1)}, bf16[288,128]{1,0:T(8,128)(2,1)S(1)}, u32[]{:S(2)}, u32[]{:S(2)}) collective-permute-start(bf16[288,128]{1,0:T(8,128)(2,1)S(1)} %get-tuple-element.64), channel_id=1, source_target_pairs={{0,2},{1,3},{2,0},{3,1},{4,6},{5,7},{6,4},{7,5},{8,10},{9,11},{10,... | collective-permute-start | bytes 221192 | tf_op jit(solution)/shard_map/ppermute | solution.py:555
  32.6 0.0 collective-permute-start.5
  32.6 11.3 %query.3 = (bf16[256,1024]{1,0:T(8,128)(2,1)S(1)}, bf16[256,1024]{1,0:T(8,128)(2,1)S(1)}, bf16[32,2048]{1,0:T(8,128)(2,1)S(1)}) custom-call(bf16[288,8192]{1,0:T(8,128)(2,1)S(1)} %get-tuple-element.56.rows_all, f32[32,128]{1,0:T(8,128)S(1)} %get-tuple-element.57.scale, bf16[8192,512]{1,0:T(8,128)(2,1)S(1)} %get-tuple-element.58.ready, ...), custom_call_target="tpu_custom_call" | custom-call | flops 9663676416 | bytes 33554432 | tf_op jit(solution)/shard_map/query/pallas_call | solution.py:416
  43.9 0.2 slots.1
  44.2 4.6 %collective-permute-start.6 = (bf16[8,2560]{1,0:T(8,128)(2,1)S(1)}, bf16[8,2560]{1,0:T(8,128)(2,1)S(1)}, u32[]{:S(2)}, u32[]{:S(2)}) collective-permute-start(bf16[8,2560]{1,0:T(8,128)(2,1)S(1)} %get-tuple-element.73), channel_id=1, source_target_pairs={{0,28},{4,24},{8,20},{12,16},{16,12},{20,8},{24,4},{28,0},{1,29},{... | collective-permute-start | bytes 122888 | tf_op jit(solution)/shard_map/ppermute | solution.py:613
  48.8 0.2 collective-permute-start.7
  49.0 0.8 %collective-permute-start.8 = (bf16[8,2560]{1,0:T(8,128)(2,1)S(1)}, bf16[8,2560]{1,0:T(8,128)(2,1)S(1)}, u32[]{:S(2)}, u32[]{:S(2)}) collective-permute-start(bf16[8,2560]{1,0:T(8,128)(2,1)S(1)} %get-tuple-element.75), channel_id=1, source_target_pairs={{0,24},{4,28},{8,16},{12,20},{16,8},{20,12},{24,0},{28,4},{1,25},{... | collective-permute-start | bytes 122888 | tf_op jit(solution)/shard_map/ppermute | solution.py:613
  49.7 2.1 %collective-permute-start.9 = (bf16[8,2560]{1,0:T(8,128)(2,1)S(1)}, bf16[8,2560]{1,0:T(8,128)(2,1)S(1)}, u32[]{:S(2)}, u32[]{:S(2)}) collective-permute-start(bf16[8,2560]{1,0:T(8,128)(2,1)S(1)} %get-tuple-element.76), channel_id=1, source_target_pairs={{0,8},{4,12},{8,0},{12,4},{16,24},{20,28},{24,16},{28,20},{1,9},{5... | collective-permute-start | bytes 122888 | tf_op jit(solution)/shard_map/ppermute | solution.py:613
  51.9 2.2 %collective-permute-start.10 = (bf16[8,2560]{1,0:T(8,128)(2,1)S(1)}, bf16[8,2560]{1,0:T(8,128)(2,1)S(1)}, u32[]{:S(2)}, u32[]{:S(2)}) collective-permute-start(bf16[8,2560]{1,0:T(8,128)(2,1)S(1)} %get-tuple-element.77), channel_id=1, source_target_pairs={{0,20},{4,16},{8,28},{12,24},{16,4},{20,0},{24,12},{28,8},{1,21},{... | collective-permute-start | bytes 122888 | tf_op jit(solution)/shard_map/ppermute | solution.py:613
  54.0 0.8 %collective-permute-start.11 = (bf16[8,2560]{1,0:T(8,128)(2,1)S(1)}, bf16[8,2560]{1,0:T(8,128)(2,1)S(1)}, u32[]{:S(2)}, u32[]{:S(2)}) collective-permute-start(bf16[8,2560]{1,0:T(8,128)(2,1)S(1)} %get-tuple-element.78), channel_id=1, source_target_pairs={{0,4},{4,0},{8,12},{12,8},{16,20},{20,16},{24,28},{28,24},{1,5},{5... | collective-permute-start | bytes 122888 | tf_op jit(solution)/shard_map/ppermute | solution.py:613
  54.8 0.2 collective-permute-done.7.rest_1_
  55.0 0.5 collective-permute-start.12
  55.5 2.1 %attention_late.1 = (bf16[128,2048]{1,0:T(8,128)(2,1)S(1)}, bf16[256,512]{1,0:T(8,128)(2,1)S(1)}) custom-call(bf16[512,512]{1,0:T(8,128)(2,1)S(1)} %get-tuple-element.70.join, s32[1,256]{1,0:T(1,128)S(1)} %copy-done.2, bf16[256,1024]{1,0:T(8,128)(2,1)S(1)} %get-tuple-element.67.first_half, bf16[256,1024]{1,0:T(8,128)(2,1)S(1)} %get-tuple-element.69.second_half, ...), custom_call_target="tpu_custom_call" | custom-call | flops 134217728 | bytes 2097152 | tf_op jit(solution)/shard_map/attention_late/pallas_call | solution.py:528
  57.7 0.4 collective-permute-done.10.rest_4_
  58.1 0.9 %collective-permute-done.12.rest_6_ = bf16[8,2560]{1,0:T(8,128)(2,1)S(1)} collective-permute-done((bf16[8,2560]{1,0:T(8,128)(2,1)S(1)}, bf16[8,2560]{1,0:T(8,128)(2,1)S(1)}, u32[]{:S(2)}, u32[]{:S(2)}) %collective-permute-start.12) | collective-permute-done | bytes 40992 | tf_op jit(solution)/shard_map/ppermute | solution.py:613
  59.0 2.3 %attention_early.1 = bf16[256,2048]{1,0:T(8,128)(2,1)} custom-call(s32[1,256]{1,0:T(1,128)S(1)} %copy-done.2, bf16[256,1024]{1,0:T(8,128)(2,1)S(1)} %get-tuple-element.67.first_half, bf16[256,1024]{1,0:T(8,128)(2,1)S(1)} %get-tuple-element.69.second_half, bf16[256,512]{1,0:T(8,128)(2,1)S(1)} %get-tuple-element.71.keyval, ...), custom_call_target="tpu_custom_call" | custom-call | flops 134217728 | bytes 2097152 | tf_op jit(solution)/shard_map/attention_early/pallas_call | solution.py:537
  (15 shorter events, 0.0 us)
Async XLA Ops:
  0.1 19.0 %copy-start.4 = (s32[256,1]{0,1:T(1,128)S(1)}, s32[256,1]{0,1:T(1,128)}, u32[]{:S(2)}) copy-start(s32[256,1]{0,1:T(1,128)} %param.22) | copy-start | bytes 3076
  14.4 1.7 %collective-permute-start = (bf16[32,4096]{1,0:T(8,128)(2,1)S(1)}, bf16[32,4096]{1,0:T(8,128)(2,1)S(1)}, u32[]{:S(2)}, u32[]{:S(2)}) collective-permute-start(bf16[32,4096]{1,0:T(8,128)(2,1)S(1)} %get-tuple-element.49), channel_id=1, source_target_pairs={{0,1},{1,0},{2,3},{3,2},{4,5},{5,4},{6,7},{7,6},{8,9},{9,8},{10,11... | collective-permute-start | bytes 786440 | tf_op jit(solution)/shard_map/ppermute | solution.py:555
  16.1 9.9 %collective-permute-start.1 = (bf16[32,4096]{1,0:T(8,128)(2,1)S(1)}, bf16[32,4096]{1,0:T(8,128)(2,1)S(1)}, u32[]{:S(2)}, u32[]{:S(2)}) collective-permute-start(bf16[32,4096]{1,0:T(8,128)(2,1)S(1)} %add_convert_fusion.1), channel_id=1, source_target_pairs={{0,2},{1,3},{2,0},{3,1},{4,6},{5,7},{6,4},{7,5},{8,10},{9,11},{10,... | collective-permute-start | bytes 786440 | tf_op jit(solution)/shard_map/ppermute | solution.py:555
  19.1 7.1 %copy-start = (f32[8192]{0:T(1024)S(1)}, f32[8192]{0:T(1024)}, u32[]{:S(2)}) copy-start(f32[8192]{0:T(1024)} %param.25) | copy-start | bytes 98308
  26.0 2.2 %copy-start.3 = (f32[2,256]{1,0:T(2,128)S(1)}, f32[2,256]{1,0:T(2,128)}, u32[]{:S(2)}) copy-start(f32[2,256]{1,0:T(2,128)} %bias.1) | copy-start | bytes 6148
  26.1 2.1 %collective-permute-start.2 = (bf16[32,4096]{1,0:T(8,128)(2,1)S(1)}, bf16[32,4096]{1,0:T(8,128)(2,1)S(1)}, u32[]{:S(2)}, u32[]{:S(2)}) collective-permute-start(bf16[32,4096]{1,0:T(8,128)(2,1)S(1)} %add_convert_fusion.own), channel_id=1, source_target_pairs={{0,1},{1,0},{2,3},{3,2},{4,5},{5,4},{6,7},{7,6},{8,9},{9,8},{10,11... | collective-permute-start | bytes 786440 | tf_op jit(solution)/shard_map/ppermute | solution.py:555
  28.2 4.4 %copy-start.1 = (f32[2048]{0:T(1024)S(1)}, f32[2048]{0:T(1024)}, u32[]{:S(2)}) copy-start(f32[2048]{0:T(1024)} %param.27) | copy-start | bytes 24580
  30.6 13.3 %collective-permute-start.3 = (bf16[288,128]{1,0:T(8,128)(2,1)S(1)}, bf16[288,128]{1,0:T(8,128)(2,1)S(1)}, u32[]{:S(2)}, u32[]{:S(2)}) collective-permute-start(bf16[288,128]{1,0:T(8,128)(2,1)S(1)} %get-tuple-element.63), channel_id=1, source_target_pairs={{0,1},{1,0},{2,3},{3,2},{4,5},{5,4},{6,7},{7,6},{8,9},{9,8},{10,11... | collective-permute-start | bytes 221192 | tf_op jit(solution)/shard_map/ppermute | solution.py:555
  31.2 12.7 %collective-permute-start.4 = (bf16[288,128]{1,0:T(8,128)(2,1)S(1)}, bf16[288,128]{1,0:T(8,128)(2,1)S(1)}, u32[]{:S(2)}, u32[]{:S(2)}) collective-permute-start(bf16[288,128]{1,0:T(8,128)(2,1)S(1)} %get-tuple-element.64), channel_id=1, source_target_pairs={{0,2},{1,3},{2,0},{3,1},{4,6},{5,7},{6,4},{7,5},{8,10},{9,11},{10,... | collective-permute-start | bytes 221192 | tf_op jit(solution)/shard_map/ppermute | solution.py:555
  32.6 11.3 %collective-permute-start.5 = (bf16[288,128]{1,0:T(8,128)(2,1)S(1)}, bf16[288,128]{1,0:T(8,128)(2,1)S(1)}, u32[]{:S(2)}, u32[]{:S(2)}) collective-permute-start(bf16[288,128]{1,0:T(8,128)(2,1)S(1)} %get-tuple-element.65), channel_id=1, source_target_pairs={{0,3},{1,2},{2,1},{3,0},{4,7},{5,6},{6,5},{7,4},{8,11},{9,10},{10,... | collective-permute-start | bytes 221192 | tf_op jit(solution)/shard_map/ppermute | solution.py:555
  32.6 22.9 %copy-start.2 = (s32[1,256]{1,0:T(1,128)S(1)}, s32[1,256]{1,0:T(1,128)}, u32[]{:S(2)}) copy-start(s32[1,256]{1,0:T(1,128)} %doc_row.3) | copy-start | bytes 3076
  44.2 9.9 %collective-permute-start.6 = (bf16[8,2560]{1,0:T(8,128)(2,1)S(1)}, bf16[8,2560]{1,0:T(8,128)(2,1)S(1)}, u32[]{:S(2)}, u32[]{:S(2)}) collective-permute-start(bf16[8,2560]{1,0:T(8,128)(2,1)S(1)} %get-tuple-element.73), channel_id=1, source_target_pairs={{0,28},{4,24},{8,20},{12,16},{16,12},{20,8},{24,4},{28,0},{1,29},{... | collective-permute-start | bytes 122888 | tf_op jit(solution)/shard_map/ppermute | solution.py:613
  48.8 6.3 %collective-permute-start.7 = (bf16[8,2560]{1,0:T(8,128)(2,1)S(1)}, bf16[8,2560]{1,0:T(8,128)(2,1)S(1)}, u32[]{:S(2)}, u32[]{:S(2)}) collective-permute-start(bf16[8,2560]{1,0:T(8,128)(2,1)S(1)} %get-tuple-element.74), channel_id=1, source_target_pairs={{0,12},{4,8},{8,4},{12,0},{16,28},{20,24},{24,20},{28,16},{1,13},{... | collective-permute-start | bytes 122888 | tf_op jit(solution)/shard_map/ppermute | solution.py:613
  49.0 8.7 %collective-permute-start.8 = (bf16[8,2560]{1,0:T(8,128)(2,1)S(1)}, bf16[8,2560]{1,0:T(8,128)(2,1)S(1)}, u32[]{:S(2)}, u32[]{:S(2)}) collective-permute-start(bf16[8,2560]{1,0:T(8,128)(2,1)S(1)} %get-tuple-element.75), channel_id=1, source_target_pairs={{0,24},{4,28},{8,16},{12,20},{16,8},{20,12},{24,0},{28,4},{1,25},{... | collective-permute-start | bytes 122888 | tf_op jit(solution)/shard_map/ppermute | solution.py:613
  49.7 7.9 %collective-permute-start.9 = (bf16[8,2560]{1,0:T(8,128)(2,1)S(1)}, bf16[8,2560]{1,0:T(8,128)(2,1)S(1)}, u32[]{:S(2)}, u32[]{:S(2)}) collective-permute-start(bf16[8,2560]{1,0:T(8,128)(2,1)S(1)} %get-tuple-element.76), channel_id=1, source_target_pairs={{0,8},{4,12},{8,0},{12,4},{16,24},{20,28},{24,16},{28,20},{1,9},{5... | collective-permute-start | bytes 122888 | tf_op jit(solution)/shard_map/ppermute | solution.py:613
  51.9 6.2 %collective-permute-start.10 = (bf16[8,2560]{1,0:T(8,128)(2,1)S(1)}, bf16[8,2560]{1,0:T(8,128)(2,1)S(1)}, u32[]{:S(2)}, u32[]{:S(2)}) collective-permute-start(bf16[8,2560]{1,0:T(8,128)(2,1)S(1)} %get-tuple-element.77), channel_id=1, source_target_pairs={{0,20},{4,16},{8,28},{12,24},{16,4},{20,0},{24,12},{28,8},{1,21},{... | collective-permute-start | bytes 122888 | tf_op jit(solution)/shard_map/ppermute | solution.py:613
  54.0 4.0 %collective-permute-start.11 = (bf16[8,2560]{1,0:T(8,128)(2,1)S(1)}, bf16[8,2560]{1,0:T(8,128)(2,1)S(1)}, u32[]{:S(2)}, u32[]{:S(2)}) collective-permute-start(bf16[8,2560]{1,0:T(8,128)(2,1)S(1)} %get-tuple-element.78), channel_id=1, source_target_pairs={{0,4},{4,0},{8,12},{12,8},{16,20},{20,16},{24,28},{28,24},{1,5},{5... | collective-permute-start | bytes 122888 | tf_op jit(solution)/shard_map/ppermute | solution.py:613
  55.0 4.0 %collective-permute-start.12 = (bf16[8,2560]{1,0:T(8,128)(2,1)S(1)}, bf16[8,2560]{1,0:T(8,128)(2,1)S(1)}, u32[]{:S(2)}, u32[]{:S(2)}) collective-permute-start(bf16[8,2560]{1,0:T(8,128)(2,1)S(1)} %get-tuple-element.79), channel_id=1, source_target_pairs={{0,16},{4,20},{8,24},{12,28},{16,0},{20,4},{24,8},{28,12},{1,17},{... | collective-permute-start | bytes 122888 | tf_op jit(solution)/shard_map/ppermute | solution.py:613

commit v8 on v7

--- a/solution.py
+++ b/solution.py
@@ -607,7 +607,7 @@
     *halves, image_queries = query_rows(rows_all, scale, text.shape[0], ready, w_query, query_bias[None, :])
     outgoing = slots_of(select, image_queries, parts, owners)
 
-    order = sorted(range(1, owners), key=far, reverse=True)
+    order = sorted(range(1, owners), key=lambda x: (x % 2 == 0, -x if x % 2 else -far(x)))
 
     def arrived(done):
         rows = [lax.ppermute(outgoing[x], ("group", "dp"), [(i, i ^ x) for i in range(owners)]) for x in order]

time: 61.6 us -> 61.2 us (level)
  no operation moved by 1% of the time
where the time goes in v8:
time: 61.2 us; the launch traced here: 61.1 us
  Pallas kernels  41.5 us (68%)
  starting transfers between devices  16.5 us (27%)
  waiting for transfers between devices  2.54 us (4%)
    pallas_call x1, Pallas kernels, merger(): pl.pallas_call(merger_kernel, out_shape=[jax.ShapeDtypeStruct((rows, colu...  14.3 us
    pallas_call x1, Pallas kernels, query_rows(): pl.pallas_call(query_kernel, out_shape=[jax.ShapeDtypeStruct((texts, colu...  11.3 us
    ppermute x7, starting transfers between devices, arrived(): lax.ppermute(outgoing[x], ('group', 'dp'), [(i, i ^ x) for i in range(own...  11 us
    pallas_call x1, Pallas kernels, weights_ahead(): pl.pallas_call(functools.partial(weights_kernel, owners), out_shape=[pltp...  6.91 us
    ppermute x6, starting transfers between devices, exchange(): return lax.ppermute(x, 'mp', [(i, i ^ bit) for i in range(count)])  5.54 us
    pallas_call x1, Pallas kernels, keyval_parts(): pl.pallas_call(keyval_kernel, out_shape=[pltpu.VMEM((rows, depth), BF16),...  2.39 us
    pallas_call x1, Pallas kernels, attention(): pl.pallas_call(functools.partial(early_kernel, early, order), out_shape=j...  2.28 us
    pallas_call x1, Pallas kernels, attention(): pl.pallas_call(functools.partial(late_kernel, early), out_shape=[pltpu.VM...  2.08 us
  transfers between devices with their start and end apart: 13, of which 4 were waited for; matrix products, arithmetic and copies ran while one was open for 0% of the time, Pallas kernels for 36%

profile of v8, /device:TPU:0, one launch (start us, length us, event | category | flops | bytes accessed | tf_op | source)
XLA Modules:
  0.0 61.1 jit_solution(4925266438402083655)
XLA Ops:
  0.0 0.1 pad_add_fusion.where
  0.1 14.3 %merger.1 = (bf16[32,4096]{1,0:T(8,128)(2,1)S(1)}, bf16[32,4096]{1,0:T(8,128)(2,1)S(1)}, bf16[256,8192]{1,0:T(8,128)(2,1)S(1)}) custom-call(s32[2]{0:T(128)S(1)} %pad_add_fusion.where, bf16[128,1280]{1,0:T(8,128)(2,1)} %bitcast.14, f32[1280]{0:T(1024)} %gain_in.1, f32[1280]{0:T(1024)} %bias_in.1, bf16[5120,1280]{1,0:T(8,128)(2,1)} %up.1, f32[1280]{0:T(1024)} %up_bias_in.1, ...), custom_call_target="tpu_custom_call" | custom-call | flops 1090519040 | bytes 34078720 | tf_op jit(solution)/shard_map/merger/pallas_call | solution.py:176
  14.4 0.5 collective-permute-start
  14.9 1.2 %collective-permute-done = bf16[32,4096]{1,0:T(8,128)(2,1)S(1)} collective-permute-done((bf16[32,4096]{1,0:T(8,128)(2,1)S(1)}, bf16[32,4096]{1,0:T(8,128)(2,1)S(1)}, u32[]{:S(2)}, u32[]{:S(2)}) %collective-permute-start) | collective-permute-done | bytes 262176 | tf_op jit(solution)/shard_map/ppermute | solution.py:555
  16.1 0.1 add_convert_fusion.1
  16.1 3.0 %collective-permute-start.1 = (bf16[32,4096]{1,0:T(8,128)(2,1)S(1)}, bf16[32,4096]{1,0:T(8,128)(2,1)S(1)}, u32[]{:S(2)}, u32[]{:S(2)}) collective-permute-start(bf16[32,4096]{1,0:T(8,128)(2,1)S(1)} %add_convert_fusion.1), channel_id=1, source_target_pairs={{0,2},{1,3},{2,0},{3,1},{4,6},{5,7},{6,4},{7,5},{8,10},{9,11},{10,... | collective-permute-start | bytes 786440 | tf_op jit(solution)/shard_map/ppermute | solution.py:555
  19.1 6.9 %weights_ahead.1 = (bf16[8192,512]{1,0:T(8,128)(2,1)S(1)}, bf16[8192,512]{1,0:T(8,128)(2,1)S(1)}, bf16[64,32]{1,0:T(8,128)(2,1)S(1)}, bf16[64,64]{1,0:T(8,128)(2,1)S(1)}, bf16[512,512]{1,0:T(8,128)(2,1)S(1)}) custom-call(s32[2]{0:T(128)S(1)} %pad_add_fusion.where, s32[1,256]{1,0:T(1,128)S(1)} %bitcast.12, bf16[8192,2,256]{2,1,0:T(2,128)(2,1)} %keyval.1, ...), custom_call_target="tpu_custom_call" | custom-call | flops 2147483648 | bytes 8388608 | tf_op jit(solution)/shard_map/weights_ahead/pallas_call | solution.py:295
  26.0 0.0 copy-start.3
  26.0 0.0 collective-permute-done.1
  26.0 0.1 add_convert_fusion.own
  26.1 0.1 collective-permute-start.2
  26.2 2.0 %keyval_own.1 = (bf16[288,8192]{1,0:T(8,128)(2,1)S(1)}, f32[288,512]{1,0:T(8,128)S(1)}) custom-call(s32[2]{0:T(128)S(1)} %pad_add_fusion.where, bf16[256,8192]{1,0:T(8,128)(2,1)S(1)} %get-tuple-element.47.text, bf16[32,4096]{1,0:T(8,128)(2,1)S(1)} %add_convert_fusion.own, f32[1,8192]{1,0:T(1,128)S(1)} %bitcast.9, bf16[8192,512]{1,0:T(8,128)(2,1)S(1)} %get-tuple-element.51.weight), custom_call_target="tpu_custom_call" | custom-call | flops 1207959552 | bytes 4194304 | tf_op jit(solution)/shard_map/keyval_own/pallas_call | solution.py:360
  28.2 0.0 copy-start.1
  28.2 0.0 collective-permute-done.2.sibling
  28.3 2.4 %keyval.2 = (bf16[288,8192]{1,0:T(8,128)(2,1)S(1)}, f32[32,128]{1,0:T(8,128)S(1)}, bf16[288,128]{1,0:T(8,128)(2,1)S(1)}, bf16[288,128]{1,0:T(8,128)(2,1)S(1)}, b...) custom-call(s32[2]{0:T(128)S(1)} %pad_add_fusion.where, ...), custom_call_target="tpu_custom_call", output_to_operand_aliasing={{0}: (1, {})} | custom-call | flops 1207959552 | bytes 4194304 | tf_op jit(solution)/shard_map/keyval/pallas_call | solution.py:369
  30.6 0.6 collective-permute-start.3
  31.2 1.4 %collective-permute-start.4 = (bf16[288,128]{1,0:T(8,128)(2,1)S(1)}, bf16[288,128]{1,0:T(8,128)(2,1)S(1)}, u32[]{:S(2)}, u32[]{:S(2)}) collective-permute-start(bf16[288,128]{1,0:T(8,128)(2,1)S(1)} %get-tuple-element.64), channel_id=1, source_target_pairs={{0,2},{1,3},{2,0},{3,1},{4,6},{5,7},{6,4},{7,5},{8,10},{9,11},{10,... | collective-permute-start | bytes 221192 | tf_op jit(solution)/shard_map/ppermute | solution.py:555
  32.6 0.0 collective-permute-start.5
  32.6 11.3 %query.3 = (bf16[256,1024]{1,0:T(8,128)(2,1)S(1)}, bf16[256,1024]{1,0:T(8,128)(2,1)S(1)}, bf16[32,2048]{1,0:T(8,128)(2,1)S(1)}) custom-call(bf16[288,8192]{1,0:T(8,128)(2,1)S(1)} %get-tuple-element.56.rows_all, f32[32,128]{1,0:T(8,128)S(1)} %get-tuple-element.57.scale, bf16[8192,512]{1,0:T(8,128)(2,1)S(1)} %get-tuple-element.58.ready, ...), custom_call_target="tpu_custom_call" | custom-call | flops 9663676416 | bytes 33554432 | tf_op jit(solution)/shard_map/query/pallas_call | solution.py:416
  43.9 0.0 collective-permute-done.4.rest_2_
  43.9 0.2 slots.1
  44.2 4.6 %collective-permute-start.6 = (bf16[8,2560]{1,0:T(8,128)(2,1)S(1)}, bf16[8,2560]{1,0:T(8,128)(2,1)S(1)}, u32[]{:S(2)}, u32[]{:S(2)}) collective-permute-start(bf16[8,2560]{1,0:T(8,128)(2,1)S(1)} %get-tuple-element.73), channel_id=1, source_target_pairs={{0,28},{4,24},{8,20},{12,16},{16,12},{20,8},{24,4},{28,0},{1,29},{... | collective-permute-start | bytes 122888 | tf_op jit(solution)/shard_map/ppermute | solution.py:613
  48.8 0.9 %collective-permute-start.8 = (bf16[8,2560]{1,0:T(8,128)(2,1)S(1)}, bf16[8,2560]{1,0:T(8,128)(2,1)S(1)}, u32[]{:S(2)}, u32[]{:S(2)}) collective-permute-start(bf16[8,2560]{1,0:T(8,128)(2,1)S(1)} %get-tuple-element.75), channel_id=1, source_target_pairs={{0,12},{4,8},{8,4},{12,0},{16,28},{20,24},{24,20},{28,16},{1,13},{... | collective-permute-start | bytes 122888 | tf_op jit(solution)/shard_map/ppermute | solution.py:613
  49.6 1.1 %collective-permute-start.9 = (bf16[8,2560]{1,0:T(8,128)(2,1)S(1)}, bf16[8,2560]{1,0:T(8,128)(2,1)S(1)}, u32[]{:S(2)}, u32[]{:S(2)}) collective-permute-start(bf16[8,2560]{1,0:T(8,128)(2,1)S(1)} %get-tuple-element.76), channel_id=1, source_target_pairs={{0,4},{4,0},{8,12},{12,8},{16,20},{20,16},{24,28},{28,24},{1,5},{5... | collective-permute-start | bytes 122888 | tf_op jit(solution)/shard_map/ppermute | solution.py:613
  50.8 2.8 %collective-permute-start.10 = (bf16[8,2560]{1,0:T(8,128)(2,1)S(1)}, bf16[8,2560]{1,0:T(8,128)(2,1)S(1)}, u32[]{:S(2)}, u32[]{:S(2)}) collective-permute-start(bf16[8,2560]{1,0:T(8,128)(2,1)S(1)} %get-tuple-element.77), channel_id=1, source_target_pairs={{0,24},{4,28},{8,16},{12,20},{16,8},{20,12},{24,0},{28,4},{1,25},{... | collective-permute-start | bytes 122888 | tf_op jit(solution)/shard_map/ppermute | solution.py:613
  53.6 1.0 %collective-permute-start.11 = (bf16[8,2560]{1,0:T(8,128)(2,1)S(1)}, bf16[8,2560]{1,0:T(8,128)(2,1)S(1)}, u32[]{:S(2)}, u32[]{:S(2)}) collective-permute-start(bf16[8,2560]{1,0:T(8,128)(2,1)S(1)} %get-tuple-element.78), channel_id=1, source_target_pairs={{0,8},{4,12},{8,0},{12,4},{16,24},{20,28},{24,16},{28,20},{1,9},{5... | collective-permute-start | bytes 122888 | tf_op jit(solution)/shard_map/ppermute | solution.py:613
  54.6 0.5 collective-permute-start.12
  55.2 2.1 %attention_late.1 = (bf16[128,2048]{1,0:T(8,128)(2,1)S(1)}, bf16[256,512]{1,0:T(8,128)(2,1)S(1)}) custom-call(bf16[512,512]{1,0:T(8,128)(2,1)S(1)} %get-tuple-element.70.join, s32[1,256]{1,0:T(1,128)S(1)} %copy-done.2, bf16[256,1024]{1,0:T(8,128)(2,1)S(1)} %get-tuple-element.67.first_half, bf16[256,1024]{1,0:T(8,128)(2,1)S(1)} %get-tuple-element.69.second_half, ...), custom_call_target="tpu_custom_call" | custom-call | flops 134217728 | bytes 2097152 | tf_op jit(solution)/shard_map/attention_late/pallas_call | solution.py:528
  57.3 0.1 collective-permute-done.10.rest_4_
  57.3 1.2 %collective-permute-done.11.rest_5_ = bf16[8,2560]{1,0:T(8,128)(2,1)S(1)} collective-permute-done((bf16[8,2560]{1,0:T(8,128)(2,1)S(1)}, bf16[8,2560]{1,0:T(8,128)(2,1)S(1)}, u32[]{:S(2)}, u32[]{:S(2)}) %collective-permute-start.11) | collective-permute-done | bytes 40992 | tf_op jit(solution)/shard_map/ppermute | solution.py:613
  58.5 0.1 collective-permute-done.12.rest_6_
  58.6 2.3 %attention_early.1 = bf16[256,2048]{1,0:T(8,128)(2,1)} custom-call(s32[1,256]{1,0:T(1,128)S(1)} %copy-done.2, bf16[256,1024]{1,0:T(8,128)(2,1)S(1)} %get-tuple-element.67.first_half, bf16[256,1024]{1,0:T(8,128)(2,1)S(1)} %get-tuple-element.69.second_half, bf16[256,512]{1,0:T(8,128)(2,1)S(1)} %get-tuple-element.71.keyval, ...), custom_call_target="tpu_custom_call" | custom-call | flops 134217728 | bytes 2097152 | tf_op jit(solution)/shard_map/attention_early/pallas_call | solution.py:537
  (15 shorter events, 0.0 us)
Async XLA Ops:
  0.1 19.0 %copy-start.4 = (s32[256,1]{0,1:T(1,128)S(1)}, s32[256,1]{0,1:T(1,128)}, u32[]{:S(2)}) copy-start(s32[256,1]{0,1:T(1,128)} %param.22) | copy-start | bytes 3076
  14.4 1.7 %collective-permute-start = (bf16[32,4096]{1,0:T(8,128)(2,1)S(1)}, bf16[32,4096]{1,0:T(8,128)(2,1)S(1)}, u32[]{:S(2)}, u32[]{:S(2)}) collective-permute-start(bf16[32,4096]{1,0:T(8,128)(2,1)S(1)} %get-tuple-element.49), channel_id=1, source_target_pairs={{0,1},{1,0},{2,3},{3,2},{4,5},{5,4},{6,7},{7,6},{8,9},{9,8},{10,11... | collective-permute-start | bytes 786440 | tf_op jit(solution)/shard_map/ppermute | solution.py:555
  16.1 9.9 %collective-permute-start.1 = (bf16[32,4096]{1,0:T(8,128)(2,1)S(1)}, bf16[32,4096]{1,0:T(8,128)(2,1)S(1)}, u32[]{:S(2)}, u32[]{:S(2)}) collective-permute-start(bf16[32,4096]{1,0:T(8,128)(2,1)S(1)} %add_convert_fusion.1), channel_id=1, source_target_pairs={{0,2},{1,3},{2,0},{3,1},{4,6},{5,7},{6,4},{7,5},{8,10},{9,11},{10,... | collective-permute-start | bytes 786440 | tf_op jit(solution)/shard_map/ppermute | solution.py:555
  19.1 7.1 %copy-start = (f32[8192]{0:T(1024)S(1)}, f32[8192]{0:T(1024)}, u32[]{:S(2)}) copy-start(f32[8192]{0:T(1024)} %param.25) | copy-start | bytes 98308
  26.0 2.2 %copy-start.3 = (f32[2,256]{1,0:T(2,128)S(1)}, f32[2,256]{1,0:T(2,128)}, u32[]{:S(2)}) copy-start(f32[2,256]{1,0:T(2,128)} %bias.1) | copy-start | bytes 6148
  26.1 2.1 %collective-permute-start.2 = (bf16[32,4096]{1,0:T(8,128)(2,1)S(1)}, bf16[32,4096]{1,0:T(8,128)(2,1)S(1)}, u32[]{:S(2)}, u32[]{:S(2)}) collective-permute-start(bf16[32,4096]{1,0:T(8,128)(2,1)S(1)} %add_convert_fusion.own), channel_id=1, source_target_pairs={{0,1},{1,0},{2,3},{3,2},{4,5},{5,4},{6,7},{7,6},{8,9},{9,8},{10,11... | collective-permute-start | bytes 786440 | tf_op jit(solution)/shard_map/ppermute | solution.py:555
  28.2 4.4 %copy-start.1 = (f32[2048]{0:T(1024)S(1)}, f32[2048]{0:T(1024)}, u32[]{:S(2)}) copy-start(f32[2048]{0:T(1024)} %param.27) | copy-start | bytes 24580
  30.6 13.3 %collective-permute-start.3 = (bf16[288,128]{1,0:T(8,128)(2,1)S(1)}, bf16[288,128]{1,0:T(8,128)(2,1)S(1)}, u32[]{:S(2)}, u32[]{:S(2)}) collective-permute-start(bf16[288,128]{1,0:T(8,128)(2,1)S(1)} %get-tuple-element.63), channel_id=1, source_target_pairs={{0,1},{1,0},{2,3},{3,2},{4,5},{5,4},{6,7},{7,6},{8,9},{9,8},{10,11... | collective-permute-start | bytes 221192 | tf_op jit(solution)/shard_map/ppermute | solution.py:555
  31.2 12.7 %collective-permute-start.4 = (bf16[288,128]{1,0:T(8,128)(2,1)S(1)}, bf16[288,128]{1,0:T(8,128)(2,1)S(1)}, u32[]{:S(2)}, u32[]{:S(2)}) collective-permute-start(bf16[288,128]{1,0:T(8,128)(2,1)S(1)} %get-tuple-element.64), channel_id=1, source_target_pairs={{0,2},{1,3},{2,0},{3,1},{4,6},{5,7},{6,4},{7,5},{8,10},{9,11},{10,... | collective-permute-start | bytes 221192 | tf_op jit(solution)/shard_map/ppermute | solution.py:555
  32.6 11.3 %collective-permute-start.5 = (bf16[288,128]{1,0:T(8,128)(2,1)S(1)}, bf16[288,128]{1,0:T(8,128)(2,1)S(1)}, u32[]{:S(2)}, u32[]{:S(2)}) collective-permute-start(bf16[288,128]{1,0:T(8,128)(2,1)S(1)} %get-tuple-element.65), channel_id=1, source_target_pairs={{0,3},{1,2},{2,1},{3,0},{4,7},{5,6},{6,5},{7,4},{8,11},{9,10},{10,... | collective-permute-start | bytes 221192 | tf_op jit(solution)/shard_map/ppermute | solution.py:555
  32.6 22.5 %copy-start.2 = (s32[1,256]{1,0:T(1,128)S(1)}, s32[1,256]{1,0:T(1,128)}, u32[]{:S(2)}) copy-start(s32[1,256]{1,0:T(1,128)} %doc_row.3) | copy-start | bytes 3076
  44.2 9.4 %collective-permute-start.6 = (bf16[8,2560]{1,0:T(8,128)(2,1)S(1)}, bf16[8,2560]{1,0:T(8,128)(2,1)S(1)}, u32[]{:S(2)}, u32[]{:S(2)}) collective-permute-start(bf16[8,2560]{1,0:T(8,128)(2,1)S(1)} %get-tuple-element.73), channel_id=1, source_target_pairs={{0,28},{4,24},{8,20},{12,16},{16,12},{20,8},{24,4},{28,0},{1,29},{... | collective-permute-start | bytes 122888 | tf_op jit(solution)/shard_map/ppermute | solution.py:613
  48.8 5.9 %collective-permute-start.7 = (bf16[8,2560]{1,0:T(8,128)(2,1)S(1)}, bf16[8,2560]{1,0:T(8,128)(2,1)S(1)}, u32[]{:S(2)}, u32[]{:S(2)}) collective-permute-start(bf16[8,2560]{1,0:T(8,128)(2,1)S(1)} %get-tuple-element.74), channel_id=1, source_target_pairs={{0,20},{4,16},{8,28},{12,24},{16,4},{20,0},{24,12},{28,8},{1,21},{... | collective-permute-start | bytes 122888 | tf_op jit(solution)/shard_map/ppermute | solution.py:613
  48.8 8.5 %collective-permute-start.8 = (bf16[8,2560]{1,0:T(8,128)(2,1)S(1)}, bf16[8,2560]{1,0:T(8,128)(2,1)S(1)}, u32[]{:S(2)}, u32[]{:S(2)}) collective-permute-start(bf16[8,2560]{1,0:T(8,128)(2,1)S(1)} %get-tuple-element.75), channel_id=1, source_target_pairs={{0,12},{4,8},{8,4},{12,0},{16,28},{20,24},{24,20},{28,16},{1,13},{... | collective-permute-start | bytes 122888 | tf_op jit(solution)/shard_map/ppermute | solution.py:613
  49.6 7.6 %collective-permute-start.9 = (bf16[8,2560]{1,0:T(8,128)(2,1)S(1)}, bf16[8,2560]{1,0:T(8,128)(2,1)S(1)}, u32[]{:S(2)}, u32[]{:S(2)}) collective-permute-start(bf16[8,2560]{1,0:T(8,128)(2,1)S(1)} %get-tuple-element.76), channel_id=1, source_target_pairs={{0,4},{4,0},{8,12},{12,8},{16,20},{20,16},{24,28},{28,24},{1,5},{5... | collective-permute-start | bytes 122888 | tf_op jit(solution)/shard_map/ppermute | solution.py:613
  50.8 6.6 %collective-permute-start.10 = (bf16[8,2560]{1,0:T(8,128)(2,1)S(1)}, bf16[8,2560]{1,0:T(8,128)(2,1)S(1)}, u32[]{:S(2)}, u32[]{:S(2)}) collective-permute-start(bf16[8,2560]{1,0:T(8,128)(2,1)S(1)} %get-tuple-element.77), channel_id=1, source_target_pairs={{0,24},{4,28},{8,16},{12,20},{16,8},{20,12},{24,0},{28,4},{1,25},{... | collective-permute-start | bytes 122888 | tf_op jit(solution)/shard_map/ppermute | solution.py:613
  53.6 4.9 %collective-permute-start.11 = (bf16[8,2560]{1,0:T(8,128)(2,1)S(1)}, bf16[8,2560]{1,0:T(8,128)(2,1)S(1)}, u32[]{:S(2)}, u32[]{:S(2)}) collective-permute-start(bf16[8,2560]{1,0:T(8,128)(2,1)S(1)} %get-tuple-element.78), channel_id=1, source_target_pairs={{0,8},{4,12},{8,0},{12,4},{16,24},{20,28},{24,16},{28,20},{1,9},{5... | collective-permute-start | bytes 122888 | tf_op jit(solution)/shard_map/ppermute | solution.py:613
  54.6 4.0 %collective-permute-start.12 = (bf16[8,2560]{1,0:T(8,128)(2,1)S(1)}, bf16[8,2560]{1,0:T(8,128)(2,1)S(1)}, u32[]{:S(2)}, u32[]{:S(2)}) collective-permute-start(bf16[8,2560]{1,0:T(8,128)(2,1)S(1)} %get-tuple-element.79), channel_id=1, source_target_pairs={{0,16},{4,20},{8,24},{12,28},{16,0},{20,4},{24,8},{28,12},{1,17},{... | collective-permute-start | bytes 122888 | tf_op jit(solution)/shard_map/ppermute | solution.py:613

commit v9 on v8

--- a/solution.py
+++ b/solution.py
@@ -21,6 +21,7 @@
 HBM = pl.BlockSpec(memory_space=pltpu.HBM)
 AHEAD = 3
 DEEP = 5
+TAIL = 1
 MIB = 1 << 20
 
 
@@ -76,9 +77,9 @@
 
 
 def merger_kernel(
-    where, patch_in, gain_in, bias_in, up, up_bias_in, down, down_bias_in, text, rms_gain_in, send, keep, text_out,
-    patch, gain, bias, up_bias, down_bias, rms_gain, bias_row, normed, merged, total, up_buf, down_buf, text_buf,
-    small_sem, up_sem, down_sem, text_sem,
+    where, patch_in, gain_in, bias_in, up, up_bias_in, down, down_bias_in, text, rms_gain_in, send, kept, text_out, hidden_out, bias_row, tail,
+    patch, gain, bias, up_bias, down_bias, rms_gain, normed, merged, total, up_buf, down_buf, text_buf,
+    small_sem, up_sem, down_sem, text_sem, tail_sem,
 ):
     slots = DEEP + 1
     step = up_buf.shape[1]
@@ -149,21 +150,39 @@
     stream(up_steps, up_copy, up_body, DEEP, down_copy)
     sums = total[...]
     hidden = (0.5 * sums * (1.0 + lax.erf(sums * math.sqrt(0.5)))).astype(BF16)
-
-    def down_body(i):
+    hidden_out[...] = hidden
+    steps = 2 * per_half - tail.shape[0]
+
+    def tail_copy(i):
+        return pltpu.make_async_copy(down.at[:, pl.ds(column(i), width)], tail.at[i - steps], tail_sem.at[i - steps])
+
+    @pl.loop(0, steps)
+    def _(i):
+        down_copy(i).wait()
+
+        @pl.when(i + DEEP < steps)
+        def _():
+            down_copy(i + DEEP).start()
+
+        @pl.when((i + DEEP >= steps) & (i + DEEP < 2 * per_half))
+        def _():
+            tail_copy(i + DEEP).start()
+
         text_norm(up_steps + i)
         part = (dot(hidden, down_buf[i % slots]) + bias_row[:, pl.ds(column(i), width)]).astype(BF16)
-        here = tile(i % per_half, width)
 
         @pl.when(i < per_half)
         def _():
-            send[:, here] = part
+            send[:, tile(i, width)] = part
 
         @pl.when(i >= per_half)
         def _():
-            keep[:, here] = part
-
-    stream(2 * per_half, down_copy, down_body, DEEP)
+            kept[:, tile(i - per_half, width)] = part
+
+    for i in range(steps, 2 * per_half):
+        text_norm(up_steps + i)
+    for i in range(steps, 2 * per_half):
+        tail_copy(i).wait()
 
 
 def merger(where, patch, gain, bias, up, up_bias, down, down_bias, text, rms_gain, rows):
@@ -175,9 +194,16 @@
     slots = DEEP + 1
     return pl.pallas_call(
         merger_kernel,
-        out_shape=[jax.ShapeDtypeStruct((rows, columns // 2), BF16)] * 2 + [pltpu.VMEM(text.shape, BF16)],
+        out_shape=[
+            jax.ShapeDtypeStruct((rows, columns // 2), BF16),
+            jax.ShapeDtypeStruct((rows, columns // 2 - TAIL * width), BF16),
+            pltpu.VMEM(text.shape, BF16),
+            jax.ShapeDtypeStruct((rows, hidden), BF16),
+            jax.ShapeDtypeStruct((1, columns), F32),
+            pltpu.VMEM((TAIL, hidden, width), BF16),
+        ],
         in_specs=[SMEM] + [HBM] * 9,
-        out_specs=[VMEM, VMEM, VMEM],
+        out_specs=[VMEM] * 6,
         scratch_shapes=[
             pltpu.VMEM(patch.shape, BF16),
             pltpu.VMEM(gain.shape, F32),
@@ -185,7 +211,6 @@
             pltpu.VMEM(up_bias.shape, F32),
             pltpu.VMEM(down_bias.shape, F32),
             pltpu.VMEM(rms_gain.shape, F32),
-            pltpu.VMEM((1, columns), F32),
             pltpu.VMEM((features // 128, patch.shape[0], 128), F32),
             pltpu.VMEM((rows, depth), BF16),
             pltpu.VMEM((rows, hidden), F32),
@@ -196,11 +221,35 @@
             pltpu.SemaphoreType.DMA((slots,)),
             pltpu.SemaphoreType.DMA((slots,)),
             pltpu.SemaphoreType.DMA((slots,)),
+            pltpu.SemaphoreType.DMA((TAIL,)),
         ],
         compiler_params=params(34),
         cost_estimate=cost(2 * rows * hidden * (depth + columns), 2 * hidden * (depth + columns)),
         name="merger",
     )(where, *map(in_hbm, (patch, gain, bias, up, up_bias, down, down_bias, text, rms_gain)))
+
+
+def keep_kernel(where, kept, hidden, bias_row, tail, keep):
+    done = kept.shape[1]
+    half = keep.shape[1]
+    keep[:, pl.ds(0, done)] = kept[...]
+    for i in range(tail.shape[0]):
+        width = tail.shape[2]
+        add = bias_row[:, pl.ds(pl.multiple_of((where[0] % 2) * half + done + i * width, width), width)]
+        keep[:, pl.ds(done + i * width, width)] = (dot(hidden[...], tail[i]) + add).astype(BF16)
+
+
+def keep_rest(where, kept, hidden, bias_row, tail):
+    rows = kept.shape[0]
+    return pl.pallas_call(
+        keep_kernel,
+        out_shape=jax.ShapeDtypeStruct((rows, bias_row.shape[1] // 2), BF16),
+        in_specs=[SMEM] + [VMEM] * 4,
+        out_specs=VMEM,
+        compiler_params=params(6),
+        cost_estimate=cost(2 * rows * tail.size, 2 * tail.size),
+        name="keep_rest",
+    )(where, kept, hidden, bias_row, in_vmem(tail))
 
 
 def owner_slots(owner_row, me, rows, capacity, slots):
@@ -585,11 +634,12 @@
         return max(abs(i % line - (i ^ x) % line) + (x >= line) for i in range(groups * line))
 
 
-    send, keep, text = merger(
+    send, kept, text, *rest = merger(
         where, patch_rows[0], ln_gain, ln_bias, merge_up, merge_up_bias, merge_down, merge_down_bias,
         text_embed[0], rms_gain[None, :], rows,
     )
-    own = (keep.astype(F32) + exchange(send, count, 1).astype(F32)).astype(BF16)
+    keep = keep_rest(where, kept, *rest)
+    own = (keep.astype(F32) + after(exchange(send, count, 1), keep).astype(F32)).astype(BF16)
     slots = owners * capacity
     weight, ready, select, place, join = weights_ahead(
         where, owner_row, after(w_keyval, own), w_query, w_query.shape[1] // 4, owners, slots

time: 61.2 us -> 60.8 us (level)
  waiting for transfers between devices: 2.54 us -> 1.45 us
  Pallas kernels: 41.5 us -> 42.2 us
    ppermute x6, waiting for transfers between devices: 1.18 us -> 0.08 us  [exchange(): return lax.ppermute(x, 'mp', [(i, i ^ bit) for i in range(count)])]
    pallas_call x0 -> x1, Pallas kernels: none -> 1.09 us  [keep_rest(): pl.pallas_call(keep_kernel, out_shape=jax.ShapeDtypeStruct((rows, bias_ro...]
  transfers between devices with their start and end apart: 13 -> 13, of which waited for: 4 -> 3; matrix products, arithmetic and copies ran while one was open for 0% -> 0% of each run, Pallas kernels for 36% -> 38%
where the time goes in v9:
time: 60.8 us; the launch traced here: 60.7 us
  Pallas kernels  42.2 us (69%)
  starting transfers between devices  16.5 us (27%)
  waiting for transfers between devices  1.45 us (2%)
    pallas_call x1, Pallas kernels, merger(): pl.pallas_call(merger_kernel, out_shape=[jax.ShapeDtypeStruct((rows, colu...  13.9 us
    pallas_call x1, Pallas kernels, query_rows(): pl.pallas_call(query_kernel, out_shape=[jax.ShapeDtypeStruct((texts, colu...  11.3 us
    ppermute x7, starting transfers between devices, arrived(): lax.ppermute(outgoing[x], ('group', 'dp'), [(i, i ^ x) for i in range(own...  11 us
    pallas_call x1, Pallas kernels, weights_ahead(): pl.pallas_call(functools.partial(weights_kernel, owners), out_shape=[pltp...  6.91 us
    ppermute x6, starting transfers between devices, exchange(): return lax.ppermute(x, 'mp', [(i, i ^ bit) for i in range(count)])  5.54 us
    pallas_call x1, Pallas kernels, keyval_parts(): pl.pallas_call(keyval_kernel, out_shape=[pltpu.VMEM((rows, depth), BF16),...  2.39 us
    pallas_call x1, Pallas kernels, attention(): pl.pallas_call(functools.partial(early_kernel, early, order), out_shape=j...  2.28 us
    pallas_call x1, Pallas kernels, attention(): pl.pallas_call(functools.partial(late_kernel, early), out_shape=[pltpu.VM...  2.08 us
  transfers between devices with their start and end apart: 13, of which 3 were waited for; matrix products, arithmetic and copies ran while one was open for 0% of the time, Pallas kernels for 38%

profile of v9, /device:TPU:0, one launch (start us, length us, event | category | flops | bytes accessed | tf_op | source)
XLA Modules:
  0.0 60.7 jit_solution(8085704051994858728)
XLA Ops:
  0.0 0.1 pad_add_fusion.where
  0.1 13.9 %merger.1 = (bf16[32,4096]{1,0:T(8,128)(2,1)S(1)}, bf16[32,3072]{1,0:T(8,128)(2,1)S(1)}, bf16[256,8192]{1,0:T(8,128)(2,1)S(1)}, bf16[32,1280]{1,0:T(8,128)(2,1)S...) custom-call(s32[2]{0:T(128)S(1)} %pad_add_fusion.where, bf16[128,1280]{1,0:T(8,128)(2,1)} %bitcast.14, ...), custom_call_target="tpu_custom_call" | custom-call | flops 1090519040 | bytes 34078720 | tf_op jit(solution)/shard_map/merger/pallas_call | solution.py:195
  14.0 0.5 collective-permute-start
  14.5 1.1 %keep_rest.1 = bf16[32,4096]{1,0:T(8,128)(2,1)S(1)} custom-call(s32[2]{0:T(128)S(1)} %pad_add_fusion.where, bf16[32,3072]{1,0:T(8,128)(2,1)S(1)} %get-tuple-element.52.kept, bf16[32,1280]{1,0:T(8,128)(2,1)S(1)} %get-tuple-element.53.hidden, f32[1,8192]{1,0:T(1,128)S(1)} %get-tuple-element.54.bias_row, bf16[1,1280,1024]{2,1,0:T(8,128)(2,1)S(1)} %get-tuple-element.55.tail), custom_call_target="tpu_custom_call" | custom-call | flops 83886080 | bytes 2621440 | tf_op jit(solution)/shard_map/keep_rest/pallas_call | solution.py:244
  15.6 0.1 collective-permute-done
  15.7 0.1 add_convert_fusion.1
  15.8 3.0 %collective-permute-start.1 = (bf16[32,4096]{1,0:T(8,128)(2,1)S(1)}, bf16[32,4096]{1,0:T(8,128)(2,1)S(1)}, u32[]{:S(2)}, u32[]{:S(2)}) collective-permute-start(bf16[32,4096]{1,0:T(8,128)(2,1)S(1)} %add_convert_fusion.1), channel_id=1, source_target_pairs={{0,2},{1,3},{2,0},{3,1},{4,6},{5,7},{6,4},{7,5},{8,10},{9,11},{10,... | collective-permute-start | bytes 786440 | tf_op jit(solution)/shard_map/ppermute | solution.py:604
  18.7 6.9 %weights_ahead.1 = (bf16[8192,512]{1,0:T(8,128)(2,1)S(1)}, bf16[8192,512]{1,0:T(8,128)(2,1)S(1)}, bf16[64,32]{1,0:T(8,128)(2,1)S(1)}, bf16[64,64]{1,0:T(8,128)(2,1)S(1)}, bf16[512,512]{1,0:T(8,128)(2,1)S(1)}) custom-call(s32[2]{0:T(128)S(1)} %pad_add_fusion.where, s32[1,256]{1,0:T(1,128)S(1)} %bitcast.12, bf16[8192,2,256]{2,1,0:T(2,128)(2,1)} %keyval.1, ...), custom_call_target="tpu_custom_call" | custom-call | flops 2147483648 | bytes 8388608 | tf_op jit(solution)/shard_map/weights_ahead/pallas_call | solution.py:344
  25.6 0.0 copy-start.3
  25.7 0.1 add_convert_fusion.own
  25.7 0.1 collective-permute-start.2
  25.8 2.0 %keyval_own.1 = (bf16[288,8192]{1,0:T(8,128)(2,1)S(1)}, f32[288,512]{1,0:T(8,128)S(1)}) custom-call(s32[2]{0:T(128)S(1)} %pad_add_fusion.where, bf16[256,8192]{1,0:T(8,128)(2,1)S(1)} %get-tuple-element.51.text, bf16[32,4096]{1,0:T(8,128)(2,1)S(1)} %add_convert_fusion.own, f32[1,8192]{1,0:T(1,128)S(1)} %bitcast.9, bf16[8192,512]{1,0:T(8,128)(2,1)S(1)} %get-tuple-element.59.weight), custom_call_target="tpu_custom_call" | custom-call | flops 1207959552 | bytes 4194304 | tf_op jit(solution)/shard_map/keyval_own/pallas_call | solution.py:409
  27.8 0.0 copy-start.1
  27.9 2.4 %keyval.2 = (bf16[288,8192]{1,0:T(8,128)(2,1)S(1)}, f32[32,128]{1,0:T(8,128)S(1)}, bf16[288,128]{1,0:T(8,128)(2,1)S(1)}, bf16[288,128]{1,0:T(8,128)(2,1)S(1)}, b...) custom-call(s32[2]{0:T(128)S(1)} %pad_add_fusion.where, ...), custom_call_target="tpu_custom_call", output_to_operand_aliasing={{0}: (1, {})} | custom-call | flops 1207959552 | bytes 4194304 | tf_op jit(solution)/shard_map/keyval/pallas_call | solution.py:418
  30.3 0.6 collective-permute-start.3
  30.8 1.4 %collective-permute-start.4 = (bf16[288,128]{1,0:T(8,128)(2,1)S(1)}, bf16[288,128]{1,0:T(8,128)(2,1)S(1)}, u32[]{:S(2)}, u32[]{:S(2)}) collective-permute-start(bf16[288,128]{1,0:T(8,128)(2,1)S(1)} %get-tuple-element.72), channel_id=1, source_target_pairs={{0,2},{1,3},{2,0},{3,1},{4,6},{5,7},{6,4},{7,5},{8,10},{9,11},{10,... | collective-permute-start | bytes 221192 | tf_op jit(solution)/shard_map/ppermute | solution.py:604
  32.2 0.0 collective-permute-start.5
  32.3 11.3 %query.3 = (bf16[256,1024]{1,0:T(8,128)(2,1)S(1)}, bf16[256,1024]{1,0:T(8,128)(2,1)S(1)}, bf16[32,2048]{1,0:T(8,128)(2,1)S(1)}) custom-call(bf16[288,8192]{1,0:T(8,128)(2,1)S(1)} %get-tuple-element.64.rows_all, f32[32,128]{1,0:T(8,128)S(1)} %get-tuple-element.65.scale, bf16[8192,512]{1,0:T(8,128)(2,1)S(1)} %get-tuple-element.66.ready, ...), custom_call_target="tpu_custom_call" | custom-call | flops 9663676416 | bytes 33554432 | tf_op jit(solution)/shard_map/query/pallas_call | solution.py:465
  43.5 0.0 collective-permute-done.3.rest_1_
  43.6 0.0 collective-permute-done.5.rest_3_
  43.6 0.2 slots.1
  43.8 4.6 %collective-permute-start.6 = (bf16[8,2560]{1,0:T(8,128)(2,1)S(1)}, bf16[8,2560]{1,0:T(8,128)(2,1)S(1)}, u32[]{:S(2)}, u32[]{:S(2)}) collective-permute-start(bf16[8,2560]{1,0:T(8,128)(2,1)S(1)} %get-tuple-element.81), channel_id=1, source_target_pairs={{0,28},{4,24},{8,20},{12,16},{16,12},{20,8},{24,4},{28,0},{1,29},{... | collective-permute-start | bytes 122888 | tf_op jit(solution)/shard_map/ppermute | solution.py:663
  48.4 0.9 %collective-permute-start.8 = (bf16[8,2560]{1,0:T(8,128)(2,1)S(1)}, bf16[8,2560]{1,0:T(8,128)(2,1)S(1)}, u32[]{:S(2)}, u32[]{:S(2)}) collective-permute-start(bf16[8,2560]{1,0:T(8,128)(2,1)S(1)} %get-tuple-element.83), channel_id=1, source_target_pairs={{0,12},{4,8},{8,4},{12,0},{16,28},{20,24},{24,20},{28,16},{1,13},{... | collective-permute-start | bytes 122888 | tf_op jit(solution)/shard_map/ppermute | solution.py:663
  49.3 1.1 %collective-permute-start.9 = (bf16[8,2560]{1,0:T(8,128)(2,1)S(1)}, bf16[8,2560]{1,0:T(8,128)(2,1)S(1)}, u32[]{:S(2)}, u32[]{:S(2)}) collective-permute-start(bf16[8,2560]{1,0:T(8,128)(2,1)S(1)} %get-tuple-element.84), channel_id=1, source_target_pairs={{0,4},{4,0},{8,12},{12,8},{16,20},{20,16},{24,28},{28,24},{1,5},{5... | collective-permute-start | bytes 122888 | tf_op jit(solution)/shard_map/ppermute | solution.py:663
  50.4 2.8 %collective-permute-start.10 = (bf16[8,2560]{1,0:T(8,128)(2,1)S(1)}, bf16[8,2560]{1,0:T(8,128)(2,1)S(1)}, u32[]{:S(2)}, u32[]{:S(2)}) collective-permute-start(bf16[8,2560]{1,0:T(8,128)(2,1)S(1)} %get-tuple-element.85), channel_id=1, source_target_pairs={{0,24},{4,28},{8,16},{12,20},{16,8},{20,12},{24,0},{28,4},{1,25},{... | collective-permute-start | bytes 122888 | tf_op jit(solution)/shard_map/ppermute | solution.py:663
  53.2 1.0 %collective-permute-start.11 = (bf16[8,2560]{1,0:T(8,128)(2,1)S(1)}, bf16[8,2560]{1,0:T(8,128)(2,1)S(1)}, u32[]{:S(2)}, u32[]{:S(2)}) collective-permute-start(bf16[8,2560]{1,0:T(8,128)(2,1)S(1)} %get-tuple-element.86), channel_id=1, source_target_pairs={{0,8},{4,12},{8,0},{12,4},{16,24},{20,28},{24,16},{28,20},{1,9},{5... | collective-permute-start | bytes 122888 | tf_op jit(solution)/shard_map/ppermute | solution.py:663
  54.3 0.5 collective-permute-start.12
  54.8 2.1 %attention_late.1 = (bf16[128,2048]{1,0:T(8,128)(2,1)S(1)}, bf16[256,512]{1,0:T(8,128)(2,1)S(1)}) custom-call(bf16[512,512]{1,0:T(8,128)(2,1)S(1)} %get-tuple-element.78.join, s32[1,256]{1,0:T(1,128)S(1)} %copy-done.2, bf16[256,1024]{1,0:T(8,128)(2,1)S(1)} %get-tuple-element.75.first_half, bf16[256,1024]{1,0:T(8,128)(2,1)S(1)} %get-tuple-element.77.second_half, ...), custom_call_target="tpu_custom_call" | custom-call | flops 134217728 | bytes 2097152 | tf_op jit(solution)/shard_map/attention_late/pallas_call | solution.py:577
  56.9 0.0 collective-permute-done.10.rest_4_
  56.9 1.2 %collective-permute-done.11.rest_5_ = bf16[8,2560]{1,0:T(8,128)(2,1)S(1)} collective-permute-done((bf16[8,2560]{1,0:T(8,128)(2,1)S(1)}, bf16[8,2560]{1,0:T(8,128)(2,1)S(1)}, u32[]{:S(2)}, u32[]{:S(2)}) %collective-permute-start.11) | collective-permute-done | bytes 40992 | tf_op jit(solution)/shard_map/ppermute | solution.py:663
  58.1 0.1 collective-permute-done.12.rest_6_
  58.3 2.3 %attention_early.1 = bf16[256,2048]{1,0:T(8,128)(2,1)} custom-call(s32[1,256]{1,0:T(1,128)S(1)} %copy-done.2, bf16[256,1024]{1,0:T(8,128)(2,1)S(1)} %get-tuple-element.75.first_half, bf16[256,1024]{1,0:T(8,128)(2,1)S(1)} %get-tuple-element.77.second_half, bf16[256,512]{1,0:T(8,128)(2,1)S(1)} %get-tuple-element.79.keyval, ...), custom_call_target="tpu_custom_call" | custom-call | flops 134217728 | bytes 2097152 | tf_op jit(solution)/shard_map/attention_early/pallas_call | solution.py:586
  (16 shorter events, 0.0 us)
Async XLA Ops:
  0.1 18.6 %copy-start.4 = (s32[256,1]{0,1:T(1,128)S(1)}, s32[256,1]{0,1:T(1,128)}, u32[]{:S(2)}) copy-start(s32[256,1]{0,1:T(1,128)} %param.22) | copy-start | bytes 3076
  14.0 1.7 %collective-permute-start = (bf16[32,4096]{1,0:T(8,128)(2,1)S(1)}, bf16[32,4096]{1,0:T(8,128)(2,1)S(1)}, u32[]{:S(2)}, u32[]{:S(2)}) collective-permute-start(bf16[32,4096]{1,0:T(8,128)(2,1)S(1)} %get-tuple-element.56), channel_id=1, source_target_pairs={{0,1},{1,0},{2,3},{3,2},{4,5},{5,4},{6,7},{7,6},{8,9},{9,8},{10,11... | collective-permute-start | bytes 786440 | tf_op jit(solution)/shard_map/ppermute | solution.py:604
  15.8 9.9 %collective-permute-start.1 = (bf16[32,4096]{1,0:T(8,128)(2,1)S(1)}, bf16[32,4096]{1,0:T(8,128)(2,1)S(1)}, u32[]{:S(2)}, u32[]{:S(2)}) collective-permute-start(bf16[32,4096]{1,0:T(8,128)(2,1)S(1)} %add_convert_fusion.1), channel_id=1, source_target_pairs={{0,2},{1,3},{2,0},{3,1},{4,6},{5,7},{6,4},{7,5},{8,10},{9,11},{10,... | collective-permute-start | bytes 786440 | tf_op jit(solution)/shard_map/ppermute | solution.py:604
  18.7 7.1 %copy-start = (f32[8192]{0:T(1024)S(1)}, f32[8192]{0:T(1024)}, u32[]{:S(2)}) copy-start(f32[8192]{0:T(1024)} %param.25) | copy-start | bytes 98308
  25.6 2.2 %copy-start.3 = (f32[2,256]{1,0:T(2,128)S(1)}, f32[2,256]{1,0:T(2,128)}, u32[]{:S(2)}) copy-start(f32[2,256]{1,0:T(2,128)} %bias.1) | copy-start | bytes 6148
  25.7 2.1 %collective-permute-start.2 = (bf16[32,4096]{1,0:T(8,128)(2,1)S(1)}, bf16[32,4096]{1,0:T(8,128)(2,1)S(1)}, u32[]{:S(2)}, u32[]{:S(2)}) collective-permute-start(bf16[32,4096]{1,0:T(8,128)(2,1)S(1)} %add_convert_fusion.own), channel_id=1, source_target_pairs={{0,1},{1,0},{2,3},{3,2},{4,5},{5,4},{6,7},{7,6},{8,9},{9,8},{10,11... | collective-permute-start | bytes 786440 | tf_op jit(solution)/shard_map/ppermute | solution.py:604
  27.8 4.4 %copy-start.1 = (f32[2048]{0:T(1024)S(1)}, f32[2048]{0:T(1024)}, u32[]{:S(2)}) copy-start(f32[2048]{0:T(1024)} %param.27) | copy-start | bytes 24580
  30.3 13.3 %collective-permute-start.3 = (bf16[288,128]{1,0:T(8,128)(2,1)S(1)}, bf16[288,128]{1,0:T(8,128)(2,1)S(1)}, u32[]{:S(2)}, u32[]{:S(2)}) collective-permute-start(bf16[288,128]{1,0:T(8,128)(2,1)S(1)} %get-tuple-element.71), channel_id=1, source_target_pairs={{0,1},{1,0},{2,3},{3,2},{4,5},{5,4},{6,7},{7,6},{8,9},{9,8},{10,11... | collective-permute-start | bytes 221192 | tf_op jit(solution)/shard_map/ppermute | solution.py:604
  30.8 12.7 %collective-permute-start.4 = (bf16[288,128]{1,0:T(8,128)(2,1)S(1)}, bf16[288,128]{1,0:T(8,128)(2,1)S(1)}, u32[]{:S(2)}, u32[]{:S(2)}) collective-permute-start(bf16[288,128]{1,0:T(8,128)(2,1)S(1)} %get-tuple-element.72), channel_id=1, source_target_pairs={{0,2},{1,3},{2,0},{3,1},{4,6},{5,7},{6,4},{7,5},{8,10},{9,11},{10,... | collective-permute-start | bytes 221192 | tf_op jit(solution)/shard_map/ppermute | solution.py:604
  32.2 11.3 %collective-permute-start.5 = (bf16[288,128]{1,0:T(8,128)(2,1)S(1)}, bf16[288,128]{1,0:T(8,128)(2,1)S(1)}, u32[]{:S(2)}, u32[]{:S(2)}) collective-permute-start(bf16[288,128]{1,0:T(8,128)(2,1)S(1)} %get-tuple-element.73), channel_id=1, source_target_pairs={{0,3},{1,2},{2,1},{3,0},{4,7},{5,6},{6,5},{7,4},{8,11},{9,10},{10,... | collective-permute-start | bytes 221192 | tf_op jit(solution)/shard_map/ppermute | solution.py:604
  32.3 22.5 %copy-start.2 = (s32[1,256]{1,0:T(1,128)S(1)}, s32[1,256]{1,0:T(1,128)}, u32[]{:S(2)}) copy-start(s32[1,256]{1,0:T(1,128)} %doc_row.3) | copy-start | bytes 3076
  43.8 9.4 %collective-permute-start.6 = (bf16[8,2560]{1,0:T(8,128)(2,1)S(1)}, bf16[8,2560]{1,0:T(8,128)(2,1)S(1)}, u32[]{:S(2)}, u32[]{:S(2)}) collective-permute-start(bf16[8,2560]{1,0:T(8,128)(2,1)S(1)} %get-tuple-element.81), channel_id=1, source_target_pairs={{0,28},{4,24},{8,20},{12,16},{16,12},{20,8},{24,4},{28,0},{1,29},{... | collective-permute-start | bytes 122888 | tf_op jit(solution)/shard_map/ppermute | solution.py:663
  48.4 5.9 %collective-permute-start.7 = (bf16[8,2560]{1,0:T(8,128)(2,1)S(1)}, bf16[8,2560]{1,0:T(8,128)(2,1)S(1)}, u32[]{:S(2)}, u32[]{:S(2)}) collective-permute-start(bf16[8,2560]{1,0:T(8,128)(2,1)S(1)} %get-tuple-element.82), channel_id=1, source_target_pairs={{0,20},{4,16},{8,28},{12,24},{16,4},{20,0},{24,12},{28,8},{1,21},{... | collective-permute-start | bytes 122888 | tf_op jit(solution)/shard_map/ppermute | solution.py:663
  48.4 8.5 %collective-permute-start.8 = (bf16[8,2560]{1,0:T(8,128)(2,1)S(1)}, bf16[8,2560]{1,0:T(8,128)(2,1)S(1)}, u32[]{:S(2)}, u32[]{:S(2)}) collective-permute-start(bf16[8,2560]{1,0:T(8,128)(2,1)S(1)} %get-tuple-element.83), channel_id=1, source_target_pairs={{0,12},{4,8},{8,4},{12,0},{16,28},{20,24},{24,20},{28,16},{1,13},{... | collective-permute-start | bytes 122888 | tf_op jit(solution)/shard_map/ppermute | solution.py:663
  49.3 7.6 %collective-permute-start.9 = (bf16[8,2560]{1,0:T(8,128)(2,1)S(1)}, bf16[8,2560]{1,0:T(8,128)(2,1)S(1)}, u32[]{:S(2)}, u32[]{:S(2)}) collective-permute-start(bf16[8,2560]{1,0:T(8,128)(2,1)S(1)} %get-tuple-element.84), channel_id=1, source_target_pairs={{0,4},{4,0},{8,12},{12,8},{16,20},{20,16},{24,28},{28,24},{1,5},{5... | collective-permute-start | bytes 122888 | tf_op jit(solution)/shard_map/ppermute | solution.py:663
  50.4 6.5 %collective-permute-start.10 = (bf16[8,2560]{1,0:T(8,128)(2,1)S(1)}, bf16[8,2560]{1,0:T(8,128)(2,1)S(1)}, u32[]{:S(2)}, u32[]{:S(2)}) collective-permute-start(bf16[8,2560]{1,0:T(8,128)(2,1)S(1)} %get-tuple-element.85), channel_id=1, source_target_pairs={{0,24},{4,28},{8,16},{12,20},{16,8},{20,12},{24,0},{28,4},{1,25},{... | collective-permute-start | bytes 122888 | tf_op jit(solution)/shard_map/ppermute | solution.py:663
  53.2 4.9 %collective-permute-start.11 = (bf16[8,2560]{1,0:T(8,128)(2,1)S(1)}, bf16[8,2560]{1,0:T(8,128)(2,1)S(1)}, u32[]{:S(2)}, u32[]{:S(2)}) collective-permute-start(bf16[8,2560]{1,0:T(8,128)(2,1)S(1)} %get-tuple-element.86), channel_id=1, source_target_pairs={{0,8},{4,12},{8,0},{12,4},{16,24},{20,28},{24,16},{28,20},{1,9},{5... | collective-permute-start | bytes 122888 | tf_op jit(solution)/shard_map/ppermute | solution.py:663
  54.3 4.0 %collective-permute-start.12 = (bf16[8,2560]{1,0:T(8,128)(2,1)S(1)}, bf16[8,2560]{1,0:T(8,128)(2,1)S(1)}, u32[]{:S(2)}, u32[]{:S(2)}) collective-permute-start(bf16[8,2560]{1,0:T(8,128)(2,1)S(1)} %get-tuple-element.87), channel_id=1, source_target_pairs={{0,16},{4,20},{8,24},{12,28},{16,0},{20,4},{24,8},{28,12},{1,17},{... | collective-permute-start | bytes 122888 | tf_op jit(solution)/shard_map/ppermute | solution.py:663
